TPU v7x, 256 devices: a whole 4x4x8 slice. The times are simulated.
256 devices in a mesh: dp: 2 (over y_hi), tm: 32 (over z, y_lo, core), tensor: 4 (over x).
Axes of the slice: x: 4, y: 4 (y_hi: 2, y_lo: 2; y = y_hi * 2 + y_lo), z: 8, core: 2. Of those that a mesh axis runs over, the one named last changes fastest.
Arguments:
- queries: bfloat16 [2, 64, 256, 1280], P('dp', 'tm', None, 'tensor'), may hold values from -140 to 140
- key_vectors: bfloat16 [2, 64, 256, 1280], P('dp', 'tm', None, 'tensor'), may hold values from -4.1 to 4.1
- value_vectors: bfloat16 [2, 64, 256, 1280], P('dp', 'tm', None, 'tensor'), may hold values from -6 to 6
- normed: bfloat16 [2, 64, 256, 1280], P('dp', 'tm'), may hold values from -6 to 6
- grad_output: bfloat16 [2, 64, 256, 1280], P('dp', 'tm'), may hold values from -6 to 6
- w_qkv: bfloat16 [3, 1280, 1280], P(None, None, 'tensor'), may hold values from -0.15625 to 0.15625
- w_out: bfloat16 [1280, 1280], P('tensor'), may hold values from -0.15625 to 0.15625
Outputs:
- grad_normed: bfloat16 [2, 64, 256, 1280], P('dp', 'tm')
- grad_qkv: float32 [3, 1280, 1280], P(None, ('dp', 'tm'), 'tensor')
- grad_out: float32 [1280, 1280], P('tensor', ('dp', 'tm'))
All inputs are finite; a program needn't handle non-finite values.
Results may differ from a plain program's by a relative error of at most 0.018.
Values may be sent and summed in bfloat16 or wider, within the bound.
No kernel may reach another device: no remote copies, remote signals or barrier semaphores. Data moves between devices by JAX's collectives and lax.ppermute only.
A program may use at most 128 MiB of HBM per device.

v0:
```python
import jax
import jax.numpy as jnp
from jax import lax
from jax.sharding import PartitionSpec as P

HS = 80


def shortened(x):
    return jax.tree.map(lambda a: a.astype(jnp.bfloat16) if a.dtype == jnp.float32 else a, x)


def to_heads(values_in):
    full_shape = values_in.shape
    return values_in.reshape(full_shape[:3] + (full_shape[3] // HS, HS))


def attend(query_heads, key_heads, value_heads):
    temper = HS ** (-0.5)
    scores = (
        jnp.einsum("cfphd,cgphd->cphfg", query_heads, key_heads, preferred_element_type=jnp.float32)
        * temper
    )
    probs = jax.nn.softmax(scores, axis=-1)
    weights = probs.astype(jnp.bfloat16)
    attended = jnp.einsum(
        "cphfg,cgphd->cfphd", weights, value_heads, preferred_element_type=jnp.float32
    )
    return (probs, weights, attended.astype(jnp.bfloat16))


def backprop(probs, weights, query_heads, key_heads, value_heads, grad_heads):
    temper = HS ** (-0.5)
    grad_probs = jnp.einsum(
        "cfphd,cgphd->cphfg", grad_heads, value_heads, preferred_element_type=jnp.float32
    )
    row_delta = jnp.sum(probs * grad_probs, axis=-1, keepdims=True)
    grad_scores = (probs * (grad_probs - row_delta)).astype(jnp.bfloat16)
    grad_q = (
        jnp.einsum("cphfg,cgphd->cfphd", grad_scores, key_heads, preferred_element_type=jnp.float32)
        * temper
    )
    grad_k = (
        jnp.einsum(
            "cphfg,cfphd->cgphd", grad_scores, query_heads, preferred_element_type=jnp.float32
        )
        * temper
    )
    grad_v = jnp.einsum(
        "cphfg,cfphd->cgphd", weights, grad_heads, preferred_element_type=jnp.float32
    )
    return (grad_q.astype(jnp.bfloat16), grad_k.astype(jnp.bfloat16), grad_v.astype(jnp.bfloat16))


def on_device(queries, key_vectors, value_vectors, normed, grad_output, w_qkv, w_out):
    width = normed.shape[-1]
    local_width = w_out.shape[0]
    rows_grad = grad_output.reshape(-1, width)
    grad_attn = lax.dot_general(
        rows_grad, w_out, (((1,), (1,)), ((), ())), preferred_element_type=jnp.float32
    )
    grad_attn = grad_attn.astype(jnp.bfloat16).reshape(queries.shape)

    def regroup(pieces):
        flat_shape = pieces[0].shape
        heads = [to_heads(item) for item in pieces]
        probs, weights, attended = attend(heads[0], heads[1], heads[2])
        grads = backprop(probs, weights, heads[0], heads[1], heads[2], heads[3])
        results = tuple((item.reshape(flat_shape) for item in (attended,) + grads))
        return jax.tree.map(
            lambda part, own: part.astype(own.dtype),
            lax.all_to_all(shortened(results), "tm", split_axis=1, concat_axis=2, tiled=True),
            results,
        )

    attended, grad_q, grad_k, grad_v = regroup(
        (
            lax.all_to_all(queries, "tm", split_axis=2, concat_axis=1, tiled=True),
            lax.all_to_all(key_vectors, "tm", split_axis=2, concat_axis=1, tiled=True),
            lax.all_to_all(value_vectors, "tm", split_axis=2, concat_axis=1, tiled=True),
            lax.all_to_all(grad_attn, "tm", split_axis=2, concat_axis=1, tiled=True),
        )
    )
    rows_norm = normed.reshape(-1, width)
    stacked = jnp.stack([item.reshape(-1, local_width) for item in (grad_q, grad_k, grad_v)])
    partial_norm = jnp.einsum("itk,idk->td", stacked, w_qkv, preferred_element_type=jnp.float32)
    grad_normed = lax.psum(partial_norm.astype(jnp.bfloat16), "tensor")
    grad_normed = grad_normed.reshape(normed.shape)
    qkv_term = jnp.einsum("td,itk->idk", rows_norm, stacked, preferred_element_type=jnp.float32)
    out_term = lax.dot_general(
        attended.reshape(-1, local_width),
        rows_grad,
        (((0,), (0,)), ((), ())),
        preferred_element_type=jnp.float32,
    )
    grad_qkv, grad_out = (
        lax.psum_scatter(qkv_term, ("dp", "tm"), scatter_dimension=1, tiled=True),
        lax.psum_scatter(out_term, ("dp", "tm"), scatter_dimension=1, tiled=True),
    )
    return (grad_normed, grad_qkv, grad_out)


def solution(mesh):
    in_specs = (
        P("dp", "tm", None, "tensor"),
        P("dp", "tm", None, "tensor"),
        P("dp", "tm", None, "tensor"),
        P("dp", "tm", None, None),
        P("dp", "tm", None, None),
        P(None, None, "tensor"),
        P("tensor", None),
    )
    out_specs = (
        P("dp", "tm", None, None),
        P(None, ("dp", "tm"), "tensor"),
        P("tensor", ("dp", "tm")),
    )
    return jax.shard_map(
        on_device, mesh=mesh, in_specs=in_specs, out_specs=out_specs, check_vma=False
    )
```

profile of v0, /device:TPU:1, one launch (start us, length us, event | category | flops | bytes accessed | tf_op | source)
XLA Modules:
  0.0 467.7 jit_solution(2173178776601920814)
XLA Ops:
  7.2 2.1 copy.43
  9.3 11.1 %all-to-all-start = ((bf16[1,2,256,320]{3,1,0,2:T(2,128)(2,1)}), bf16[1,2,256,320]{3,1,0,2:T(2,128)(2,1)S(1)}, u32[]{:S(2)}, u32[]{:S(2)}) async-start(bf16[1,2,256,320]{3,1,0,2:T(2,128)(2,1)} %copy.43), calls=%async_computation | async-start | bytes 786432 | tf_op jit(solution)/shard_map/all_to_all | solution.py:78
  21.5 12.7 %all-to-all-done = bf16[1,2,256,320]{3,1,0,2:T(2,128)(2,1)S(1)} async-done(((bf16[1,2,256,320]{3,1,0,2:T(2,128)(2,1)}), bf16[1,2,256,320]{3,1,0,2:T(2,128)(2,1)S(1)}, u32[]{:S(2)}, u32[]{:S(2)}) %all-to-all-start) | async-done | bytes 327712 | tf_op jit(solution)/shard_map/all_to_all | solution.py:78
  34.2 5.2 %all-to-all-start.1 = ((bf16[1,2,256,320]{3,1,0,2:T(2,128)(2,1)}), bf16[1,2,256,320]{3,1,0,2:T(2,128)(2,1)S(1)}, u32[]{:S(2)}, u32[]{:S(2)}) async-start(bf16[1,2,256,320]{3,1,0,2:T(2,128)(2,1)} %copy.46), calls=%async_computation.1 | async-start | bytes 786432 | tf_op jit(solution)/shard_map/all_to_all | solution.py:79
  39.4 2.9 convolution_convert_fusion.2
  44.1 2.0 copy.51
  46.1 7.2 %all-to-all-done.1 = bf16[1,2,256,320]{3,1,0,2:T(2,128)(2,1)S(1)} async-done(((bf16[1,2,256,320]{3,1,0,2:T(2,128)(2,1)}), bf16[1,2,256,320]{3,1,0,2:T(2,128)(2,1)S(1)}, u32[]{:S(2)}, u32[]{:S(2)}) %all-to-all-start.1) | async-done | bytes 327712 | tf_op jit(solution)/shard_map/all_to_all | solution.py:79
  53.3 5.8 %all-to-all-start.2 = ((bf16[1,2,256,320]{3,1,0,2:T(2,128)(2,1)}), bf16[1,2,256,320]{3,1,0,2:T(2,128)(2,1)}, u32[]{:S(2)}, u32[]{:S(2)}) async-start(bf16[1,2,256,320]{3,1,0,2:T(2,128)(2,1)} %copy.51), calls=%async_computation.2 | async-start | bytes 786432 | tf_op jit(solution)/shard_map/all_to_all | solution.py:81
  59.2 1.9 copy.54
  61.1 12.0 %all-to-all-done.2 = bf16[1,2,256,320]{3,1,0,2:T(2,128)(2,1)} async-done(((bf16[1,2,256,320]{3,1,0,2:T(2,128)(2,1)}), bf16[1,2,256,320]{3,1,0,2:T(2,128)(2,1)}, u32[]{:S(2)}, u32[]{:S(2)}) %all-to-all-start.2) | async-done | bytes 327712 | tf_op jit(solution)/shard_map/all_to_all | solution.py:81
  73.1 5.8 %all-to-all-start.3 = ((bf16[1,2,256,320]{3,1,0,2:T(2,128)(2,1)}), bf16[1,2,256,320]{3,1,0,2:T(2,128)(2,1)}, u32[]{:S(2)}, u32[]{:S(2)}) async-start(bf16[1,2,256,320]{3,1,0,2:T(2,128)(2,1)} %copy.54), calls=%async_computation.3 | async-start | bytes 786432 | tf_op jit(solution)/shard_map/all_to_all | solution.py:80
  85.3 2.1 reshape.119
  87.4 5.5 %all-to-all-done.3 = bf16[1,2,256,320]{3,1,0,2:T(2,128)(2,1)} async-done(((bf16[1,2,256,320]{3,1,0,2:T(2,128)(2,1)}), bf16[1,2,256,320]{3,1,0,2:T(2,128)(2,1)}, u32[]{:S(2)}, u32[]{:S(2)}) %all-to-all-start.3) | async-done | bytes 327712 | tf_op jit(solution)/shard_map/all_to_all | solution.py:80
  94.7 2.1 reshape.120
  98.5 2.2 multiply_reduce_fusion
  103.3 2.2 reshape.121
  105.5 5.8 %all-to-all-start.4 = ((bf16[1,64,8,320]{3,2,0,1:T(8,128)(2,1)}), bf16[1,64,8,320]{3,2,0,1:T(8,128)(2,1)}, u32[]{:S(2)}, u32[]{:S(2)}) async-start(bf16[1,64,8,320]{3,2,0,1:T(8,128)(2,1)} %bitcast.96), calls=%async_computation.4 | async-start | bytes 786432 | tf_op jit(solution)/shard_map/all_to_all | solution.py:72
  113.2 12.1 %all-to-all-done.4 = bf16[1,64,8,320]{3,2,0,1:T(8,128)(2,1)} async-done(((bf16[1,64,8,320]{3,2,0,1:T(8,128)(2,1)}), bf16[1,64,8,320]{3,2,0,1:T(8,128)(2,1)}, u32[]{:S(2)}, u32[]{:S(2)}) %all-to-all-start.4) | async-done | bytes 327712 | tf_op jit(solution)/shard_map/all_to_all | solution.py:72
  125.3 5.2 %all-to-all-start.5 = ((bf16[1,64,8,320]{3,2,0,1:T(8,128)(2,1)}), bf16[1,64,8,320]{3,2,0,1:T(8,128)(2,1)S(1)}, u32[]{:S(2)}, u32[]{:S(2)}) async-start(bf16[1,64,8,320]{3,2,0,1:T(8,128)(2,1)} %bitcast.19), calls=%async_computation.5 | async-start | bytes 786432 | tf_op jit(solution)/shard_map/all_to_all | solution.py:72
  133.6 10.8 %all-to-all-done.5 = bf16[1,64,8,320]{3,2,0,1:T(8,128)(2,1)S(1)} async-done(((bf16[1,64,8,320]{3,2,0,1:T(8,128)(2,1)}), bf16[1,64,8,320]{3,2,0,1:T(8,128)(2,1)S(1)}, u32[]{:S(2)}, u32[]{:S(2)}) %all-to-all-start.5) | async-done | bytes 327712 | tf_op jit(solution)/shard_map/all_to_all | solution.py:72
  144.4 5.8 %all-to-all-start.6 = ((bf16[1,64,8,320]{3,2,0,1:T(8,128)(2,1)}), bf16[1,64,8,320]{3,2,0,1:T(8,128)(2,1)}, u32[]{:S(2)}, u32[]{:S(2)}) async-start(bf16[1,64,8,320]{3,2,0,1:T(8,128)(2,1)} %bitcast.95), calls=%async_computation.6 | async-start | bytes 786432 | tf_op jit(solution)/shard_map/all_to_all | solution.py:72
  153.5 10.6 %all-to-all-done.6 = bf16[1,64,8,320]{3,2,0,1:T(8,128)(2,1)} async-done(((bf16[1,64,8,320]{3,2,0,1:T(8,128)(2,1)}), bf16[1,64,8,320]{3,2,0,1:T(8,128)(2,1)}, u32[]{:S(2)}, u32[]{:S(2)}) %all-to-all-start.6) | async-done | bytes 327712 | tf_op jit(solution)/shard_map/all_to_all | solution.py:72
  164.2 5.3 %all-to-all-start.7 = ((bf16[1,64,8,320]{3,2,0,1:T(8,128)(2,1)}), bf16[1,64,8,320]{3,2,0,1:T(8,128)(2,1)S(1)}, u32[]{:S(2)}, u32[]{:S(2)}) async-start(bf16[1,64,8,320]{3,2,0,1:T(8,128)(2,1)} %bitcast.93), calls=%async_computation.7 | async-start | bytes 786432 | tf_op jit(solution)/shard_map/all_to_all | solution.py:72
  171.3 1.9 copy.72
  174.0 1.9 copy.73
  177.8 5.3 %convolution_bitcast_fusion = f32[3,1280,320]{1,2,0:T(8,128)} fusion(bf16[512,1280,1]{1,0,2:T(8,128)(2,1)} %bitcast.105, bf16[1,512,320]{1,2,0:T(8,128)(2,1)} %copy.74, bf16[1,512,320]{1,2,0:T(8,128)(2,1)} %copy.73, bf16[1,512,320]{1,2,0:T(8,128)(2,1)} %copy.72), kind=kOutput, calls=%fused_computation.1 | convolution fusion | flops 1259274240 | bytes 7208960 | tf_op jit(solution)/shard_map/td,itk->idk/dot_general | solution.py:89
  183.1 9.1 %copy.75 = f32[3,1280,320]{2,0,1:T(4,128)} copy(f32[3,1280,320]{1,2,0:T(8,128)} %convolution_bitcast_fusion) | data formatting | bytes 9830400 | tf_op jit(solution)/shard_map/td,itk->idk/transpose | solution.py:89
  192.3 3.5 fusion.38
  196.9 2.6 fusion.1
  201.5 202.2 %all-reduce.8.cloned.1.call-done = (f32[3,1280,320]{2,0,1:T(4,128)}, f32[320,1280]{0,1:T(8,128)}) async-done(((f32[3,1280,320]{2,0,1:T(4,128)}, f32[320,1280]{0,1:T(8,128)}), (f32[3,1280,320]{2,0,1:T(4,128)}, f32[320,1280]{0,1:T(8,128)})) %all-reduce.8.cloned.1.call-update) | async-done | bytes 6553616
  406.6 51.8 %all-reduce.6.cloned.1.call-done = bf16[1,2,256,1280]{3,2,1,0:T(8,128)(2,1)} async-done(((bf16[1,2,256,1280]{3,2,1,0:T(8,128)(2,1)}), bf16[1,2,256,1280]{3,2,1,0:T(8,128)(2,1)}) %all-reduce.6.cloned.1.call-update) | async-done | bytes 1310736 | tf_op jit(solution)/shard_map/psum | solution.py:87
  458.4 2.5 copy.127
  (59 shorter events, 33.5 us)
Async XLA Ops:
  7.2 188.7 %copy-start = (bf16[3,1280,320]{1,2,0:T(8,128)(2,1)S(1)}, bf16[3,1280,320]{1,2,0:T(8,128)(2,1)}, u32[]{:S(2)}) copy-start(bf16[3,1280,320]{1,2,0:T(8,128)(2,1)} %param.12) | copy-start | bytes 7372804
  7.2 13.2 %copy-start.8 = (bf16[1,2,256,320]{2,3,1,0:T(8,128)(2,1)S(1)}, bf16[1,2,256,320]{2,3,1,0:T(8,128)(2,1)}, u32[]{:S(2)}) copy-start(bf16[1,2,256,320]{2,3,1,0:T(8,128)(2,1)} %param.8) | copy-start | bytes 983044
  9.3 24.9 %all-to-all-start = ((bf16[1,2,256,320]{3,1,0,2:T(2,128)(2,1)}), bf16[1,2,256,320]{3,1,0,2:T(2,128)(2,1)S(1)}, u32[]{:S(2)}, u32[]{:S(2)}) async-start(bf16[1,2,256,320]{3,1,0,2:T(2,128)(2,1)} %copy.43), calls=%async_computation | async-start | bytes 786432 | tf_op jit(solution)/shard_map/all_to_all | solution.py:78
  34.2 19.1 %all-to-all-start.1 = ((bf16[1,2,256,320]{3,1,0,2:T(2,128)(2,1)}), bf16[1,2,256,320]{3,1,0,2:T(2,128)(2,1)S(1)}, u32[]{:S(2)}, u32[]{:S(2)}) async-start(bf16[1,2,256,320]{3,1,0,2:T(2,128)(2,1)} %copy.46), calls=%async_computation.1 | async-start | bytes 786432 | tf_op jit(solution)/shard_map/all_to_all | solution.py:79
  53.3 19.8 %all-to-all-start.2 = ((bf16[1,2,256,320]{3,1,0,2:T(2,128)(2,1)}), bf16[1,2,256,320]{3,1,0,2:T(2,128)(2,1)}, u32[]{:S(2)}, u32[]{:S(2)}) async-start(bf16[1,2,256,320]{3,1,0,2:T(2,128)(2,1)} %copy.51), calls=%async_computation.2 | async-start | bytes 786432 | tf_op jit(solution)/shard_map/all_to_all | solution.py:81
  73.1 19.8 %all-to-all-start.3 = ((bf16[1,2,256,320]{3,1,0,2:T(2,128)(2,1)}), bf16[1,2,256,320]{3,1,0,2:T(2,128)(2,1)}, u32[]{:S(2)}, u32[]{:S(2)}) async-start(bf16[1,2,256,320]{3,1,0,2:T(2,128)(2,1)} %copy.54), calls=%async_computation.3 | async-start | bytes 786432 | tf_op jit(solution)/shard_map/all_to_all | solution.py:80
  83.3 13.6 %copy-start.1 = (bf16[64,8,4,80]{3,2,1,0:T(4,128)(2,1)}, bf16[64,8,4,80]{3,2,1,0:T(4,128)(2,1)S(1)}, u32[]{:S(2)}) copy-start(bf16[64,8,4,80]{3,2,1,0:T(4,128)(2,1)S(1)} %reshape.116) | copy-start | bytes 983044
  98.5 2.2 copy-start.6
  100.7 1.0 copy-start.2
  105.5 19.8 %all-to-all-start.4 = ((bf16[1,64,8,320]{3,2,0,1:T(8,128)(2,1)}), bf16[1,64,8,320]{3,2,0,1:T(8,128)(2,1)}, u32[]{:S(2)}, u32[]{:S(2)}) async-start(bf16[1,64,8,320]{3,2,0,1:T(8,128)(2,1)} %bitcast.96), calls=%async_computation.4 | async-start | bytes 786432 | tf_op jit(solution)/shard_map/all_to_all | solution.py:72
  111.7 18.8 %copy-start.7 = (bf16[64,8,4,80]{3,2,1,0:T(4,128)(2,1)S(1)}, bf16[64,8,4,80]{3,2,1,0:T(4,128)(2,1)}, u32[]{:S(2)}) copy-start(bf16[64,8,4,80]{3,2,1,0:T(4,128)(2,1)} %reshape.119) | copy-start | bytes 983044
  125.3 19.1 %all-to-all-start.5 = ((bf16[1,64,8,320]{3,2,0,1:T(8,128)(2,1)}), bf16[1,64,8,320]{3,2,0,1:T(8,128)(2,1)S(1)}, u32[]{:S(2)}, u32[]{:S(2)}) async-start(bf16[1,64,8,320]{3,2,0,1:T(8,128)(2,1)} %bitcast.19), calls=%async_computation.5 | async-start | bytes 786432 | tf_op jit(solution)/shard_map/all_to_all | solution.py:72
  144.4 19.8 %all-to-all-start.6 = ((bf16[1,64,8,320]{3,2,0,1:T(8,128)(2,1)}), bf16[1,64,8,320]{3,2,0,1:T(8,128)(2,1)}, u32[]{:S(2)}, u32[]{:S(2)}) async-start(bf16[1,64,8,320]{3,2,0,1:T(8,128)(2,1)} %bitcast.95), calls=%async_computation.6 | async-start | bytes 786432 | tf_op jit(solution)/shard_map/all_to_all | solution.py:72
  164.2 28.1 %all-to-all-start.7 = ((bf16[1,64,8,320]{3,2,0,1:T(8,128)(2,1)}), bf16[1,64,8,320]{3,2,0,1:T(8,128)(2,1)S(1)}, u32[]{:S(2)}, u32[]{:S(2)}) async-start(bf16[1,64,8,320]{3,2,0,1:T(8,128)(2,1)} %bitcast.93), calls=%async_computation.7 | async-start | bytes 786432 | tf_op jit(solution)/shard_map/all_to_all | solution.py:72
  169.5 234.1 %all-reduce.8.cloned.1.call-start = ((), (), s32[]{:S(2)}) async-start(), calls=%async_computation.9 | async-start | bytes 19660800
  195.8 1.0 copy-start.3
  195.8 1.1 copy-start.4
  195.8 1.2 copy-start.5
  195.8 262.6 %all-reduce.6.cloned.1.call-start = ((), (), s32[]{:S(2)}) async-start(), calls=%async_computation.8 | async-start | bytes 2621440 | tf_op jit(solution)/shard_map/psum | solution.py:87
  199.5 0.7 copy-start.9
Sparse Core Ops, SparseCore 0:
  195.9 207.6 all-reduce.7
  406.6 51.8 all-reduce.5
where the time goes:
time: 470 us; the launch traced here: 468 us
  waiting for transfers between devices  325 us (69%)
  local copies, waits for them, and re-layouts  55.2 us (12%)
  starting transfers between devices  50.2 us (11%)
  matrix products  22.2 us (5%)
  between operations  15 us (3%)
    unnamed x3, waiting for transfers between devices  202 us
    psum x1, waiting for transfers between devices, on_device(): grad_normed = lax.psum(partial_norm.astype(jnp.bfloat16), 'tensor')  51.8 us
    all_to_all x4, waiting for transfers between devices, regroup(): lax.all_to_all(shortened(results), 'tm', split_axis=1, concat_axis=2, til...  33.5 us
    all_to_all x4, starting transfers between devices, regroup(): lax.all_to_all(shortened(results), 'tm', split_axis=1, concat_axis=2, til...  22.2 us
    unnamed x28, local copies, waits for them, and re-layouts  13.7 us
    all_to_all x1, waiting for transfers between devices, on_device(): lax.all_to_all(queries, 'tm', split_axis=2, concat_axis=1, tiled=True)  12.7 us
    all_to_all x1, waiting for transfers between devices, on_device(): lax.all_to_all(grad_attn, 'tm', split_axis=2, concat_axis=1, tiled=True)  12 us
    all_to_all x1, starting transfers between devices, on_device(): lax.all_to_all(queries, 'tm', split_axis=2, concat_axis=1, tiled=True)  11.1 us
  transfers between devices with their start and end apart: 10, of which 9 were waited for; matrix products, arithmetic and copies ran while one was open for 12% of the time, Pallas kernels for 0%

commit v1 on v0

v1 whole, which is shorter than its diff:
```python
import functools

import jax
import jax.numpy as jnp
import numpy as np
from jax import lax
from jax.experimental import pallas as pl
from jax.experimental.pallas import tpu as pltpu
from jax.sharding import Mesh
from jax.sharding import PartitionSpec as P

HS = 80
HEADS = 4
W = HEADS * HS
D = 1280
NX = 4
NT = 32
FR = 2
PT = 8
TOK = 512
TEMPER = HS ** (-0.5)
TM = ("z", "yl", "core")
Y = ("dp", "yl")
BF = jnp.bfloat16
F32 = jnp.float32
LIMIT = 48 * 1024 * 1024


def feature_order():
    order = np.zeros(D, np.int32)
    at = 0
    for core in range(2):
        for y in range(4):
            for z in range(8):
                dp, yl = divmod(y, 2)
                start = (((dp * 8 + z) * 2 + yl) * 2 + core) * 20
                order[at : at + 20] = np.arange(start, start + 20)
                at += 20
    return order.reshape(NX, 1, W)


def dot(a, b):
    return lax.dot_general(a, b, (((1,), (0,)), ((), ())), preferred_element_type=F32)


def dot_nt(a, b):
    return lax.dot_general(a, b, (((1,), (1,)), ((), ())), preferred_element_type=F32)


def call(kernel, out_shape, flops=0, grid_spec=None, **kw):
    params = pltpu.CompilerParams(vmem_limit_bytes=LIMIT)
    cost = pl.CostEstimate(flops=flops, bytes_accessed=4_000_000, transcendentals=0)
    if grid_spec is not None:
        kw["grid_spec"] = grid_spec
    return pl.pallas_call(kernel, out_shape=out_shape, compiler_params=params, cost_estimate=cost, **kw)


def to_chunks(rows):
    width = rows.shape[-1]
    low = rows[: TOK // 2].reshape(NT, PT, width)
    high = rows[TOK // 2 :].reshape(NT, PT, width)
    return jnp.concatenate([low, high], axis=1).astype(BF)


def one_hot(feat_ref):
    places = lax.broadcasted_iota(jnp.int32, (D, W), 0)
    return jnp.where(places == feat_ref[...], 1.0, 0.0).astype(BF)


def pick_kernel(feat_ref, n_ref, go_ref, out_ref):
    pick = one_hot(feat_ref)
    for at, ref in enumerate((n_ref, go_ref)):
        rows = dot(ref[...].reshape(TOK, D), pick)
        out_ref[:, :, at * W : (at + 1) * W] = to_chunks(rows)


def pack_kernel(q_ref, k_ref, v_ref, out_ref):
    for at, ref in enumerate((q_ref, k_ref, v_ref)):
        rows = ref[...].astype(F32).reshape(TOK, W)
        out_ref[:, :, at * W : (at + 1) * W] = to_chunks(rows)


def reorder_kernel(feat_ref, w_ref, out_ref):
    for at in range(NX):
        out_ref[at] = dot(w_ref[...], one_hot(feat_ref.at[at])).astype(BF)


def attend_kernel(qkv_ref, ngo_ref, wout_ref, wqkv_ref, grads_ref, gnp_ref, g_s, kt_s, vt_s):
    acc = jnp.zeros((TOK, W), F32)
    for at in range(NX):
        acc = acc + dot_nt(ngo_ref[at].reshape(TOK, 2 * W)[:, W:], wout_ref[at])
    ga = acc.astype(BF)
    qkv = qkv_ref[...].reshape(TOK, 3 * W)
    q, k, v = qkv[:, :W], qkv[:, W : 2 * W], qkv[:, 2 * W :]
    q_t = q.astype(F32).T.astype(BF)
    ga_t = ga.astype(F32).T.astype(BF)
    block = 256
    row_patch = lax.broadcasted_iota(jnp.int32, (block, TOK), 0) % PT
    col_patch = lax.broadcasted_iota(jnp.int32, (block, TOK), 1) % PT
    same = row_patch == col_patch
    for h in range(HEADS):
        cols = slice(h * HS, (h + 1) * HS)
        kh, vh = k[:, cols], v[:, cols]
        dk_t = dv_t = None
        for b in range(TOK // block):
            rows = slice(b * block, (b + 1) * block)
            scores = dot_nt(q[rows, cols], kh) * TEMPER
            scores = jnp.where(same, scores, -jnp.inf)
            top = jnp.max(scores, axis=1, keepdims=True)
            powers = jnp.exp(scores - top)
            probs = powers / jnp.sum(powers, axis=1, keepdims=True)
            weights = probs.astype(BF)
            g_s[rows, 3 * W + h * HS : 3 * W + (h + 1) * HS] = dot(weights, vh)
            grad_probs = dot_nt(ga[rows, cols], vh)
            delta = jnp.sum(probs * grad_probs, axis=1, keepdims=True)
            grad_scores = (probs * (grad_probs - delta)).astype(BF)
            g_s[rows, h * HS : (h + 1) * HS] = dot(grad_scores, kh) * TEMPER
            dk_part = dot(q_t[cols, rows], grad_scores)
            dv_part = dot(ga_t[cols, rows], weights)
            dk_t = dk_part if dk_t is None else dk_t + dk_part
            dv_t = dv_part if dv_t is None else dv_t + dv_part
        kt_s[cols, :] = dk_t * TEMPER
        vt_s[cols, :] = dv_t
    g_s[:, W : 2 * W] = kt_s[...].T
    g_s[:, 2 * W : 3 * W] = vt_s[...].T
    grads = g_s[...].astype(BF)
    grads_ref[...] = grads
    for at in range(NX):
        part = jnp.zeros((TOK, W), F32)
        for i in range(3):
            part = part + dot_nt(grads[:, i * W : (i + 1) * W], wqkv_ref[i, at * W : (at + 1) * W, :])
        gnp_ref[at] = part.astype(BF)


def weight_kernel(half_ref, ngo_ref, grads_ref, out_ref):
    del half_ref
    ngo_t = ngo_ref[0].reshape(TOK, 2 * W).astype(F32).T.astype(BF)
    out_ref[:, : 3 * W] = dot(ngo_t[:W], grads_ref[:, : 3 * W]).astype(out_ref.dtype)
    out_ref[:, 3 * W :] = dot(ngo_t[W:], grads_ref[:, 3 * W :]).astype(out_ref.dtype)


def weight_half(half, ngo, grads, dtype):
    spec = pltpu.PrefetchScalarGridSpec(
        num_scalar_prefetch=1,
        grid=(2,),
        in_specs=[
            pl.BlockSpec((1, NT, 2 * PT, 2 * W), lambda j, half: (half[0] * 2 + j, 0, 0, 0)),
            pl.BlockSpec((TOK, 4 * W), lambda j, half: (0, 0)),
        ],
        out_specs=pl.BlockSpec((W, 4 * W), lambda j, half: (j, 0)),
    )
    return call(weight_kernel, jax.ShapeDtypeStruct((2 * W, 4 * W), dtype), 850_000_000, spec)(half, ngo, grads)


def spread_kernel(in_ref, out_ref):
    for at in range(NX):
        block = in_ref[at].astype(F32)
        for f in range(FR):
            rows = block[:, f * PT : (f + 1) * PT, :].reshape(NT * PT, W)
            out_ref[f, :, at * W : (at + 1) * W] = rows.astype(BF)


def on_device(queries, key_vectors, value_vectors, normed, grad_output, w_qkv, w_out):
    order = jnp.asarray(feature_order())
    x = lax.axis_index("x")
    core = lax.axis_index("core")
    mine = lax.dynamic_index_in_dim(order, x, 0, keepdims=False)
    ngo = call(pick_kernel, jax.ShapeDtypeStruct((NT, 2 * PT, 2 * W), BF), 850_000_000)(
        mine, normed[0], grad_output[0]
    )
    ngo = lax.all_to_all(ngo, TM, 0, 0, tiled=True)
    ngo = lax.all_gather(ngo, "x", axis=0)
    qkv = call(pack_kernel, jax.ShapeDtypeStruct((NT, 2 * PT, 3 * W), BF))(
        queries[0], key_vectors[0], value_vectors[0]
    )
    qkv = lax.all_to_all(qkv, TM, 0, 0, tiled=True)
    w_ordered = call(reorder_kernel, jax.ShapeDtypeStruct((NX, W, W), BF), 1_000_000_000)(order, w_out)
    grads, part_norm = call(
        attend_kernel,
        (jax.ShapeDtypeStruct((TOK, 4 * W), BF), jax.ShapeDtypeStruct((NX, TOK, W), BF)),
        5_000_000_000,
        scratch_shapes=[pltpu.VMEM((TOK, 4 * W), F32), pltpu.VMEM((W, TOK), F32), pltpu.VMEM((W, TOK), F32)],
    )(qkv, ngo, w_ordered, w_qkv)

    sent = weight_half((1 - core).reshape(1), ngo, grads, BF)
    got = lax.ppermute(sent, "core", [(0, 1), (1, 0)])
    kept = weight_half(core.reshape(1), ngo, grads, F32)
    both = (kept + got.astype(F32)).astype(BF).reshape(4, D // 8, 4 * W)
    quarter = lax.psum_scatter(both, Y, scatter_dimension=0, tiled=True)

    part_norm = lax.all_to_all(part_norm, "x", 0, 0, tiled=True)
    own_norm = jnp.sum(part_norm.astype(F32), axis=0).astype(BF).reshape(NT, 2 * PT, W)
    own_norm = lax.all_to_all(own_norm, TM, 0, 0, tiled=True)
    all_norm = lax.all_gather(own_norm, "x", axis=0)
    grad_normed = call(spread_kernel, jax.ShapeDtypeStruct((FR, 256, D), BF))(all_norm)

    pieces = lax.all_to_all(quarter.reshape(8, 20, 4 * W), "z", 0, 0, tiled=True)
    total = jnp.sum(pieces.astype(F32), axis=0)
    grad_qkv = total[:, : 3 * W].reshape(20, 3, W).transpose(1, 0, 2)
    grad_out = total[:, 3 * W :].T
    return (grad_normed[None], grad_qkv, grad_out)


def solution(mesh):
    own = Mesh(mesh.devices.reshape(2, 8, 2, 2, 4), ("dp", "z", "yl", "core", "x"))
    in_specs = (
        P("dp", TM, None, "x"),
        P("dp", TM, None, "x"),
        P("dp", TM, None, "x"),
        P("dp", TM, None, None),
        P("dp", TM, None, None),
        P(None, None, "x"),
        P("x", None),
    )
    out_specs = (
        P("dp", TM, None, None),
        P(None, ("dp",) + TM, "x"),
        P("x", ("dp",) + TM),
    )
    return jax.shard_map(on_device, mesh=own, in_specs=in_specs, out_specs=out_specs, check_vma=False)
```

time: 470 us -> 184 us (0.39)
  waiting for transfers between devices: 325 us -> 39.5 us
  blocking collectives: 0 us -> 73.4 us
  starting transfers between devices: 50.2 us -> 10.1 us
  local copies, waits for them, and re-layouts: 55.2 us -> 17.2 us
  Pallas kernels: 0 us -> 25.2 us
  matrix products: 22.2 us -> 0 us
    unnamed x3, waiting for transfers between devices: 202 us -> 0.05 us
    all_to_all x0 -> x3, blocking collectives: none -> 73.4 us  [the longest x1 30.8 us: on_device(): ngo = lax.all_to_all(ngo, TM, 0, 0, tiled=True)]
    psum x1 -> x0, waiting for transfers between devices: 51.8 us -> none  [on_device(): grad_normed = lax.psum(partial_norm.astype(jnp.bfloat16), 'tensor')]
    all_to_all x8 -> x2, waiting for transfers between devices: 70.9 us -> 19.8 us  [the longest x1 19.7 us: on_device(): qkv = lax.all_to_all(qkv, TM, 0, 0, tiled=True)]
    all_to_all x8 -> x2, starting transfers between devices: 50.1 us -> 8.41 us  [the longest x1 4.93 us: on_device(): qkv = lax.all_to_all(qkv, TM, 0, 0, tiled=True)]
    pallas_call x0 -> x7, Pallas kernels: none -> 25.2 us  [the longest x1 14.4 us: on_device(): call(attend_kernel, (jax.ShapeDtypeStruct((TOK, 4 * W), BF), jax.ShapeDty...]
    dot_general x9 -> x0, matrix products: 20.5 us -> none  [the longest x1 5.28 us: on_device(): jnp.einsum('td,itk->idk', rows_norm, stacked, preferred_element_type=jnp....]
    all_gather x0 -> x2, waiting for transfers between devices: none -> 19.4 us  [the longest x1 19.4 us: on_device(): all_norm = lax.all_gather(own_norm, 'x', axis=0)]
  transfers between devices with their start and end apart: 10 -> 6, of which waited for: 9 -> 4; matrix products, arithmetic and copies ran while one was open for 12% -> 5% of each run, Pallas kernels for 0% -> 4%
where the time goes in v1:
time: 184 us; the launch traced here: 183 us
  blocking collectives  73.4 us (40%)
  waiting for transfers between devices  39.5 us (21%)
  Pallas kernels  25.2 us (14%)
  local copies, waits for them, and re-layouts  17.2 us (9%)
  between operations  13.9 us (8%)
  starting transfers between devices  10.1 us (5%)
  other arithmetic  3.87 us (2%)
    all_to_all x1, blocking collectives, on_device(): ngo = lax.all_to_all(ngo, TM, 0, 0, tiled=True)  30.8 us
    all_to_all x1, blocking collectives, on_device(): own_norm = lax.all_to_all(own_norm, TM, 0, 0, tiled=True)  21.7 us
    all_to_all x1, blocking collectives, on_device(): part_norm = lax.all_to_all(part_norm, 'x', 0, 0, tiled=True)  20.9 us
    all_to_all x1, waiting for transfers between devices, on_device(): qkv = lax.all_to_all(qkv, TM, 0, 0, tiled=True)  19.7 us
    all_gather x1, waiting for transfers between devices, on_device(): all_norm = lax.all_gather(own_norm, 'x', axis=0)  19.4 us
    pallas_call x1, Pallas kernels, on_device(): call(attend_kernel, (jax.ShapeDtypeStruct((TOK, 4 * W), BF), jax.ShapeDty...  14.4 us
    unnamed x27, local copies, waits for them, and re-layouts  12.9 us
    all_to_all x1, starting transfers between devices, on_device(): qkv = lax.all_to_all(qkv, TM, 0, 0, tiled=True)  4.93 us
  transfers between devices with their start and end apart: 6, of which 4 were waited for; matrix products, arithmetic and copies ran while one was open for 5% of the time, Pallas kernels for 4%

profile of v1, /device:TPU:1, one launch (start us, length us, event | category | flops | bytes accessed | tf_op | source)
XLA Modules:
  0.0 183.3 jit_solution(13792214676494833117)
XLA Ops:
  7.2 0.7 dynamic-slice_bitcast_fusion.feat_ref
  7.9 1.3 copy-done.2
  9.2 1.3 copy-done.3
  10.5 1.6 shard_map.104
  12.2 30.8 %all_to_all.25 = bf16[32,16,640]{2,1,0:T(8,128)(2,1)} all-to-all(bf16[32,16,640]{2,1,0:T(8,128)(2,1)S(1)} %shard_map.104), channel_id=1, replica_groups=mesh['dp'=2,'z'=8,'yl'=2,'core'=2,'x'=4] {'z','yl','core'}, dimensions={0} | all-to-all | bytes 1310720 | tf_op jit(solution)/shard_map/all_to_all | solution.py:171
  43.0 0.2 copy.34
  43.5 0.2 copy.36
  43.7 1.2 shard_map.103
  44.9 4.9 %all-to-all-start = ((bf16[32,16,960]{2,1,0:T(8,128)(2,1)}), bf16[32,16,960]{2,1,0:T(8,128)(2,1)S(1)}, u32[]{:S(2)}, u32[]{:S(2)}) async-start(bf16[32,16,960]{2,1,0:T(8,128)(2,1)} %shard_map.103), calls=%async_computation | async-start | bytes 2097152 | tf_op jit(solution)/shard_map/all_to_all | solution.py:176
  49.9 0.2 reduce-scatter.2.cloned.1.call-start
  50.1 5.3 %copy.37.wqkv_ref = bf16[3,1280,320]{2,1,0:T(8,128)(2,1)} copy(bf16[3,1280,320]{1,2,0:T(8,128)(2,1)} %param.13) | data formatting | bytes 4915200 | tf_op args[5]
  55.5 1.9 %shard_map.105.wout_ref = bf16[4,320,320]{2,1,0:T(8,128)(2,1)S(1)} custom-call(s32[4,1,320]{2,1,0:T(1,128)S(1)} %copy-done.4, bf16[320,1280]{1,0:T(8,128)(2,1)S(1)} %copy-done.5), custom_call_target="tpu_custom_call" | custom-call | flops 1000000000 | bytes 4000000 | tf_op jit(solution)/shard_map/pallas_call | solution.py:177
  57.3 1.0 copy-done.6
  58.3 19.7 %all-to-all-done.qkv_ref = bf16[32,16,960]{2,1,0:T(8,128)(2,1)S(1)} async-done(((bf16[32,16,960]{2,1,0:T(8,128)(2,1)}), bf16[32,16,960]{2,1,0:T(8,128)(2,1)S(1)}, u32[]{:S(2)}, u32[]{:S(2)}) %all-to-all-start) | async-done | bytes 983072 | tf_op jit(solution)/shard_map/all_to_all | solution.py:176
  78.1 1.2 copy-done.7
  79.3 14.4 %shard_map.106 = (bf16[512,1280]{1,0:T(8,128)(2,1)S(1)}, bf16[4,512,320]{2,1,0:T(8,128)(2,1)S(1)}) custom-call(bf16[32,16,960]{2,1,0:T(8,128)(2,1)S(1)} %all-to-all-done.qkv_ref, bf16[4,32,16,640]{3,2,1,0:T(8,128)(2,1)} %bitcast.17, bf16[4,320,320]{2,1,0:T(8,128)(2,1)S(1)} %copy-done.7, bf16[3,1280,320]{2,1,0:T(8,128)(2,1)} %copy.37.wqkv_ref), custom_call_target="tpu_custom_call" | custom-call | flops 5000000000 | bytes 4000000 | tf_op jit(solution)/shard_map/pallas_call | solution.py:178
  93.8 1.9 %shard_map.109 = bf16[640,1280]{1,0:T(8,128)(2,1)S(1)} custom-call(s32[1]{0:T(128)} %bitcast.11.half_ref, bf16[4,32,16,640]{3,2,1,0:T(8,128)(2,1)S(1)} %bitcast.18, bf16[512,1280]{1,0:T(8,128)(2,1)S(1)} %get-tuple-element.6.grads_ref), custom_call_target="tpu_custom_call" | custom-call | flops 850000000 | bytes 4000000 | tf_op jit(solution)/shard_map/pallas_call | solution.py:152
  95.6 1.4 collective-permute-start
  97.0 2.9 %shard_map.108 = f32[640,1280]{1,0:T(8,128)} custom-call(s32[1]{0:T(128)} %bitcast.10.half_ref, bf16[4,32,16,640]{3,2,1,0:T(8,128)(2,1)S(1)} %bitcast.19, bf16[512,1280]{1,0:T(8,128)(2,1)S(1)} %get-tuple-element.6.grads_ref), custom_call_target="tpu_custom_call" | custom-call | flops 850000000 | bytes 4000000 | tf_op jit(solution)/shard_map/pallas_call | solution.py:152
  99.9 0.3 collective-permute-done
  100.2 3.5 %add_convert_fusion = bf16[640,1280]{1,0:T(8,128)(2,1)} fusion(f32[640,1280]{1,0:T(8,128)} %shard_map.108, bf16[640,1280]{1,0:T(8,128)(2,1)S(1)} %collective-permute-done), kind=kLoop, calls=%fused_computation | loop fusion | flops 2457600 | bytes 6553600 | tf_op jit(solution)/shard_map/convert_element_type | solution.py:188
  103.7 0.7 copy.38
  104.4 20.9 %all_to_all.26 = bf16[4,512,320]{1,2,0:T(8,128)(2,1)S(1)} all-to-all(bf16[4,512,320]{1,2,0:T(8,128)(2,1)S(1)} %copy.38), channel_id=1, replica_groups=mesh['dp'=2,'z'=8,'yl'=2,'core'=2,'x'=4] {'x'}, dimensions={0} | all-to-all | bytes 2621440 | tf_op jit(solution)/shard_map/all_to_all | solution.py:191
  125.3 0.3 reduce_sum.21
  125.9 21.7 %all_to_all.27 = bf16[32,16,320]{2,1,0:T(8,128)(2,1)} all-to-all(bf16[32,16,320]{2,1,0:T(8,128)(2,1)S(1)} %bitcast.27), channel_id=1, replica_groups=mesh['dp'=2,'z'=8,'yl'=2,'core'=2,'x'=4] {'z','yl','core'}, dimensions={0} | all-to-all | bytes 655360 | tf_op jit(solution)/shard_map/all_to_all | solution.py:193
  147.6 1.9 %reshape.28 = bf16[8,20,1280]{2,1,0:T(8,128)(2,1)} reshape(bf16[1,160,1280]{2,1,0:T(8,128)(2,1)} %reduce-scatter.2.cloned.1.call-done) | data formatting | bytes 819200 | tf_op jit(solution)/shard_map/reshape | solution.py:197
  149.5 3.5 %all-to-all-start.4 = ((bf16[8,20,1280]{2,1,0:T(8,128)(2,1)}), bf16[8,20,1280]{2,1,0:T(8,128)(2,1)S(1)}, u32[]{:S(2)}, u32[]{:S(2)}) async-start(bf16[8,20,1280]{2,1,0:T(8,128)(2,1)} %reshape.28), calls=%async_computation.5 | async-start | bytes 983040 | tf_op jit(solution)/shard_map/all_to_all | solution.py:197
  153.0 19.4 %all-gather.7.cloned.1.call-done = bf16[128,16,320]{2,1,0:T(8,128)(2,1)} async-done(((bf16[32,16,320]{2,1,0:T(8,128)(2,1)}), bf16[128,16,320]{2,1,0:T(8,128)(2,1)}) %all-gather.7.cloned.1.call-update) | async-done | bytes 1310736 | tf_op jit(solution)/shard_map/all_gather | solution.py:194
  172.4 1.4 copy-done.1
  173.8 1.4 shard_map.107
  175.3 0.7 slice_bitcast_fusion
  176.1 0.7 copy.40
  (30 shorter events, 0.9 us)
Async XLA Ops:
  7.2 71.0 %all-gather.5.cloned.1.call-start = ((), (), s32[]{:S(2)}) async-start(), calls=%async_computation.7 | async-start | bytes 3276800 | tf_op jit(solution)/shard_map/all_gather | solution.py:172
  7.9 1.3 copy-start.2
  9.2 1.3 copy-start.3
  12.2 30.9 %copy-start.8 = (bf16[1,2,256,320]{2,3,1,0:T(8,128)(2,1)S(1)}, bf16[1,2,256,320]{2,3,1,0:T(8,128)(2,1)}, u32[]{:S(2)}) copy-start(bf16[1,2,256,320]{2,3,1,0:T(8,128)(2,1)} %param.8) | copy-start | bytes 983044
  12.2 31.1 %copy-start.9 = (bf16[1,2,256,320]{2,3,1,0:T(8,128)(2,1)S(1)}, bf16[1,2,256,320]{2,3,1,0:T(8,128)(2,1)}, u32[]{:S(2)}) copy-start(bf16[1,2,256,320]{2,3,1,0:T(8,128)(2,1)} %param.9) | copy-start | bytes 983044
  12.2 31.3 %copy-start.10 = (bf16[1,2,256,320]{2,3,1,0:T(8,128)(2,1)S(1)}, bf16[1,2,256,320]{2,3,1,0:T(8,128)(2,1)}, u32[]{:S(2)}) copy-start(bf16[1,2,256,320]{2,3,1,0:T(8,128)(2,1)} %param.10) | copy-start | bytes 983044
  44.9 33.1 %all-to-all-start = ((bf16[32,16,960]{2,1,0:T(8,128)(2,1)}), bf16[32,16,960]{2,1,0:T(8,128)(2,1)S(1)}, u32[]{:S(2)}, u32[]{:S(2)}) async-start(bf16[32,16,960]{2,1,0:T(8,128)(2,1)} %shard_map.103), calls=%async_computation | async-start | bytes 2097152 | tf_op jit(solution)/shard_map/all_to_all | solution.py:176
  49.9 5.6 %copy-start.4 = (s32[4,1,320]{2,1,0:T(1,128)S(1)}, s32[4,1,320]{2,1,0:T(1,128)}, u32[]{:S(2)}) copy-start(s32[4,1,320]{2,1,0:T(1,128)} %constant.23.clone.feat_ref) | copy-start | bytes 15364
  49.9 5.6 %copy-start.5 = (bf16[320,1280]{1,0:T(8,128)(2,1)S(1)}, bf16[320,1280]{1,0:T(8,128)(2,1)}, u32[]{:S(2)}) copy-start(bf16[320,1280]{1,0:T(8,128)(2,1)} %w_ref.1) | copy-start | bytes 2457604
  49.9 97.8 %reduce-scatter.2.cloned.1.call-start = ((), (), s32[]{:S(2)}) async-start(), calls=%async_computation.6 | async-start | bytes 2048000 | tf_op jit(solution)/shard_map/reduce_scatter | solution.py:189
  57.3 1.0 copy-start.6
  78.1 1.2 copy-start.7
  79.3 14.4 %copy-start = (bf16[128,16,640]{2,1,0:T(8,128)(2,1)S(1)}, bf16[128,16,640]{2,1,0:T(8,128)(2,1)}, u32[]{:S(2)}) copy-start(bf16[128,16,640]{2,1,0:T(8,128)(2,1)} %all-gather.5.cloned.1.call-done) | copy-start | bytes 7864324
  95.6 4.5 %collective-permute-start = (bf16[640,1280]{1,0:T(8,128)(2,1)S(1)}, bf16[640,1280]{1,0:T(8,128)(2,1)S(1)}, u32[]{:S(2)}, u32[]{:S(2)}) collective-permute-start(bf16[640,1280]{1,0:T(8,128)(2,1)S(1)} %shard_map.109), channel_id=1, source_target_pairs={{0,4},{4,0},{1,5},{5,1},{2,6},{6,2},{3,7},{7,3},{8,12},{12,8},{9,1... | collective-permute-start | bytes 4915208 | tf_op jit(solution)/shard_map/ppermute | solution.py:186
  103.7 68.8 %all-gather.7.cloned.1.call-start = ((), (), s32[]{:S(2)}) async-start(), calls=%async_computation.8 | async-start | bytes 1966080 | tf_op jit(solution)/shard_map/all_gather | solution.py:194
  149.5 25.7 %all-to-all-start.4 = ((bf16[8,20,1280]{2,1,0:T(8,128)(2,1)}), bf16[8,20,1280]{2,1,0:T(8,128)(2,1)S(1)}, u32[]{:S(2)}, u32[]{:S(2)}) async-start(bf16[8,20,1280]{2,1,0:T(8,128)(2,1)} %reshape.28), calls=%async_computation.5 | async-start | bytes 983040 | tf_op jit(solution)/shard_map/all_to_all | solution.py:197
  172.4 1.4 copy-start.1
Sparse Core Ops, SparseCore 0:
  43.1 34.9 all-gather.4
  103.8 27.3 reduce-scatter.1
  147.7 24.6 all-gather.6

commit v2 on v1

v2 whole, which is shorter than its diff:
```python
import functools

import jax
import jax.numpy as jnp
import numpy as np
from jax import lax
from jax.experimental import pallas as pl
from jax.experimental.pallas import tpu as pltpu
from jax.sharding import Mesh
from jax.sharding import PartitionSpec as P

HS = 80
HEADS = 4
W = HEADS * HS
D = 1280
NX = 4
NT = 32
FR = 2
PT = 8
TOK = 512
FRAMES = 64
LANES = 128
TILES = 4 * W // LANES
BLOCK = 128
TEMPER = HS ** (-0.5)
TM = ("z", "yl", "core")
Y = ("dp", "yl")
BF = jnp.bfloat16
F32 = jnp.float32
LIMIT = 48 * 1024 * 1024


def feature_order():
    order = np.zeros(D, np.int32)
    at = 0
    for core in range(2):
        for y in range(4):
            for z in range(8):
                dp, yl = divmod(y, 2)
                start = (((dp * 8 + z) * 2 + yl) * 2 + core) * 20
                order[at : at + 20] = np.arange(start, start + 20)
                at += 20
    return order.reshape(NX, 1, W)


def dot(a, b):
    return lax.dot_general(a, b, (((1,), (0,)), ((), ())), preferred_element_type=F32)


def dot_nt(a, b):
    return lax.dot_general(a, b, (((1,), (1,)), ((), ())), preferred_element_type=F32)


def call(kernel, out_shape, flops=0, grid_spec=None, limit=LIMIT, **kw):
    params = pltpu.CompilerParams(vmem_limit_bytes=limit)
    cost = pl.CostEstimate(flops=flops, bytes_accessed=4_000_000, transcendentals=0)
    if grid_spec is not None:
        kw["grid_spec"] = grid_spec
    return pl.pallas_call(kernel, out_shape=out_shape, compiler_params=params, cost_estimate=cost, **kw)


def to_chunks(rows):
    width = rows.shape[-1]
    low = rows[: TOK // 2].reshape(NT, PT, width)
    high = rows[TOK // 2 :].reshape(NT, PT, width)
    return jnp.concatenate([low, high], axis=1).astype(BF)


def one_hot(feat_ref):
    places = lax.broadcasted_iota(jnp.int32, (D, W), 0)
    return jnp.where(places == feat_ref[...], 1.0, 0.0).astype(BF)


def prepare_kernel(feat_ref, n_ref, go_ref, q_ref, k_ref, v_ref, ngo_ref, qkv_ref):
    pick = one_hot(feat_ref)
    for at, ref in enumerate((n_ref, go_ref)):
        rows = dot(ref[...].reshape(TOK, D), pick)
        ngo_ref[:, :, at * W : (at + 1) * W] = to_chunks(rows)
    for at, ref in enumerate((q_ref, k_ref, v_ref)):
        rows = jnp.concatenate([ref[f].astype(F32).T for f in range(FR)], axis=0)
        qkv_ref[:, :, at * W : (at + 1) * W] = to_chunks(rows)


def reorder_kernel(feat_ref, w_ref, out_ref):
    for at in range(NX):
        out_ref[at] = dot(w_ref[...], one_hot(feat_ref.at[at])).astype(BF)


def attend_kernel(x_ref, qkv_ref, ngo_ref, wout_ref, wqkv_ref, grads_ref, *rest):
    norm_refs, (wide_s, rows_s, all_t, g_t, norm_s) = rest[:NX], rest[NX:]
    acc = jnp.zeros((TOK, W), F32)
    for at in range(NX):
        acc = acc + dot_nt(ngo_ref[at].reshape(TOK, 2 * W)[:, W:], wout_ref[at])
    ga = acc.astype(BF).astype(F32)
    half = LANES // 2
    for t in range(7):
        wide_s[t] = qkv_ref[:, :, t * LANES : (t + 1) * LANES].reshape(TOK, LANES).astype(F32)
    wide_s[7, :, :half] = qkv_ref[:, :, 7 * LANES :].reshape(TOK, half).astype(F32)
    wide_s[7, :, half:] = ga[:, :half]
    for t in (8, 9):
        wide_s[t] = ga[:, (t - 8) * LANES + half : (t - 7) * LANES + half]
    for p in range(PT):
        for t in range(TILES):
            rows_s[p * FRAMES : (p + 1) * FRAMES, t * LANES : (t + 1) * LANES] = wide_s[
                t, pl.ds(p, FRAMES, stride=PT), :
            ].astype(BF)
    all_t[...] = rows_s[...].T
    row_patch = lax.broadcasted_iota(jnp.int32, (BLOCK, BLOCK), 0) // FRAMES
    col_patch = lax.broadcasted_iota(jnp.int32, (BLOCK, BLOCK), 1) // FRAMES
    same = row_patch == col_patch
    for b in range(TOK // BLOCK):
        rows = slice(b * BLOCK, (b + 1) * BLOCK)
        for h in range(HEADS):
            at = [slice(i * W + h * HS, i * W + (h + 1) * HS) for i in range(4)]
            q_t, k_t, v_t, ga_t = [all_t[cols, rows] for cols in at]
            scores = dot(rows_s[rows, at[1]], q_t) * TEMPER
            scores = jnp.where(same, scores, -jnp.inf)
            powers = jnp.exp(scores - jnp.max(scores, axis=0, keepdims=True))
            probs = powers * (1.0 / jnp.sum(powers, axis=0, keepdims=True))
            weights = probs.astype(BF)
            g_t[at[3], rows] = dot(v_t, weights)
            grad_probs = dot(rows_s[rows, at[2]], ga_t)
            delta = jnp.sum(probs * grad_probs, axis=0, keepdims=True)
            grad_scores = (probs * (grad_probs - delta)).astype(BF)
            g_t[at[0], rows] = dot(k_t, grad_scores) * TEMPER
            g_t[at[1], rows] = dot_nt(q_t, grad_scores) * TEMPER
            g_t[at[2], rows] = dot_nt(ga_t, weights)
    for t in range(TILES):
        tile = g_t[t * LANES : (t + 1) * LANES, :].T
        for p in range(PT):
            wide_s[t, pl.ds(p, FRAMES, stride=PT), :] = tile[p * FRAMES : (p + 1) * FRAMES]
    for t in range(TILES):
        grads_ref[:, t * LANES : (t + 1) * LANES] = wide_s[t].astype(BF)
    norm = dot(grads_ref[:, : 3 * W], wqkv_ref[...])
    for at in range(NX):
        part = norm[:, at * W : (at + 1) * W].reshape(NT, 2 * PT, W)
        slot = lax.rem(at + NX - x_ref[0], NX)
        for f in range(FR):
            norm_s[slot, :, f * W : (f + 1) * W] = part[:, f * PT : (f + 1) * PT, :].reshape(NT * PT, W).astype(BF)
    for at in range(NX):
        norm_refs[at][...] = norm_s[at]


def attend(x, qkv, ngo, w_ordered, w_qkv):
    scalar = pl.BlockSpec(memory_space=pltpu.SMEM)
    whole = pl.BlockSpec(memory_space=pltpu.VMEM)
    return call(
        attend_kernel,
        (jax.ShapeDtypeStruct((TOK, 4 * W), BF),) + (jax.ShapeDtypeStruct((TOK // 2, 2 * W), BF),) * NX,
        5_000_000_000,
        in_specs=[scalar] + [whole] * 4,
        scratch_shapes=[
            pltpu.VMEM((TILES, TOK, LANES), F32),
            pltpu.VMEM((TOK, 4 * W), BF),
            pltpu.VMEM((4 * W, TOK), BF),
            pltpu.VMEM((4 * W, TOK), F32),
            pltpu.VMEM((NX, TOK // 2, 2 * W), BF),
        ],
    )(x, qkv, ngo, w_ordered, w_qkv)


def weight_kernel(half_ref, ngo_ref, grads_ref, *refs):
    del half_ref
    out_ref = refs[-1]
    ngo_t = ngo_ref[0].reshape(TOK, 2 * W).astype(F32).T.astype(BF)
    for rows, cols in ((slice(0, W), slice(0, 3 * W)), (slice(W, 2 * W), slice(3 * W, 4 * W))):
        total = dot(ngo_t[rows], grads_ref[:, cols])
        if len(refs) == 2:
            total = total + refs[0][:, cols].astype(F32)
        out_ref[:, cols] = total.astype(BF)


def weight_half(half, ngo, grads, *got):
    block = pl.BlockSpec((W, 4 * W), lambda j, half: (j, 0))
    spec = pltpu.PrefetchScalarGridSpec(
        num_scalar_prefetch=1,
        grid=(2,),
        in_specs=[
            pl.BlockSpec((1, NT, 2 * PT, 2 * W), lambda j, half: (half[0] * 2 + j, 0, 0, 0)),
            pl.BlockSpec((TOK, 4 * W), lambda j, half: (0, 0)),
        ]
        + [block] * len(got),
        out_specs=block,
    )
    shape = jax.ShapeDtypeStruct((2 * W, 4 * W), BF)
    return call(weight_kernel, shape, 4_000_000_000, spec)(half, ngo, grads, *got)


def add_kernel(*refs):
    total = refs[0][...].astype(F32)
    for ref in refs[1:-1]:
        total = total + ref[...].astype(F32)
    refs[-1][...] = total.astype(BF)


def spread_kernel(x_ref, *refs):
    out_ref = refs[-1]
    for at in range(NX):
        for k in range(NX):

            @pl.when(lax.rem(x_ref[0] + NX - k, NX) == at)
            def _(at=at, k=k):
                for f in range(FR):
                    out_ref[f, :, at * W : (at + 1) * W] = refs[k][:, f * W : (f + 1) * W]


def shift(array, k):
    return lax.ppermute(array, "x", [(i, (i + k) % NX) for i in range(NX)])


def on_device(queries, key_vectors, value_vectors, normed, grad_output, w_qkv, w_out):
    order = jnp.asarray(feature_order())
    x = lax.axis_index("x")
    core = lax.axis_index("core")
    scalar = pl.BlockSpec(memory_space=pltpu.SMEM)
    whole = pl.BlockSpec(memory_space=pltpu.VMEM)
    mine = lax.dynamic_index_in_dim(order, x, 0, keepdims=False)
    ngo, qkv = call(
        prepare_kernel,
        (jax.ShapeDtypeStruct((NT, 2 * PT, 2 * W), BF), jax.ShapeDtypeStruct((NT, 2 * PT, 3 * W), BF)),
        850_000_000,
        limit=60 * 1024 * 1024,
    )(mine, normed[0], grad_output[0], *[jnp.swapaxes(item[0], 1, 2) for item in (queries, key_vectors, value_vectors)])
    ngo = lax.all_to_all(ngo, TM, 0, 0, tiled=True)
    ngo = lax.all_gather(ngo, "x", axis=0)
    qkv = lax.all_to_all(qkv, TM, 0, 0, tiled=True)
    w_ordered = call(reorder_kernel, jax.ShapeDtypeStruct((NX, W, W), BF), 1_000_000_000)(order, w_out)
    grads, *parts = attend(x.reshape(1), qkv, ngo, w_ordered, jnp.swapaxes(w_qkv, 1, 2).reshape(3 * W, D))

    moved = [parts[0]] + [shift(parts[k], k) for k in range(1, NX)]
    sent = weight_half((1 - core).reshape(1), ngo, grads)
    got = lax.ppermute(sent, "core", [(0, 1), (1, 0)])
    both = weight_half(core.reshape(1), ngo, grads, got).reshape(4, D // 8, 4 * W)
    quarter = lax.psum_scatter(both, Y, scatter_dimension=0, tiled=True)

    own_norm = call(add_kernel, jax.ShapeDtypeStruct((TOK // 2, 2 * W), BF), 40_000_000_000)(*moved)
    own_norm = lax.all_to_all(own_norm.reshape(NT, PT, 2 * W), TM, 0, 0, tiled=True).reshape(TOK // 2, 2 * W)
    all_norm = [own_norm] + [shift(own_norm, k) for k in range(1, NX)]
    grad_normed = call(
        spread_kernel, jax.ShapeDtypeStruct((FR, TOK // 2, D), BF), in_specs=[scalar] + [whole] * NX
    )(x.reshape(1), *all_norm)

    pieces = lax.all_to_all(quarter.reshape(8, 20, 4 * W), "z", 0, 0, tiled=True)
    total = jnp.sum(pieces.astype(F32), axis=0)
    grad_qkv = total[:, : 3 * W].reshape(20, 3, W).transpose(1, 0, 2)
    grad_out = total[:, 3 * W :].T
    return (grad_normed[None], grad_qkv, grad_out)


def solution(mesh):
    own = Mesh(mesh.devices.reshape(2, 8, 2, 2, 4), ("dp", "z", "yl", "core", "x"))
    in_specs = (
        P("dp", TM, None, "x"),
        P("dp", TM, None, "x"),
        P("dp", TM, None, "x"),
        P("dp", TM, None, None),
        P("dp", TM, None, None),
        P(None, None, "x"),
        P("x", None),
    )
    out_specs = (
        P("dp", TM, None, None),
        P(None, ("dp",) + TM, "x"),
        P("x", ("dp",) + TM),
    )
    return jax.shard_map(on_device, mesh=own, in_specs=in_specs, out_specs=out_specs, check_vma=False)
```

time: 184 us -> 171 us (0.929)
  blocking collectives: 73.4 us -> 30.8 us
  waiting for transfers between devices: 39.5 us -> 66.2 us
  starting transfers between devices: 10.1 us -> 28.9 us
  local copies, waits for them, and re-layouts: 17.2 us -> 4.6 us
  other arithmetic: 3.87 us -> 0.08 us
    all_to_all x2 -> x0, blocking collectives: 42.6 us -> none  [the longest x1 21.7 us: on_device(): own_norm = lax.all_to_all(own_norm, TM, 0, 0, tiled=True)]
    ppermute x0 -> x6, waiting for transfers between devices: none -> 27.2 us  [shift(): return lax.ppermute(array, 'x', [(i, (i + k) % NX) for i in range(NX)])]
    all_gather x1 -> x0, waiting for transfers between devices: 19.4 us -> none  [on_device(): all_norm = lax.all_gather(own_norm, 'x', axis=0)]
    unnamed x27 -> x7, local copies, waits for them, and re-layouts: 12.9 us -> 0.67 us
    all_to_all x0 -> x1, starting transfers between devices: none -> 9.27 us  [on_device(): lax.all_to_all(own_norm.reshape(NT, PT, 2 * W), TM, 0, 0, tiled=True)]
    reduce_scatter x1, waiting for transfers between devices: 0.02 us -> 8.34 us  [on_device(): quarter = lax.psum_scatter(both, Y, scatter_dimension=0, tiled=True)]
    ppermute x0 -> x6, starting transfers between devices: none -> 7.75 us  [shift(): return lax.ppermute(array, 'x', [(i, (i + k) % NX) for i in range(NX)])]
    all_to_all x1, waiting for transfers between devices: 19.7 us -> 26.3 us  [on_device(): qkv = lax.all_to_all(qkv, TM, 0, 0, tiled=True)]
  transfers between devices with their start and end apart: 6 -> 12, of which waited for: 4 -> 10; matrix products, arithmetic and copies ran while one was open for 5% -> 1% of each run, Pallas kernels for 4% -> 5%
where the time goes in v2:
time: 171 us; the launch traced here: 170 us
  waiting for transfers between devices  66.2 us (39%)
  blocking collectives  30.8 us (18%)
  starting transfers between devices  28.9 us (17%)
  Pallas kernels  25.6 us (15%)
  between operations  14.1 us (8%)
  local copies, waits for them, and re-layouts  4.6 us (3%)
    all_to_all x1, blocking collectives, on_device(): ngo = lax.all_to_all(ngo, TM, 0, 0, tiled=True)  30.8 us
    ppermute x6, waiting for transfers between devices, shift(): return lax.ppermute(array, 'x', [(i, (i + k) % NX) for i in range(NX)])  27.2 us
    all_to_all x1, waiting for transfers between devices, on_device(): qkv = lax.all_to_all(qkv, TM, 0, 0, tiled=True)  26.3 us
    pallas_call x1, Pallas kernels, attend(): call(attend_kernel, (jax.ShapeDtypeStruct((TOK, 4 * W), BF),) + (jax.Shap...  11 us
    all_to_all x1, starting transfers between devices, on_device(): lax.all_to_all(own_norm.reshape(NT, PT, 2 * W), TM, 0, 0, tiled=True)  9.27 us
    reduce_scatter x1, waiting for transfers between devices, on_device(): quarter = lax.psum_scatter(both, Y, scatter_dimension=0, tiled=True)  8.34 us
    ppermute x6, starting transfers between devices, shift(): return lax.ppermute(array, 'x', [(i, (i + k) % NX) for i in range(NX)])  7.75 us
    all_to_all x1, starting transfers between devices, on_device(): lax.all_to_all(quarter.reshape(8, 20, 4 * W), 'z', 0, 0, tiled=True)  5.78 us
  transfers between devices with their start and end apart: 12, of which 10 were waited for; matrix products, arithmetic and copies ran while one was open for 1% of the time, Pallas kernels for 5%

profile of v2, /device:TPU:1, one launch (start us, length us, event | category | flops | bytes accessed | tf_op | source)
XLA Modules:
  0.0 170.3 jit_solution(16700216697945124818)
XLA Ops:
  7.2 1.3 dynamic-slice_bitcast_fusion.feat_ref
  8.5 4.8 %shard_map.103 = (bf16[32,16,640]{2,1,0:T(8,128)(2,1)}, bf16[32,16,960]{2,1,0:T(8,128)(2,1)}) custom-call(s32[1,320]{1,0:T(1,128)} %dynamic-slice_bitcast_fusion.feat_ref, bf16[2,256,1280]{2,1,0:T(8,128)(2,1)} %bitcast.34, bf16[2,256,1280]{2,1,0:T(8,128)(2,1)} %bitcast.35, bf16[2,320,256]{2,1,0:T(8,128)(2,1)} %bitcast.38, bf16[2,320,256]{2,1,0:T(8,128)(2,1)} %bitcast.39, ...), custom_call_target="tpu_custom_call" | custom-call | flops 850000000 | bytes 4000000 | tf_op jit(solution)/shard_map/pallas_call | solution.py:218
  13.3 30.8 %all_to_all.20 = bf16[32,16,640]{2,1,0:T(8,128)(2,1)} all-to-all(bf16[32,16,640]{2,1,0:T(8,128)(2,1)} %get-tuple-element.11), channel_id=1, replica_groups=mesh['dp'=2,'z'=8,'yl'=2,'core'=2,'x'=4] {'z','yl','core'}, dimensions={0} | all-to-all | bytes 1310720 | tf_op jit(solution)/shard_map/all_to_all | solution.py:224
  44.1 5.1 %all-to-all-start = ((bf16[32,16,960]{2,1,0:T(8,128)(2,1)}), bf16[32,16,960]{2,1,0:T(8,128)(2,1)S(1)}, u32[]{:S(2)}, u32[]{:S(2)}) async-start(bf16[32,16,960]{2,1,0:T(8,128)(2,1)} %get-tuple-element.10), calls=%async_computation | async-start | bytes 2097152 | tf_op jit(solution)/shard_map/all_to_all | solution.py:226
  49.3 1.9 %shard_map.104.wout_ref = bf16[4,320,320]{2,1,0:T(8,128)(2,1)S(1)} custom-call(s32[4,1,320]{2,1,0:T(1,128)S(1)} %copy-done, bf16[320,1280]{1,0:T(8,128)(2,1)S(1)} %copy-done.2), custom_call_target="tpu_custom_call" | custom-call | flops 1000000000 | bytes 4000000 | tf_op jit(solution)/shard_map/pallas_call | solution.py:227
  51.2 26.3 %all-to-all-done.qkv_ref = bf16[32,16,960]{2,1,0:T(8,128)(2,1)S(1)} async-done(((bf16[32,16,960]{2,1,0:T(8,128)(2,1)}), bf16[32,16,960]{2,1,0:T(8,128)(2,1)S(1)}, u32[]{:S(2)}, u32[]{:S(2)}) %all-to-all-start) | async-done | bytes 983072 | tf_op jit(solution)/shard_map/all_to_all | solution.py:226
  77.4 1.8 %all-gather.3.cloned.1.call-done = bf16[128,16,640]{2,1,0:T(8,128)(2,1)} async-done(((bf16[32,16,640]{2,1,0:T(8,128)(2,1)}), bf16[128,16,640]{2,1,0:T(8,128)(2,1)}) %all-gather.3.cloned.1.call-update) | async-done | bytes 2621456 | tf_op jit(solution)/shard_map/all_gather | solution.py:225
  79.2 11.0 %shard_map.105 = (bf16[512,1280]{1,0:T(8,128)(2,1)S(1)}, bf16[256,640]{1,0:T(8,128)(2,1)S(1)}, bf16[256,640]{1,0:T(8,128)(2,1)S(1)}, bf16[256,640]{1,0:T(8,128)(2,1)S(1)}, bf16[256,640]{1,0:T(8,128)(2,1)S(1)}) custom-call(s32[1]{0:T(128)} %bitcast.x_ref, bf16[32,16,960]{2,1,0:T(8,128)(2,1)S(1)} %all-to-all-done.qkv_ref, bf16[4,32,16,640]{3,2,1,0:T(8,128)(2,1)} %bitcast.31, ...), custom_call_target="tpu_custom_call" | custom-call | flops 5000000000 | bytes 4000000 | tf_op jit(solution)/shard_map/pallas_call | solution.py:147
  90.3 1.7 shard_map.108
  92.0 0.9 collective-permute-start.6
  92.9 0.3 collective-permute-start
  93.2 2.2 %collective-permute-start.1 = (bf16[256,640]{1,0:T(8,128)(2,1)S(1)}, bf16[256,640]{1,0:T(8,128)(2,1)S(1)}, u32[]{:S(2)}, u32[]{:S(2)}) collective-permute-start(bf16[256,640]{1,0:T(8,128)(2,1)S(1)} %get-tuple-element.14), channel_id=1, source_target_pairs={{0,2},{1,3},{2,0},{3,1},{4,6},{5,7},{6,4},{7,5},{8,10},{9,11},{10,... | collective-permute-start | bytes 983048 | tf_op jit(solution)/shard_map/ppermute | solution.py:208
  95.5 1.1 collective-permute-start.2
  96.6 3.6 %shard_map.109 = bf16[640,1280]{1,0:T(8,128)(2,1)} custom-call(s32[1]{0:T(128)} %bitcast.16.half_ref, bf16[4,32,16,640]{3,2,1,0:T(8,128)(2,1)} %bitcast.32, bf16[512,1280]{1,0:T(8,128)(2,1)S(1)} %get-tuple-element.16.grads_ref, bf16[640,1280]{1,0:T(8,128)(2,1)S(1)} %collective-permute-done.6.refs_0_), custom_call_target="tpu_custom_call" | custom-call | flops 4000000000 | bytes 4000000 | tf_op jit(solution)/shard_map/pallas_call | solution.py:186
  100.3 3.2 %collective-permute-done.refs_1_ = bf16[256,640]{1,0:T(8,128)(2,1)S(1)} collective-permute-done((bf16[256,640]{1,0:T(8,128)(2,1)S(1)}, bf16[256,640]{1,0:T(8,128)(2,1)S(1)}, u32[]{:S(2)}, u32[]{:S(2)}) %collective-permute-start) | collective-permute-done | bytes 327712 | tf_op jit(solution)/shard_map/ppermute | solution.py:208
  103.5 6.9 %collective-permute-done.1.refs_2_ = bf16[256,640]{1,0:T(8,128)(2,1)S(1)} collective-permute-done((bf16[256,640]{1,0:T(8,128)(2,1)S(1)}, bf16[256,640]{1,0:T(8,128)(2,1)S(1)}, u32[]{:S(2)}, u32[]{:S(2)}) %collective-permute-start.1) | collective-permute-done | bytes 327712 | tf_op jit(solution)/shard_map/ppermute | solution.py:208
  110.3 0.4 collective-permute-done.2.refs_3_
  110.7 0.9 shard_map.106
  111.6 9.3 %all-to-all-start.2 = ((bf16[32,8,640]{2,1,0:T(8,128)(2,1)}), bf16[32,8,640]{2,1,0:T(8,128)(2,1)S(1)}, u32[]{:S(2)}, u32[]{:S(2)}) async-start(bf16[32,8,640]{2,1,0:T(8,128)(2,1)} %bitcast.13), calls=%async_computation.2 | async-start | bytes 655360 | tf_op jit(solution)/shard_map/all_to_all | solution.py:237
  120.9 8.3 %reduce-scatter.2.cloned.1.call-done = bf16[1,160,1280]{2,1,0:T(8,128)(2,1)} async-done(((bf16[4,160,1280]{2,1,0:T(8,128)(2,1)}), bf16[1,160,1280]{2,1,0:T(8,128)(2,1)}) %reduce-scatter.2.cloned.1.call-update) | async-done | bytes 409616 | tf_op jit(solution)/shard_map/reduce_scatter | solution.py:234
  129.2 1.9 %reshape.41 = bf16[8,20,1280]{2,1,0:T(8,128)(2,1)} reshape(bf16[1,160,1280]{2,1,0:T(8,128)(2,1)} %reduce-scatter.2.cloned.1.call-done) | data formatting | bytes 819200 | tf_op jit(solution)/shard_map/reshape | solution.py:243
  131.1 2.6 %all-to-all-done.2 = bf16[32,8,640]{2,1,0:T(8,128)(2,1)S(1)} async-done(((bf16[32,8,640]{2,1,0:T(8,128)(2,1)}), bf16[32,8,640]{2,1,0:T(8,128)(2,1)S(1)}, u32[]{:S(2)}, u32[]{:S(2)}) %all-to-all-start.2) | async-done | bytes 327712 | tf_op jit(solution)/shard_map/all_to_all | solution.py:237
  133.7 5.8 %all-to-all-start.3 = ((bf16[8,20,1280]{2,1,0:T(8,128)(2,1)}), bf16[8,20,1280]{2,1,0:T(8,128)(2,1)S(1)}, u32[]{:S(2)}, u32[]{:S(2)}) async-start(bf16[8,20,1280]{2,1,0:T(8,128)(2,1)} %reshape.41), calls=%async_computation.4 | async-start | bytes 983040 | tf_op jit(solution)/shard_map/all_to_all | solution.py:243
  139.4 2.6 %collective-permute-start.5 = (bf16[256,640]{1,0:T(8,128)(2,1)S(1)}, bf16[256,640]{1,0:T(8,128)(2,1)S(1)}, u32[]{:S(2)}, u32[]{:S(2)}) collective-permute-start(bf16[256,640]{1,0:T(8,128)(2,1)S(1)} %bitcast.27), channel_id=1, source_target_pairs={{0,3},{1,0},{2,1},{3,2},{4,7},{5,4},{6,5},{7,6},{8,11},{9,8},{10,9... | collective-permute-start | bytes 983048 | tf_op jit(solution)/shard_map/ppermute | solution.py:208
  142.0 0.8 collective-permute-start.4
  142.8 0.7 collective-permute-start.3
  143.5 5.2 %collective-permute-done.5.refs_3_ = bf16[256,640]{1,0:T(8,128)(2,1)S(1)} collective-permute-done((bf16[256,640]{1,0:T(8,128)(2,1)S(1)}, bf16[256,640]{1,0:T(8,128)(2,1)S(1)}, u32[]{:S(2)}, u32[]{:S(2)}) %collective-permute-start.5) | collective-permute-done | bytes 327712 | tf_op jit(solution)/shard_map/ppermute | solution.py:208
  148.6 2.6 %collective-permute-done.4.refs_2_ = bf16[256,640]{1,0:T(8,128)(2,1)S(1)} collective-permute-done((bf16[256,640]{1,0:T(8,128)(2,1)S(1)}, bf16[256,640]{1,0:T(8,128)(2,1)S(1)}, u32[]{:S(2)}, u32[]{:S(2)}) %collective-permute-start.4) | collective-permute-done | bytes 327712 | tf_op jit(solution)/shard_map/ppermute | solution.py:208
  151.2 9.0 %collective-permute-done.3.refs_1_ = bf16[256,640]{1,0:T(8,128)(2,1)S(1)} collective-permute-done((bf16[256,640]{1,0:T(8,128)(2,1)S(1)}, bf16[256,640]{1,0:T(8,128)(2,1)S(1)}, u32[]{:S(2)}, u32[]{:S(2)}) %collective-permute-start.3) | collective-permute-done | bytes 327712 | tf_op jit(solution)/shard_map/ppermute | solution.py:208
  160.2 1.7 %shard_map.107 = bf16[2,256,1280]{2,1,0:T(8,128)(2,1)} custom-call(s32[1]{0:T(128)} %bitcast.x_ref, bf16[256,640]{1,0:T(8,128)(2,1)S(1)} %bitcast.30, bf16[256,640]{1,0:T(8,128)(2,1)S(1)} %collective-permute-done.3.refs_1_, bf16[256,640]{1,0:T(8,128)(2,1)S(1)} %collective-permute-done.4.refs_2_, bf16[256,640]{1,0:T(8,128)(2,1)S(1)} %collective-permute-done.5.refs_3_), custom_call_target="tpu_custom_call" | custom-call | bytes 4000000 | tf_op jit(solution)/shard_map/pallas_call | solution.py:239
  162.0 0.7 slice_bitcast_fusion
  162.8 0.7 copy.13
  (15 shorter events, 0.3 us)
Async XLA Ops:
  7.2 72.1 %all-gather.3.cloned.1.call-start = ((), (), s32[]{:S(2)}) async-start(), calls=%async_computation.6 | async-start | bytes 3276800 | tf_op jit(solution)/shard_map/all_gather | solution.py:225
  44.1 5.2 %copy-start = (s32[4,1,320]{2,1,0:T(1,128)S(1)}, s32[4,1,320]{2,1,0:T(1,128)}, u32[]{:S(2)}) copy-start(s32[4,1,320]{2,1,0:T(1,128)} %constant.21.clone.feat_ref) | copy-start | bytes 15364
  44.1 5.2 %copy-start.2 = (bf16[320,1280]{1,0:T(8,128)(2,1)S(1)}, bf16[320,1280]{1,0:T(8,128)(2,1)}, u32[]{:S(2)}) copy-start(bf16[320,1280]{1,0:T(8,128)(2,1)} %w_ref.1) | copy-start | bytes 2457604
  44.1 33.3 %all-to-all-start = ((bf16[32,16,960]{2,1,0:T(8,128)(2,1)}), bf16[32,16,960]{2,1,0:T(8,128)(2,1)S(1)}, u32[]{:S(2)}, u32[]{:S(2)}) async-start(bf16[32,16,960]{2,1,0:T(8,128)(2,1)} %get-tuple-element.10), calls=%async_computation | async-start | bytes 2097152 | tf_op jit(solution)/shard_map/all_to_all | solution.py:226
  49.2 80.0 %reduce-scatter.2.cloned.1.call-start = ((), (), s32[]{:S(2)}) async-start(), calls=%async_computation.5 | async-start | bytes 2048000 | tf_op jit(solution)/shard_map/reduce_scatter | solution.py:234
  79.2 11.1 %copy-start.1 = (bf16[128,16,640]{2,1,0:T(8,128)(2,1)S(1)}, bf16[128,16,640]{2,1,0:T(8,128)(2,1)}, u32[]{:S(2)}) copy-start(bf16[128,16,640]{2,1,0:T(8,128)(2,1)} %all-gather.3.cloned.1.call-done) | copy-start | bytes 7864324
  92.0 4.7 %collective-permute-start.6 = (bf16[640,1280]{1,0:T(8,128)(2,1)S(1)}, bf16[640,1280]{1,0:T(8,128)(2,1)S(1)}, u32[]{:S(2)}, u32[]{:S(2)}) collective-permute-start(bf16[640,1280]{1,0:T(8,128)(2,1)S(1)} %shard_map.108), channel_id=1, source_target_pairs={{0,4},{4,0},{1,5},{5,1},{2,6},{6,2},{3,7},{7,3},{8,12},{12,8},{9,1... | collective-permute-start | bytes 4915208 | tf_op jit(solution)/shard_map/ppermute | solution.py:232
  92.9 10.6 %collective-permute-start = (bf16[256,640]{1,0:T(8,128)(2,1)S(1)}, bf16[256,640]{1,0:T(8,128)(2,1)S(1)}, u32[]{:S(2)}, u32[]{:S(2)}) collective-permute-start(bf16[256,640]{1,0:T(8,128)(2,1)S(1)} %get-tuple-element.13), channel_id=1, source_target_pairs={{0,1},{1,2},{2,3},{3,0},{4,5},{5,6},{6,7},{7,4},{8,9},{9,10},{10,1... | collective-permute-start | bytes 983048 | tf_op jit(solution)/shard_map/ppermute | solution.py:208
  93.2 17.1 %collective-permute-start.1 = (bf16[256,640]{1,0:T(8,128)(2,1)S(1)}, bf16[256,640]{1,0:T(8,128)(2,1)S(1)}, u32[]{:S(2)}, u32[]{:S(2)}) collective-permute-start(bf16[256,640]{1,0:T(8,128)(2,1)S(1)} %get-tuple-element.14), channel_id=1, source_target_pairs={{0,2},{1,3},{2,0},{3,1},{4,6},{5,7},{6,4},{7,5},{8,10},{9,11},{10,... | collective-permute-start | bytes 983048 | tf_op jit(solution)/shard_map/ppermute | solution.py:208
  95.5 15.2 %collective-permute-start.2 = (bf16[256,640]{1,0:T(8,128)(2,1)S(1)}, bf16[256,640]{1,0:T(8,128)(2,1)S(1)}, u32[]{:S(2)}, u32[]{:S(2)}) collective-permute-start(bf16[256,640]{1,0:T(8,128)(2,1)S(1)} %get-tuple-element.15), channel_id=1, source_target_pairs={{0,3},{1,0},{2,1},{3,2},{4,7},{5,4},{6,5},{7,6},{8,11},{9,8},{10,9... | collective-permute-start | bytes 983048 | tf_op jit(solution)/shard_map/ppermute | solution.py:208
  111.6 22.1 %all-to-all-start.2 = ((bf16[32,8,640]{2,1,0:T(8,128)(2,1)}), bf16[32,8,640]{2,1,0:T(8,128)(2,1)S(1)}, u32[]{:S(2)}, u32[]{:S(2)}) async-start(bf16[32,8,640]{2,1,0:T(8,128)(2,1)} %bitcast.13), calls=%async_computation.2 | async-start | bytes 655360 | tf_op jit(solution)/shard_map/all_to_all | solution.py:237
  133.7 28.3 %all-to-all-start.3 = ((bf16[8,20,1280]{2,1,0:T(8,128)(2,1)}), bf16[8,20,1280]{2,1,0:T(8,128)(2,1)S(1)}, u32[]{:S(2)}, u32[]{:S(2)}) async-start(bf16[8,20,1280]{2,1,0:T(8,128)(2,1)} %reshape.41), calls=%async_computation.4 | async-start | bytes 983040 | tf_op jit(solution)/shard_map/all_to_all | solution.py:243
  139.4 9.2 %collective-permute-start.5 = (bf16[256,640]{1,0:T(8,128)(2,1)S(1)}, bf16[256,640]{1,0:T(8,128)(2,1)S(1)}, u32[]{:S(2)}, u32[]{:S(2)}) collective-permute-start(bf16[256,640]{1,0:T(8,128)(2,1)S(1)} %bitcast.27), channel_id=1, source_target_pairs={{0,3},{1,0},{2,1},{3,2},{4,7},{5,4},{6,5},{7,6},{8,11},{9,8},{10,9... | collective-permute-start | bytes 983048 | tf_op jit(solution)/shard_map/ppermute | solution.py:208
  142.0 9.2 %collective-permute-start.4 = (bf16[256,640]{1,0:T(8,128)(2,1)S(1)}, bf16[256,640]{1,0:T(8,128)(2,1)S(1)}, u32[]{:S(2)}, u32[]{:S(2)}) collective-permute-start(bf16[256,640]{1,0:T(8,128)(2,1)S(1)} %bitcast.28), channel_id=1, source_target_pairs={{0,2},{1,3},{2,0},{3,1},{4,6},{5,7},{6,4},{7,5},{8,10},{9,11},{10,... | collective-permute-start | bytes 983048 | tf_op jit(solution)/shard_map/ppermute | solution.py:208
  142.8 17.4 %collective-permute-start.3 = (bf16[256,640]{1,0:T(8,128)(2,1)S(1)}, bf16[256,640]{1,0:T(8,128)(2,1)S(1)}, u32[]{:S(2)}, u32[]{:S(2)}) collective-permute-start(bf16[256,640]{1,0:T(8,128)(2,1)S(1)} %bitcast.29), channel_id=1, source_target_pairs={{0,1},{1,2},{2,3},{3,0},{4,5},{5,6},{6,7},{7,4},{8,9},{9,10},{10,1... | collective-permute-start | bytes 983048 | tf_op jit(solution)/shard_map/ppermute | solution.py:208
Sparse Core Ops, SparseCore 0:
  44.3 34.9 all-gather.2
  100.4 28.7 reduce-scatter.1

commit v3 on v2

--- a/solution.py
+++ b/solution.py
@@ -20,6 +20,7 @@
 TOK = 512
 FRAMES = 64
 LANES = 128
+GO = 384
 TILES = 4 * W // LANES
 BLOCK = 128
 TEMPER = HS ** (-0.5)
@@ -61,21 +62,48 @@
 
 def to_chunks(rows):
     width = rows.shape[-1]
-    low = rows[: TOK // 2].reshape(NT, PT, width)
-    high = rows[TOK // 2 :].reshape(NT, PT, width)
+    half = rows.shape[0] // 2
+    low = rows[:half].reshape(-1, PT, width)
+    high = rows[half:].reshape(-1, PT, width)
     return jnp.concatenate([low, high], axis=1).astype(BF)
 
 
-def one_hot(feat_ref):
+def one_hot(feat):
     places = lax.broadcasted_iota(jnp.int32, (D, W), 0)
-    return jnp.where(places == feat_ref[...], 1.0, 0.0).astype(BF)
-
-
-def prepare_kernel(feat_ref, n_ref, go_ref, q_ref, k_ref, v_ref, ngo_ref, qkv_ref):
-    pick = one_hot(feat_ref)
-    for at, ref in enumerate((n_ref, go_ref)):
-        rows = dot(ref[...].reshape(TOK, D), pick)
-        ngo_ref[:, :, at * W : (at + 1) * W] = to_chunks(rows)
+    return jnp.where(places == feat, 1.0, 0.0).astype(BF)
+
+
+def pick_kernel(x_ref, order_ref, go_ref, n_ref, out_ref, pick_s):
+    @pl.when(pl.program_id(0) == 0)
+    def _():
+        pick_s[...] = one_hot(order_ref[x_ref[0]])
+
+    for at, ref in enumerate((go_ref, n_ref)):
+        rows = dot(ref[...].reshape(-1, D), pick_s[...])
+        out_ref[:, :, at * W : (at + 1) * W] = to_chunks(rows)
+
+
+def pick(x, order, grad_output, normed):
+    steps = 4
+    block = pl.BlockSpec((FR, NT * PT // steps, D), lambda i: (0, i, 0))
+    return call(
+        pick_kernel,
+        jax.ShapeDtypeStruct((NT, 2 * PT, 2 * W), BF),
+        850_000_000,
+        limit=60 * 1024 * 1024,
+        grid=(steps,),
+        in_specs=[
+            pl.BlockSpec(memory_space=pltpu.SMEM),
+            pl.BlockSpec((NX, 1, W), lambda i: (0, 0, 0)),
+            block,
+            block,
+        ],
+        out_specs=pl.BlockSpec((NT // steps, 2 * PT, 2 * W), lambda i: (i, 0, 0)),
+        scratch_shapes=[pltpu.VMEM((D, W), BF)],
+    )(x, order, grad_output, normed)
+
+
+def pack_kernel(q_ref, k_ref, v_ref, qkv_ref):
     for at, ref in enumerate((q_ref, k_ref, v_ref)):
         rows = jnp.concatenate([ref[f].astype(F32).T for f in range(FR)], axis=0)
         qkv_ref[:, :, at * W : (at + 1) * W] = to_chunks(rows)
@@ -83,19 +111,26 @@
 
 def reorder_kernel(feat_ref, w_ref, out_ref):
     for at in range(NX):
-        out_ref[at] = dot(w_ref[...], one_hot(feat_ref.at[at])).astype(BF)
-
-
-def attend_kernel(x_ref, qkv_ref, ngo_ref, wout_ref, wqkv_ref, grads_ref, *rest):
-    norm_refs, (wide_s, rows_s, all_t, g_t, norm_s) = rest[:NX], rest[NX:]
-    acc = jnp.zeros((TOK, W), F32)
-    for at in range(NX):
-        acc = acc + dot_nt(ngo_ref[at].reshape(TOK, 2 * W)[:, W:], wout_ref[at])
-    ga = acc.astype(BF).astype(F32)
+        out_ref[at] = dot(w_ref[...], one_hot(feat_ref[at])).astype(BF)
+
+
+def attend_kernel(x_ref, qkv_ref, gon_ref, wout_ref, wqkv_hbm, grads_ref, *rest):
+    norm_refs, (wide_s, rows_s, all_t, g_t, norm_s, go_s, wqkv_s, sems) = rest[:NX], rest[NX:]
+    copies = [
+        pltpu.make_async_copy(gon_ref.at[at, :, :, pl.ds(0, GO)], go_s.at[at], sems.at[at]) for at in range(NX)
+    ]
+    copies.append(pltpu.make_async_copy(wqkv_hbm, wqkv_s, sems.at[NX]))
+    for copy in copies:
+        copy.start()
     half = LANES // 2
     for t in range(7):
         wide_s[t] = qkv_ref[:, :, t * LANES : (t + 1) * LANES].reshape(TOK, LANES).astype(F32)
     wide_s[7, :, :half] = qkv_ref[:, :, 7 * LANES :].reshape(TOK, half).astype(F32)
+    acc = jnp.zeros((TOK, W), F32)
+    for at in range(NX):
+        copies[at].wait()
+        acc = acc + dot_nt(go_s[at].reshape(TOK, GO)[:, :W], wout_ref[at])
+    ga = acc.astype(BF).astype(F32)
     wide_s[7, :, half:] = ga[:, :half]
     for t in (8, 9):
         wide_s[t] = ga[:, (t - 8) * LANES + half : (t - 7) * LANES + half]
@@ -131,7 +166,8 @@
             wide_s[t, pl.ds(p, FRAMES, stride=PT), :] = tile[p * FRAMES : (p + 1) * FRAMES]
     for t in range(TILES):
         grads_ref[:, t * LANES : (t + 1) * LANES] = wide_s[t].astype(BF)
-    norm = dot(grads_ref[:, : 3 * W], wqkv_ref[...])
+    copies[NX].wait()
+    norm = dot(grads_ref[:, : 3 * W], wqkv_s[...])
     for at in range(NX):
         part = norm[:, at * W : (at + 1) * W].reshape(NT, 2 * PT, W)
         slot = lax.rem(at + NX - x_ref[0], NX)
@@ -141,36 +177,40 @@
         norm_refs[at][...] = norm_s[at]
 
 
-def attend(x, qkv, ngo, w_ordered, w_qkv):
+def attend(x, qkv, gon, w_ordered, w_qkv):
     scalar = pl.BlockSpec(memory_space=pltpu.SMEM)
     whole = pl.BlockSpec(memory_space=pltpu.VMEM)
+    hbm = pl.BlockSpec(memory_space=pl.ANY)
     return call(
         attend_kernel,
         (jax.ShapeDtypeStruct((TOK, 4 * W), BF),) + (jax.ShapeDtypeStruct((TOK // 2, 2 * W), BF),) * NX,
         5_000_000_000,
-        in_specs=[scalar] + [whole] * 4,
+        in_specs=[scalar, whole, hbm, whole, hbm],
         scratch_shapes=[
             pltpu.VMEM((TILES, TOK, LANES), F32),
             pltpu.VMEM((TOK, 4 * W), BF),
             pltpu.VMEM((4 * W, TOK), BF),
             pltpu.VMEM((4 * W, TOK), F32),
             pltpu.VMEM((NX, TOK // 2, 2 * W), BF),
+            pltpu.VMEM((NX, NT, 2 * PT, GO), BF),
+            pltpu.VMEM((3 * W, D), BF),
+            pltpu.SemaphoreType.DMA((NX + 1,)),
         ],
-    )(x, qkv, ngo, w_ordered, w_qkv)
-
-
-def weight_kernel(half_ref, ngo_ref, grads_ref, *refs):
+    )(x, qkv, gon, w_ordered, w_qkv)
+
+
+def weight_kernel(half_ref, gon_ref, grads_ref, *refs):
     del half_ref
     out_ref = refs[-1]
-    ngo_t = ngo_ref[0].reshape(TOK, 2 * W).astype(F32).T.astype(BF)
-    for rows, cols in ((slice(0, W), slice(0, 3 * W)), (slice(W, 2 * W), slice(3 * W, 4 * W))):
-        total = dot(ngo_t[rows], grads_ref[:, cols])
+    gon_t = gon_ref[0].reshape(TOK, 2 * W).astype(F32).T.astype(BF)
+    for rows, cols in ((slice(W, 2 * W), slice(0, 3 * W)), (slice(0, W), slice(3 * W, 4 * W))):
+        total = dot(gon_t[rows], grads_ref[:, cols])
         if len(refs) == 2:
             total = total + refs[0][:, cols].astype(F32)
         out_ref[:, cols] = total.astype(BF)
 
 
-def weight_half(half, ngo, grads, *got):
+def weight_half(half, gon, grads, *got):
     block = pl.BlockSpec((W, 4 * W), lambda j, half: (j, 0))
     spec = pltpu.PrefetchScalarGridSpec(
         num_scalar_prefetch=1,
@@ -183,7 +223,7 @@
         out_specs=block,
     )
     shape = jax.ShapeDtypeStruct((2 * W, 4 * W), BF)
-    return call(weight_kernel, shape, 4_000_000_000, spec)(half, ngo, grads, *got)
+    return call(weight_kernel, shape, 4_000_000_000, spec)(half, gon, grads, *got)
 
 
 def add_kernel(*refs):
@@ -202,6 +242,15 @@
             def _(at=at, k=k):
                 for f in range(FR):
                     out_ref[f, :, at * W : (at + 1) * W] = refs[k][:, f * W : (f + 1) * W]
+
+
+def total_kernel(in_ref, qkv_ref, out_ref):
+    total = in_ref[0].astype(F32)
+    for at in range(1, 8):
+        total = total + in_ref[at].astype(F32)
+    for i in range(3):
+        qkv_ref[i] = total[:, i * W : (i + 1) * W]
+    out_ref[...] = total[:, 3 * W :]
 
 
 def shift(array, k):
@@ -214,37 +263,37 @@
     core = lax.axis_index("core")
     scalar = pl.BlockSpec(memory_space=pltpu.SMEM)
     whole = pl.BlockSpec(memory_space=pltpu.VMEM)
-    mine = lax.dynamic_index_in_dim(order, x, 0, keepdims=False)
-    ngo, qkv = call(
-        prepare_kernel,
-        (jax.ShapeDtypeStruct((NT, 2 * PT, 2 * W), BF), jax.ShapeDtypeStruct((NT, 2 * PT, 3 * W), BF)),
-        850_000_000,
-        limit=60 * 1024 * 1024,
-    )(mine, normed[0], grad_output[0], *[jnp.swapaxes(item[0], 1, 2) for item in (queries, key_vectors, value_vectors)])
-    ngo = lax.all_to_all(ngo, TM, 0, 0, tiled=True)
-    ngo = lax.all_gather(ngo, "x", axis=0)
+    gon = pick(x.reshape(1), order, grad_output[0], normed[0])
+    gon = lax.all_to_all(gon, TM, 0, 0, tiled=True)
+    gon = lax.all_gather(gon, "x", axis=0)
+    qkv = call(pack_kernel, jax.ShapeDtypeStruct((NT, 2 * PT, 3 * W), BF), 30_000_000_000)(
+        *[jnp.swapaxes(item[0], 1, 2) for item in (queries, key_vectors, value_vectors)]
+    )
     qkv = lax.all_to_all(qkv, TM, 0, 0, tiled=True)
     w_ordered = call(reorder_kernel, jax.ShapeDtypeStruct((NX, W, W), BF), 1_000_000_000)(order, w_out)
-    grads, *parts = attend(x.reshape(1), qkv, ngo, w_ordered, jnp.swapaxes(w_qkv, 1, 2).reshape(3 * W, D))
+    grads, *parts = attend(x.reshape(1), qkv, gon, w_ordered, jnp.swapaxes(w_qkv, 1, 2).reshape(3 * W, D))
 
     moved = [parts[0]] + [shift(parts[k], k) for k in range(1, NX)]
-    sent = weight_half((1 - core).reshape(1), ngo, grads)
+    sent = weight_half((1 - core).reshape(1), gon, grads)
     got = lax.ppermute(sent, "core", [(0, 1), (1, 0)])
-    both = weight_half(core.reshape(1), ngo, grads, got).reshape(4, D // 8, 4 * W)
+    both = weight_half(core.reshape(1), gon, grads, got).reshape(4, D // 8, 4 * W)
     quarter = lax.psum_scatter(both, Y, scatter_dimension=0, tiled=True)
 
     own_norm = call(add_kernel, jax.ShapeDtypeStruct((TOK // 2, 2 * W), BF), 40_000_000_000)(*moved)
     own_norm = lax.all_to_all(own_norm.reshape(NT, PT, 2 * W), TM, 0, 0, tiled=True).reshape(TOK // 2, 2 * W)
     all_norm = [own_norm] + [shift(own_norm, k) for k in range(1, NX)]
     grad_normed = call(
-        spread_kernel, jax.ShapeDtypeStruct((FR, TOK // 2, D), BF), in_specs=[scalar] + [whole] * NX
+        spread_kernel,
+        jax.ShapeDtypeStruct((FR, TOK // 2, D), BF),
+        40_000_000_000,
+        in_specs=[scalar] + [whole] * NX,
     )(x.reshape(1), *all_norm)
 
     pieces = lax.all_to_all(quarter.reshape(8, 20, 4 * W), "z", 0, 0, tiled=True)
-    total = jnp.sum(pieces.astype(F32), axis=0)
-    grad_qkv = total[:, : 3 * W].reshape(20, 3, W).transpose(1, 0, 2)
-    grad_out = total[:, 3 * W :].T
-    return (grad_normed[None], grad_qkv, grad_out)
+    grad_qkv, grad_out = call(
+        total_kernel, (jax.ShapeDtypeStruct((3, 20, W), F32), jax.ShapeDtypeStruct((20, W), F32))
+    )(pieces)
+    return (grad_normed[None], grad_qkv, grad_out.T)
 
 
 def solution(mesh):

time: 171 us -> 164 us (0.959)
  blocking collectives: 30.8 us -> 51.7 us
  waiting for transfers between devices: 66.2 us -> 49.9 us
  starting transfers between devices: 28.9 us -> 17.8 us
  local copies, waits for them, and re-layouts: 4.6 us -> 1.89 us
    all_to_all x1 -> x2, blocking collectives: 30.8 us -> 51.7 us  [the longest x1 31 us: on_device(): gon = lax.all_to_all(gon, TM, 0, 0, tiled=True)]
    all_to_all x1 -> x0, starting transfers between devices: 9.27 us -> none  [on_device(): lax.all_to_all(own_norm.reshape(NT, PT, 2 * W), TM, 0, 0, tiled=True)]
    reduce_scatter x1, waiting for transfers between devices: 8.34 us -> 0.01 us  [on_device(): quarter = lax.psum_scatter(both, Y, scatter_dimension=0, tiled=True)]
    ppermute x6, waiting for transfers between devices: 27.2 us -> 22.2 us  [shift(): return lax.ppermute(array, 'x', [(i, (i + k) % NX) for i in range(NX)])]
    all_to_all x1 -> x0, waiting for transfers between devices: 2.57 us -> none  [on_device(): lax.all_to_all(own_norm.reshape(NT, PT, 2 * W), TM, 0, 0, tiled=True)]
    pallas_call x4 -> x6, Pallas kernels: 11.8 us -> 14.3 us  [the longest x2 5.31 us: weight_half(): return call(weight_kernel, shape, 4000000000, spec)(half, gon, grads, *got)]
    all_to_all x1, starting transfers between devices: 5.78 us -> 3.48 us  [on_device(): lax.all_to_all(quarter.reshape(8, 20, 4 * W), 'z', 0, 0, tiled=True)]
  transfers between devices with their start and end apart: 12 -> 11, of which waited for: 10 -> 8; matrix products, arithmetic and copies ran while one was open for 1% -> 1% of each run, Pallas kernels for 5% -> 6%
where the time goes in v3:
time: 164 us; the launch traced here: 162 us
  blocking collectives  51.7 us (32%)
  waiting for transfers between devices  49.9 us (30%)
  Pallas kernels  26.3 us (16%)
  starting transfers between devices  17.8 us (11%)
  between operations  14.2 us (9%)
  local copies, waits for them, and re-layouts  1.89 us (1%)
    all_to_all x1, blocking collectives, on_device(): gon = lax.all_to_all(gon, TM, 0, 0, tiled=True)  31 us
    all_to_all x1, waiting for transfers between devices, on_device(): qkv = lax.all_to_all(qkv, TM, 0, 0, tiled=True)  26.3 us
    ppermute x6, waiting for transfers between devices, shift(): return lax.ppermute(array, 'x', [(i, (i + k) % NX) for i in range(NX)])  22.2 us
    all_to_all x1, blocking collectives, on_device(): lax.all_to_all(own_norm.reshape(NT, PT, 2 * W), TM, 0, 0, tiled=True)  20.7 us
    pallas_call x1, Pallas kernels, attend(): call(attend_kernel, (jax.ShapeDtypeStruct((TOK, 4 * W), BF),) + (jax.Shap...  10 us
    ppermute x6, starting transfers between devices, shift(): return lax.ppermute(array, 'x', [(i, (i + k) % NX) for i in range(NX)])  7.76 us
    pallas_call x2, Pallas kernels, weight_half(): return call(weight_kernel, shape, 4000000000, spec)(half, gon, grads, *got)  5.31 us
    all_to_all x1, starting transfers between devices, on_device(): qkv = lax.all_to_all(qkv, TM, 0, 0, tiled=True)  5.06 us
  transfers between devices with their start and end apart: 11, of which 8 were waited for; matrix products, arithmetic and copies ran while one was open for 1% of the time, Pallas kernels for 6%

profile of v3, /device:TPU:1, one launch (start us, length us, event | category | flops | bytes accessed | tf_op | source)
XLA Modules:
  0.0 161.8 jit_solution(14161849426452011677)
XLA Ops:
  7.2 0.0 all-gather.3.cloned.1.call-start
  7.2 4.9 %shard_map.104 = bf16[32,16,640]{2,1,0:T(8,128)(2,1)} custom-call(s32[1]{0:T(128)} %bitcast.x_ref, s32[4,1,320]{2,1,0:T(1,128)} %constant.13.clone.order_ref.feat_ref, bf16[2,256,1280]{2,1,0:T(8,128)(2,1)} %bitcast.34, bf16[2,256,1280]{2,1,0:T(8,128)(2,1)} %bitcast.35), custom_call_target="tpu_custom_call" | custom-call | flops 850000000 | bytes 4000000 | tf_op jit(solution)/shard_map/pallas_call | solution.py:89
  12.1 31.0 %all_to_all.20 = bf16[32,16,640]{2,1,0:T(8,128)(2,1)} all-to-all(bf16[32,16,640]{2,1,0:T(8,128)(2,1)} %shard_map.104), channel_id=1, replica_groups=mesh['dp'=2,'z'=8,'yl'=2,'core'=2,'x'=4] {'z','yl','core'}, dimensions={0} | all-to-all | bytes 1310720 | tf_op jit(solution)/shard_map/all_to_all | solution.py:267
  43.1 0.0 all-gather.3.cloned.1.call-update
  43.2 1.5 shard_map.103
  44.7 5.1 %all-to-all-start = ((bf16[32,16,960]{2,1,0:T(8,128)(2,1)}), bf16[32,16,960]{2,1,0:T(8,128)(2,1)S(1)}, u32[]{:S(2)}, u32[]{:S(2)}) async-start(bf16[32,16,960]{2,1,0:T(8,128)(2,1)} %shard_map.103), calls=%async_computation | async-start | bytes 2097152 | tf_op jit(solution)/shard_map/all_to_all | solution.py:272
  49.8 0.0 reduce-scatter.2.cloned.1.call-start
  49.9 1.9 %shard_map.105.wout_ref = bf16[4,320,320]{2,1,0:T(8,128)(2,1)S(1)} custom-call(s32[4,1,320]{2,1,0:T(1,128)S(1)} %copy-done, bf16[320,1280]{1,0:T(8,128)(2,1)S(1)} %copy-done.2), custom_call_target="tpu_custom_call" | custom-call | flops 1000000000 | bytes 4000000 | tf_op jit(solution)/shard_map/pallas_call | solution.py:273
  51.8 26.3 %all-to-all-done.qkv_ref = bf16[32,16,960]{2,1,0:T(8,128)(2,1)S(1)} async-done(((bf16[32,16,960]{2,1,0:T(8,128)(2,1)}), bf16[32,16,960]{2,1,0:T(8,128)(2,1)S(1)}, u32[]{:S(2)}, u32[]{:S(2)}) %all-to-all-start) | async-done | bytes 983072 | tf_op jit(solution)/shard_map/all_to_all | solution.py:272
  78.0 0.3 all-gather.3.cloned.1.call-done
  78.3 10.0 %shard_map.106 = (bf16[512,1280]{1,0:T(8,128)(2,1)S(1)}, bf16[256,640]{1,0:T(8,128)(2,1)S(1)}, bf16[256,640]{1,0:T(8,128)(2,1)S(1)}, bf16[256,640]{1,0:T(8,128)(2,1)S(1)}, bf16[256,640]{1,0:T(8,128)(2,1)S(1)}) custom-call(s32[1]{0:T(128)} %bitcast.x_ref, bf16[32,16,960]{2,1,0:T(8,128)(2,1)S(1)} %all-to-all-done.qkv_ref, bf16[4,32,16,640]{3,2,1,0:T(8,128)(2,1)} %bitcast.28, ...), custom_call_target="tpu_custom_call" | custom-call | flops 5000000000 | bytes 4000000 | tf_op jit(solution)/shard_map/pallas_call | solution.py:184
  88.3 1.7 %shard_map.109 = bf16[640,1280]{1,0:T(8,128)(2,1)S(1)} custom-call(s32[1]{0:T(128)} %bitcast.16.half_ref, bf16[4,32,16,640]{3,2,1,0:T(8,128)(2,1)S(1)} %bitcast.30, bf16[512,1280]{1,0:T(8,128)(2,1)S(1)} %get-tuple-element.14.grads_ref), custom_call_target="tpu_custom_call" | custom-call | flops 4000000000 | bytes 4000000 | tf_op jit(solution)/shard_map/pallas_call | solution.py:226
  90.0 1.4 collective-permute-start.6
  91.4 1.2 collective-permute-start
  92.6 2.5 %collective-permute-start.1 = (bf16[256,640]{1,0:T(8,128)(2,1)S(1)}, bf16[256,640]{1,0:T(8,128)(2,1)S(1)}, u32[]{:S(2)}, u32[]{:S(2)}) collective-permute-start(bf16[256,640]{1,0:T(8,128)(2,1)S(1)} %get-tuple-element.12), channel_id=1, source_target_pairs={{0,2},{1,3},{2,0},{3,1},{4,6},{5,7},{6,4},{7,5},{8,10},{9,11},{10,... | collective-permute-start | bytes 983048 | tf_op jit(solution)/shard_map/ppermute | solution.py:257
  95.1 1.1 collective-permute-start.2
  96.2 3.6 %shard_map.110 = bf16[640,1280]{1,0:T(8,128)(2,1)} custom-call(s32[1]{0:T(128)} %bitcast.15.half_ref, bf16[4,32,16,640]{3,2,1,0:T(8,128)(2,1)} %bitcast.29, bf16[512,1280]{1,0:T(8,128)(2,1)S(1)} %get-tuple-element.14.grads_ref, bf16[640,1280]{1,0:T(8,128)(2,1)S(1)} %collective-permute-done.6.refs_0_), custom_call_target="tpu_custom_call" | custom-call | flops 4000000000 | bytes 4000000 | tf_op jit(solution)/shard_map/pallas_call | solution.py:226
  99.9 2.0 %collective-permute-done.refs_1_ = bf16[256,640]{1,0:T(8,128)(2,1)S(1)} collective-permute-done((bf16[256,640]{1,0:T(8,128)(2,1)S(1)}, bf16[256,640]{1,0:T(8,128)(2,1)S(1)}, u32[]{:S(2)}, u32[]{:S(2)}) %collective-permute-start) | collective-permute-done | bytes 327712 | tf_op jit(solution)/shard_map/ppermute | solution.py:257
  101.9 8.0 %collective-permute-done.1.refs_2_ = bf16[256,640]{1,0:T(8,128)(2,1)S(1)} collective-permute-done((bf16[256,640]{1,0:T(8,128)(2,1)S(1)}, bf16[256,640]{1,0:T(8,128)(2,1)S(1)}, u32[]{:S(2)}, u32[]{:S(2)}) %collective-permute-start.1) | collective-permute-done | bytes 327712 | tf_op jit(solution)/shard_map/ppermute | solution.py:257
  109.9 0.2 shard_map.107
  110.1 20.7 %all_to_all.21 = bf16[32,8,640]{2,1,0:T(8,128)(2,1)S(1)} all-to-all(bf16[32,8,640]{2,1,0:T(8,128)(2,1)S(1)} %bitcast.27), channel_id=1, replica_groups=mesh['dp'=2,'z'=8,'yl'=2,'core'=2,'x'=4] {'z','yl','core'}, dimensions={0} | all-to-all | bytes 655360 | tf_op jit(solution)/shard_map/all_to_all | solution.py:283
  130.8 2.4 %collective-permute-start.5 = (bf16[256,640]{1,0:T(8,128)(2,1)S(1)}, bf16[256,640]{1,0:T(8,128)(2,1)S(1)}, u32[]{:S(2)}, u32[]{:S(2)}) collective-permute-start(bf16[256,640]{1,0:T(8,128)(2,1)S(1)} %bitcast.23), channel_id=1, source_target_pairs={{0,3},{1,0},{2,1},{3,2},{4,7},{5,4},{6,5},{7,6},{8,11},{9,8},{10,9... | collective-permute-start | bytes 983048 | tf_op jit(solution)/shard_map/ppermute | solution.py:257
  133.1 0.4 collective-permute-start.4
  133.5 0.2 collective-permute-start.3
  133.7 1.9 %reshape.39 = bf16[8,20,1280]{2,1,0:T(8,128)(2,1)} reshape(bf16[1,160,1280]{2,1,0:T(8,128)(2,1)} %reduce-scatter.2.cloned.1.call-done) | data formatting | bytes 819200 | tf_op jit(solution)/shard_map/reshape | solution.py:292
  135.6 3.5 %all-to-all-start.3 = ((bf16[8,20,1280]{2,1,0:T(8,128)(2,1)}), bf16[8,20,1280]{2,1,0:T(8,128)(2,1)S(1)}, u32[]{:S(2)}, u32[]{:S(2)}) async-start(bf16[8,20,1280]{2,1,0:T(8,128)(2,1)} %reshape.39), calls=%async_computation.4 | async-start | bytes 983040 | tf_op jit(solution)/shard_map/all_to_all | solution.py:292
  139.1 0.5 collective-permute-done.5.refs_3_
  139.5 2.8 %collective-permute-done.4.refs_2_ = bf16[256,640]{1,0:T(8,128)(2,1)S(1)} collective-permute-done((bf16[256,640]{1,0:T(8,128)(2,1)S(1)}, bf16[256,640]{1,0:T(8,128)(2,1)S(1)}, u32[]{:S(2)}, u32[]{:S(2)}) %collective-permute-start.4) | collective-permute-done | bytes 327712 | tf_op jit(solution)/shard_map/ppermute | solution.py:257
  142.4 8.9 %collective-permute-done.3.refs_1_ = bf16[256,640]{1,0:T(8,128)(2,1)S(1)} collective-permute-done((bf16[256,640]{1,0:T(8,128)(2,1)S(1)}, bf16[256,640]{1,0:T(8,128)(2,1)S(1)}, u32[]{:S(2)}, u32[]{:S(2)}) %collective-permute-start.3) | collective-permute-done | bytes 327712 | tf_op jit(solution)/shard_map/ppermute | solution.py:257
  151.3 1.7 %shard_map.108 = bf16[2,256,1280]{2,1,0:T(8,128)(2,1)} custom-call(s32[1]{0:T(128)} %bitcast.x_ref, bf16[256,640]{1,0:T(8,128)(2,1)S(1)} %bitcast.26, bf16[256,640]{1,0:T(8,128)(2,1)S(1)} %collective-permute-done.3.refs_1_, bf16[256,640]{1,0:T(8,128)(2,1)S(1)} %collective-permute-done.4.refs_2_, bf16[256,640]{1,0:T(8,128)(2,1)S(1)} %collective-permute-done.5.refs_3_), custom_call_target="tpu_custom_call" | custom-call | flops 40000000000 | bytes 4000000 | tf_op jit(solution)/shard_map/pallas_call | solution.py:285
  153.0 1.2 all-to-all-done.3.in_ref
  154.2 0.8 shard_map.111
  (16 shorter events, 0.0 us)
Async XLA Ops:
  7.2 71.1 %all-gather.3.cloned.1.call-start = ((), (), s32[]{:S(2)}) async-start(), calls=%async_computation.6 | async-start | bytes 3276800 | tf_op jit(solution)/shard_map/all_gather | solution.py:268
  12.1 31.0 %copy-start.3 = (bf16[1,2,256,320]{2,3,1,0:T(8,128)(2,1)S(1)}, bf16[1,2,256,320]{2,3,1,0:T(8,128)(2,1)}, u32[]{:S(2)}) copy-start(bf16[1,2,256,320]{2,3,1,0:T(8,128)(2,1)} %param.8) | copy-start | bytes 983044
  12.1 31.0 %copy-start.4 = (bf16[1,2,256,320]{2,3,1,0:T(8,128)(2,1)S(1)}, bf16[1,2,256,320]{2,3,1,0:T(8,128)(2,1)}, u32[]{:S(2)}) copy-start(bf16[1,2,256,320]{2,3,1,0:T(8,128)(2,1)} %param.9) | copy-start | bytes 983044
  12.1 31.1 %copy-start.5 = (bf16[1,2,256,320]{2,3,1,0:T(8,128)(2,1)S(1)}, bf16[1,2,256,320]{2,3,1,0:T(8,128)(2,1)}, u32[]{:S(2)}) copy-start(bf16[1,2,256,320]{2,3,1,0:T(8,128)(2,1)} %param.10) | copy-start | bytes 983044
  44.7 5.1 %copy-start = (s32[4,1,320]{2,1,0:T(1,128)S(1)}, s32[4,1,320]{2,1,0:T(1,128)}, u32[]{:S(2)}) copy-start(s32[4,1,320]{2,1,0:T(1,128)} %constant.13.clone.order_ref.feat_ref) | copy-start | bytes 15364
  44.7 5.1 %copy-start.2 = (bf16[320,1280]{1,0:T(8,128)(2,1)S(1)}, bf16[320,1280]{1,0:T(8,128)(2,1)}, u32[]{:S(2)}) copy-start(bf16[320,1280]{1,0:T(8,128)(2,1)} %w_ref.1) | copy-start | bytes 2457604
  44.7 33.3 %all-to-all-start = ((bf16[32,16,960]{2,1,0:T(8,128)(2,1)}), bf16[32,16,960]{2,1,0:T(8,128)(2,1)S(1)}, u32[]{:S(2)}, u32[]{:S(2)}) async-start(bf16[32,16,960]{2,1,0:T(8,128)(2,1)} %shard_map.103), calls=%async_computation | async-start | bytes 2097152 | tf_op jit(solution)/shard_map/all_to_all | solution.py:272
  49.8 83.9 %reduce-scatter.2.cloned.1.call-start = ((), (), s32[]{:S(2)}) async-start(), calls=%async_computation.5 | async-start | bytes 2048000 | tf_op jit(solution)/shard_map/reduce_scatter | solution.py:280
  78.3 10.0 %copy-start.1 = (bf16[128,16,640]{2,1,0:T(8,128)(2,1)S(1)}, bf16[128,16,640]{2,1,0:T(8,128)(2,1)}, u32[]{:S(2)}) copy-start(bf16[128,16,640]{2,1,0:T(8,128)(2,1)} %all-gather.3.cloned.1.call-done) | copy-start | bytes 7864324
  90.0 6.2 %collective-permute-start.6 = (bf16[640,1280]{1,0:T(8,128)(2,1)S(1)}, bf16[640,1280]{1,0:T(8,128)(2,1)S(1)}, u32[]{:S(2)}, u32[]{:S(2)}) collective-permute-start(bf16[640,1280]{1,0:T(8,128)(2,1)S(1)} %shard_map.109), channel_id=1, source_target_pairs={{0,4},{4,0},{1,5},{5,1},{2,6},{6,2},{3,7},{7,3},{8,12},{12,8},{9,1... | collective-permute-start | bytes 4915208 | tf_op jit(solution)/shard_map/ppermute | solution.py:278
  91.4 10.5 %collective-permute-start = (bf16[256,640]{1,0:T(8,128)(2,1)S(1)}, bf16[256,640]{1,0:T(8,128)(2,1)S(1)}, u32[]{:S(2)}, u32[]{:S(2)}) collective-permute-start(bf16[256,640]{1,0:T(8,128)(2,1)S(1)} %get-tuple-element.11), channel_id=1, source_target_pairs={{0,1},{1,2},{2,3},{3,0},{4,5},{5,6},{6,7},{7,4},{8,9},{9,10},{10,1... | collective-permute-start | bytes 983048 | tf_op jit(solution)/shard_map/ppermute | solution.py:257
  92.6 17.3 %collective-permute-start.1 = (bf16[256,640]{1,0:T(8,128)(2,1)S(1)}, bf16[256,640]{1,0:T(8,128)(2,1)S(1)}, u32[]{:S(2)}, u32[]{:S(2)}) collective-permute-start(bf16[256,640]{1,0:T(8,128)(2,1)S(1)} %get-tuple-element.12), channel_id=1, source_target_pairs={{0,2},{1,3},{2,0},{3,1},{4,6},{5,7},{6,4},{7,5},{8,10},{9,11},{10,... | collective-permute-start | bytes 983048 | tf_op jit(solution)/shard_map/ppermute | solution.py:257
  95.1 14.8 %collective-permute-start.2 = (bf16[256,640]{1,0:T(8,128)(2,1)S(1)}, bf16[256,640]{1,0:T(8,128)(2,1)S(1)}, u32[]{:S(2)}, u32[]{:S(2)}) collective-permute-start(bf16[256,640]{1,0:T(8,128)(2,1)S(1)} %get-tuple-element.13), channel_id=1, source_target_pairs={{0,3},{1,0},{2,1},{3,2},{4,7},{5,4},{6,5},{7,6},{8,11},{9,8},{10,9... | collective-permute-start | bytes 983048 | tf_op jit(solution)/shard_map/ppermute | solution.py:257
  130.8 8.7 %collective-permute-start.5 = (bf16[256,640]{1,0:T(8,128)(2,1)S(1)}, bf16[256,640]{1,0:T(8,128)(2,1)S(1)}, u32[]{:S(2)}, u32[]{:S(2)}) collective-permute-start(bf16[256,640]{1,0:T(8,128)(2,1)S(1)} %bitcast.23), channel_id=1, source_target_pairs={{0,3},{1,0},{2,1},{3,2},{4,7},{5,4},{6,5},{7,6},{8,11},{9,8},{10,9... | collective-permute-start | bytes 983048 | tf_op jit(solution)/shard_map/ppermute | solution.py:257
  133.1 9.2 %collective-permute-start.4 = (bf16[256,640]{1,0:T(8,128)(2,1)S(1)}, bf16[256,640]{1,0:T(8,128)(2,1)S(1)}, u32[]{:S(2)}, u32[]{:S(2)}) collective-permute-start(bf16[256,640]{1,0:T(8,128)(2,1)S(1)} %bitcast.24), channel_id=1, source_target_pairs={{0,2},{1,3},{2,0},{3,1},{4,6},{5,7},{6,4},{7,5},{8,10},{9,11},{10,... | collective-permute-start | bytes 983048 | tf_op jit(solution)/shard_map/ppermute | solution.py:257
  133.5 17.8 %collective-permute-start.3 = (bf16[256,640]{1,0:T(8,128)(2,1)S(1)}, bf16[256,640]{1,0:T(8,128)(2,1)S(1)}, u32[]{:S(2)}, u32[]{:S(2)}) collective-permute-start(bf16[256,640]{1,0:T(8,128)(2,1)S(1)} %bitcast.25), channel_id=1, source_target_pairs={{0,1},{1,2},{2,3},{3,0},{4,5},{5,6},{6,7},{7,4},{8,9},{9,10},{10,1... | collective-permute-start | bytes 983048 | tf_op jit(solution)/shard_map/ppermute | solution.py:257
  135.6 18.6 %all-to-all-start.3 = ((bf16[8,20,1280]{2,1,0:T(8,128)(2,1)}), bf16[8,20,1280]{2,1,0:T(8,128)(2,1)S(1)}, u32[]{:S(2)}, u32[]{:S(2)}) async-start(bf16[8,20,1280]{2,1,0:T(8,128)(2,1)} %reshape.39), calls=%async_computation.4 | async-start | bytes 983040 | tf_op jit(solution)/shard_map/all_to_all | solution.py:292
Sparse Core Ops, SparseCore 0:
  43.3 34.9 all-gather.2
  100.0 28.3 reduce-scatter.1

commit v4 on v3

--- a/solution.py
+++ b/solution.py
@@ -20,9 +20,11 @@
 TOK = 512
 FRAMES = 64
 LANES = 128
+STEPS = 2
 GO = 384
 TILES = 4 * W // LANES
-BLOCK = 128
+HALF_TILES = 5
+BLOCK = 256
 TEMPER = HS ** (-0.5)
 TM = ("z", "yl", "core")
 Y = ("dp", "yl")
@@ -68,102 +70,157 @@
     return jnp.concatenate([low, high], axis=1).astype(BF)
 
 
-def one_hot(feat):
-    places = lax.broadcasted_iota(jnp.int32, (D, W), 0)
+def one_hot(feat, among):
+    places = lax.broadcasted_iota(jnp.int32, (among, W), 0)
     return jnp.where(places == feat, 1.0, 0.0).astype(BF)
 
 
-def pick_kernel(x_ref, order_ref, go_ref, n_ref, out_ref, pick_s):
-    @pl.when(pl.program_id(0) == 0)
-    def _():
-        pick_s[...] = one_hot(order_ref[x_ref[0]])
-
-    for at, ref in enumerate((go_ref, n_ref)):
-        rows = dot(ref[...].reshape(-1, D), pick_s[...])
-        out_ref[:, :, at * W : (at + 1) * W] = to_chunks(rows)
+def pick_kernel(x_ref, order_ref, go_hbm, n_hbm, out_hbm, rows_s, out_s, sems, out_sems):
+    part = NT * PT // STEPS
+    first = lax.rem(x_ref[0], 2) * (D // 2)
+    fetches = [
+        [
+            pltpu.make_async_copy(
+                hbm.at[f, pl.ds(i * part, part), pl.ds(pl.multiple_of(first, LANES), D // 2)],
+                rows_s.at[at, i, f],
+                sems.at[(at * STEPS + i) * FR + f],
+            )
+            for at, hbm in enumerate((go_hbm, n_hbm))
+            for f in range(FR)
+        ]
+        for i in range(STEPS)
+    ]
+    for group in fetches:
+        for fetch in group:
+            fetch.start()
+    pick = one_hot(order_ref[x_ref[0]] - first, D // 2)
+    chunks = NT // STEPS
+    stores = []
+    for i in range(STEPS):
+        for fetch in fetches[i]:
+            fetch.wait()
+        for at in range(2):
+            rows = dot(rows_s[at, i].reshape(FR * part, D // 2), pick)
+            out_s[i * chunks : (i + 1) * chunks, :, at * W : (at + 1) * W] = to_chunks(rows)
+        own = pl.ds(i * chunks, chunks)
+        stores.append(pltpu.make_async_copy(out_s.at[own], out_hbm.at[own], out_sems.at[i]))
+        stores[-1].start()
+    for store in stores:
+        store.wait()
 
 
 def pick(x, order, grad_output, normed):
-    steps = 4
-    block = pl.BlockSpec((FR, NT * PT // steps, D), lambda i: (0, i, 0))
+    hbm = pl.BlockSpec(memory_space=pl.ANY)
+    shape = (NT, 2 * PT, 2 * W)
     return call(
         pick_kernel,
-        jax.ShapeDtypeStruct((NT, 2 * PT, 2 * W), BF),
+        jax.ShapeDtypeStruct(shape, BF),
         850_000_000,
         limit=60 * 1024 * 1024,
-        grid=(steps,),
         in_specs=[
             pl.BlockSpec(memory_space=pltpu.SMEM),
-            pl.BlockSpec((NX, 1, W), lambda i: (0, 0, 0)),
-            block,
-            block,
+            pl.BlockSpec(memory_space=pltpu.VMEM),
+            hbm,
+            hbm,
         ],
-        out_specs=pl.BlockSpec((NT // steps, 2 * PT, 2 * W), lambda i: (i, 0, 0)),
-        scratch_shapes=[pltpu.VMEM((D, W), BF)],
+        out_specs=hbm,
+        scratch_shapes=[
+            pltpu.VMEM((2, STEPS, FR, NT * PT // STEPS, D // 2), BF),
+            pltpu.VMEM(shape, BF),
+            pltpu.SemaphoreType.DMA((2 * STEPS * FR,)),
+            pltpu.SemaphoreType.DMA((STEPS,)),
+        ],
     )(x, order, grad_output, normed)
 
 
-def pack_kernel(q_ref, k_ref, v_ref, qkv_ref):
-    for at, ref in enumerate((q_ref, k_ref, v_ref)):
-        rows = jnp.concatenate([ref[f].astype(F32).T for f in range(FR)], axis=0)
-        qkv_ref[:, :, at * W : (at + 1) * W] = to_chunks(rows)
+def pack_kernel(q_ref, k_ref, v_ref, out_ref):
+    packed = [
+        ref[...].reshape(FR * W, NT * PT).astype(F32).T.reshape(NT, PT, FR * W) for ref in (q_ref, k_ref, v_ref)
+    ]
+    out_ref[...] = jnp.concatenate(packed, axis=1).astype(BF)
 
 
 def reorder_kernel(feat_ref, w_ref, out_ref):
     for at in range(NX):
-        out_ref[at] = dot(w_ref[...], one_hot(feat_ref[at])).astype(BF)
+        out_ref[at] = dot(w_ref[...], one_hot(feat_ref[at], D)).astype(BF)
+
+
+def place(p, f):
+    return (p // 4) * BLOCK + f * (BLOCK // 2) + (p % 4) * NT
 
 
 def attend_kernel(x_ref, qkv_ref, gon_ref, wout_ref, wqkv_hbm, grads_ref, *rest):
-    norm_refs, (wide_s, rows_s, all_t, g_t, norm_s, go_s, wqkv_s, sems) = rest[:NX], rest[NX:]
+    norm_refs, (wide_s, rows_s, v_s, qkvg_t, g_t, norm_s, go_s, wqkv_s, sems) = rest[:NX], rest[NX:]
     copies = [
         pltpu.make_async_copy(gon_ref.at[at, :, :, pl.ds(0, GO)], go_s.at[at], sems.at[at]) for at in range(NX)
     ]
     copies.append(pltpu.make_async_copy(wqkv_hbm, wqkv_s, sems.at[NX]))
     for copy in copies:
         copy.start()
-    half = LANES // 2
-    for t in range(7):
-        wide_s[t] = qkv_ref[:, :, t * LANES : (t + 1) * LANES].reshape(TOK, LANES).astype(F32)
-    wide_s[7, :, :half] = qkv_ref[:, :, 7 * LANES :].reshape(TOK, half).astype(F32)
+    half = BLOCK // 2
+    values = qkv_ref[...].astype(F32)
+    for a in range(3):
+        own = values[:, a * PT : (a + 1) * PT, :].reshape(NT * PT, FR * W)
+        for t in range(HALF_TILES):
+            wide_s[t, : NT * PT, :] = own[:, t * LANES : (t + 1) * LANES]
+        for p in range(PT):
+            for t in range(HALF_TILES):
+                rows_s[p * NT : (p + 1) * NT, t * LANES : (t + 1) * LANES] = wide_s[t, pl.ds(p, NT, stride=PT), :]
+        rows = rows_s[...]
+        if a > 0:
+            v_s[a - 1] = rows.astype(BF)
+        turned = rows.T.astype(BF)
+        for b in range(TOK // BLOCK):
+            for f in range(FR):
+                start = b * BLOCK + f * half
+                qkvg_t[a * W : (a + 1) * W, start : start + half] = turned[
+                    f * W : (f + 1) * W, b * half : (b + 1) * half
+                ]
     acc = jnp.zeros((TOK, W), F32)
     for at in range(NX):
         copies[at].wait()
         acc = acc + dot_nt(go_s[at].reshape(TOK, GO)[:, :W], wout_ref[at])
-    ga = acc.astype(BF).astype(F32)
-    wide_s[7, :, half:] = ga[:, :half]
-    for t in (8, 9):
-        wide_s[t] = ga[:, (t - 8) * LANES + half : (t - 7) * LANES + half]
+    wide_s[0] = acc[:, :LANES]
+    wide_s[1] = acc[:, LANES : 2 * LANES]
+    wide_s[2, :, : W - 2 * LANES] = acc[:, 2 * LANES :]
     for p in range(PT):
-        for t in range(TILES):
-            rows_s[p * FRAMES : (p + 1) * FRAMES, t * LANES : (t + 1) * LANES] = wide_s[
-                t, pl.ds(p, FRAMES, stride=PT), :
-            ].astype(BF)
-    all_t[...] = rows_s[...].T
-    row_patch = lax.broadcasted_iota(jnp.int32, (BLOCK, BLOCK), 0) // FRAMES
-    col_patch = lax.broadcasted_iota(jnp.int32, (BLOCK, BLOCK), 1) // FRAMES
+        for f in range(FR):
+            at = place(p, f)
+            for t in range(3):
+                wide = min(LANES, W - t * LANES)
+                piece = wide_s[t, pl.ds(f * PT + p, NT, stride=FR * PT), :]
+                g_t[at : at + NT, t * LANES : t * LANES + wide] = piece[:, :wide]
+    qkvg_t[3 * W :, :] = g_t[:TOK, :W].T.astype(BF)
+    row_patch = lax.broadcasted_iota(jnp.int32, (BLOCK, BLOCK), 0) // NT % 4
+    col_patch = lax.broadcasted_iota(jnp.int32, (BLOCK, BLOCK), 1) // NT % 4
     same = row_patch == col_patch
     for b in range(TOK // BLOCK):
-        rows = slice(b * BLOCK, (b + 1) * BLOCK)
+        cols = slice(b * BLOCK, (b + 1) * BLOCK)
+        own = slice(b * half, (b + 1) * half)
         for h in range(HEADS):
-            at = [slice(i * W + h * HS, i * W + (h + 1) * HS) for i in range(4)]
-            q_t, k_t, v_t, ga_t = [all_t[cols, rows] for cols in at]
-            scores = dot(rows_s[rows, at[1]], q_t) * TEMPER
+            heads = [slice(i * W + h * HS, i * W + (h + 1) * HS) for i in range(4)]
+            q_t, k_t, v_t, ga_t = [qkvg_t[head, cols] for head in heads]
+            k_rows, v_rows = [
+                jnp.concatenate([v_s[i, own, heads[f]] for f in range(FR)], axis=0) for i in range(2)
+            ]
+            scores = dot(k_rows, q_t) * TEMPER
             scores = jnp.where(same, scores, -jnp.inf)
             powers = jnp.exp(scores - jnp.max(scores, axis=0, keepdims=True))
             probs = powers * (1.0 / jnp.sum(powers, axis=0, keepdims=True))
             weights = probs.astype(BF)
-            g_t[at[3], rows] = dot(v_t, weights)
-            grad_probs = dot(rows_s[rows, at[2]], ga_t)
+            g_t[heads[3], cols] = dot(v_t, weights)
+            grad_probs = dot(v_rows, ga_t)
             delta = jnp.sum(probs * grad_probs, axis=0, keepdims=True)
             grad_scores = (probs * (grad_probs - delta)).astype(BF)
-            g_t[at[0], rows] = dot(k_t, grad_scores) * TEMPER
-            g_t[at[1], rows] = dot_nt(q_t, grad_scores) * TEMPER
-            g_t[at[2], rows] = dot_nt(ga_t, weights)
+            g_t[heads[0], cols] = dot(k_t, grad_scores) * TEMPER
+            g_t[heads[1], cols] = dot_nt(q_t, grad_scores) * TEMPER
+            g_t[heads[2], cols] = dot_nt(ga_t, weights)
     for t in range(TILES):
         tile = g_t[t * LANES : (t + 1) * LANES, :].T
         for p in range(PT):
-            wide_s[t, pl.ds(p, FRAMES, stride=PT), :] = tile[p * FRAMES : (p + 1) * FRAMES]
+            for f in range(FR):
+                at = place(p, f)
+                wide_s[t, pl.ds(f * PT + p, NT, stride=FR * PT), :] = tile[at : at + NT]
     for t in range(TILES):
         grads_ref[:, t * LANES : (t + 1) * LANES] = wide_s[t].astype(BF)
     copies[NX].wait()
@@ -188,7 +245,8 @@
         in_specs=[scalar, whole, hbm, whole, hbm],
         scratch_shapes=[
             pltpu.VMEM((TILES, TOK, LANES), F32),
-            pltpu.VMEM((TOK, 4 * W), BF),
+            pltpu.VMEM((NT * PT, FR * W), F32),
+            pltpu.VMEM((2, NT * PT, FR * W), BF),
             pltpu.VMEM((4 * W, TOK), BF),
             pltpu.VMEM((4 * W, TOK), F32),
             pltpu.VMEM((NX, TOK // 2, 2 * W), BF),
@@ -244,6 +302,12 @@
                     out_ref[f, :, at * W : (at + 1) * W] = refs[k][:, f * W : (f + 1) * W]
 
 
+def regroup_kernel(in_ref, out_ref):
+    rows = in_ref[...].astype(F32)
+    for at in range(8):
+        out_ref[at] = rows[at * 20 : (at + 1) * 20].astype(BF)
+
+
 def total_kernel(in_ref, qkv_ref, out_ref):
     total = in_ref[0].astype(F32)
     for at in range(1, 8):
@@ -266,7 +330,7 @@
     gon = pick(x.reshape(1), order, grad_output[0], normed[0])
     gon = lax.all_to_all(gon, TM, 0, 0, tiled=True)
     gon = lax.all_gather(gon, "x", axis=0)
-    qkv = call(pack_kernel, jax.ShapeDtypeStruct((NT, 2 * PT, 3 * W), BF), 30_000_000_000)(
+    qkv = call(pack_kernel, jax.ShapeDtypeStruct((NT, 3 * PT, FR * W), BF), 30_000_000_000)(
         *[jnp.swapaxes(item[0], 1, 2) for item in (queries, key_vectors, value_vectors)]
     )
     qkv = lax.all_to_all(qkv, TM, 0, 0, tiled=True)
@@ -289,7 +353,8 @@
         in_specs=[scalar] + [whole] * NX,
     )(x.reshape(1), *all_norm)
 
-    pieces = lax.all_to_all(quarter.reshape(8, 20, 4 * W), "z", 0, 0, tiled=True)
+    pieces = call(regroup_kernel, jax.ShapeDtypeStruct((8, 20, 4 * W), BF), limit=60 * 1024 * 1024)(quarter.reshape(D // 8, 4 * W))
+    pieces = lax.all_to_all(pieces, "z", 0, 0, tiled=True)
     grad_qkv, grad_out = call(
         total_kernel, (jax.ShapeDtypeStruct((3, 20, W), F32), jax.ShapeDtypeStruct((20, W), F32))
     )(pieces)

time: 164 us -> 164 us (level)
  local copies, waits for them, and re-layouts: 1.89 us -> 0.03 us
  starting transfers between devices: 17.8 us -> 16.1 us
    reshape x1 -> x0, local copies, waits for them, and re-layouts: 1.87 us -> none  [on_device(): quarter.reshape(8, 20, 4 * W)]
    all_gather x1, waiting for transfers between devices: 0.25 us -> 1.91 us  [on_device(): gon = lax.all_gather(gon, 'x', axis=0)]
    pallas_call x2 -> x3, Pallas kernels: 6.47 us -> 7.01 us  [the longest x1 3.91 us: pick(): call(pick_kernel, jax.ShapeDtypeStruct(shape, BF), 850000000, limit=60 *...]
  transfers between devices with their start and end apart: 11 -> 11, of which waited for: 8 -> 9; matrix products, arithmetic and copies ran while one was open for 1% -> 0% of each run, Pallas kernels for 6% -> 7%
where the time goes in v4:
time: 164 us; the launch traced here: 161 us
  blocking collectives  52.9 us (32%)
  waiting for transfers between devices  50.5 us (31%)
  Pallas kernels  27.5 us (17%)
  starting transfers between devices  16.1 us (10%)
  between operations  14.2 us (9%)
    all_to_all x1, blocking collectives, on_device(): gon = lax.all_to_all(gon, TM, 0, 0, tiled=True)  31 us
    all_to_all x1, waiting for transfers between devices, on_device(): qkv = lax.all_to_all(qkv, TM, 0, 0, tiled=True)  24.7 us
    ppermute x6, waiting for transfers between devices, shift(): return lax.ppermute(array, 'x', [(i, (i + k) % NX) for i in range(NX)])  22.8 us
    all_to_all x1, blocking collectives, on_device(): lax.all_to_all(own_norm.reshape(NT, PT, 2 * W), TM, 0, 0, tiled=True)  21.9 us
    pallas_call x1, Pallas kernels, attend(): call(attend_kernel, (jax.ShapeDtypeStruct((TOK, 4 * W), BF),) + (jax.Shap...  10.7 us
    ppermute x6, starting transfers between devices, shift(): return lax.ppermute(array, 'x', [(i, (i + k) % NX) for i in range(NX)])  6.59 us
    pallas_call x2, Pallas kernels, weight_half(): return call(weight_kernel, shape, 4000000000, spec)(half, gon, grads, *got)  5.31 us
    all_to_all x1, starting transfers between devices, on_device(): qkv = lax.all_to_all(qkv, TM, 0, 0, tiled=True)  5.06 us
  transfers between devices with their start and end apart: 11, of which 9 were waited for; matrix products, arithmetic and copies ran while one was open for 0% of the time, Pallas kernels for 7%

profile of v4, /device:TPU:1, one launch (start us, length us, event | category | flops | bytes accessed | tf_op | source)
XLA Modules:
  0.0 161.2 jit_solution(12086452962282619103)
XLA Ops:
  7.2 0.0 all-gather.3.cloned.1.call-start
  7.2 3.9 %shard_map.104 = bf16[32,16,640]{2,1,0:T(8,128)(2,1)} custom-call(s32[1]{0:T(128)} %bitcast.x_ref, s32[4,1,320]{2,1,0:T(1,128)} %constant.13.clone.order_ref.feat_ref, bf16[2,256,1280]{2,1,0:T(8,128)(2,1)} %bitcast.35, bf16[2,256,1280]{2,1,0:T(8,128)(2,1)} %bitcast.36), custom_call_target="tpu_custom_call" | custom-call | flops 850000000 | bytes 4000000 | tf_op jit(solution)/shard_map/pallas_call | solution.py:115
  11.2 31.0 %all_to_all.20 = bf16[32,16,640]{2,1,0:T(8,128)(2,1)} all-to-all(bf16[32,16,640]{2,1,0:T(8,128)(2,1)} %shard_map.104), channel_id=1, replica_groups=mesh['dp'=2,'z'=8,'yl'=2,'core'=2,'x'=4] {'z','yl','core'}, dimensions={0} | all-to-all | bytes 1310720 | tf_op jit(solution)/shard_map/all_to_all | solution.py:331
  42.2 1.3 shard_map.103
  43.5 5.1 %all-to-all-start = ((bf16[32,24,640]{2,1,0:T(8,128)(2,1)}), bf16[32,24,640]{2,1,0:T(8,128)(2,1)S(1)}, u32[]{:S(2)}, u32[]{:S(2)}) async-start(bf16[32,24,640]{2,1,0:T(8,128)(2,1)} %shard_map.103), calls=%async_computation | async-start | bytes 1966080 | tf_op jit(solution)/shard_map/all_to_all | solution.py:336
  48.6 0.2 reduce-scatter.2.cloned.1.call-start
  48.8 1.9 %shard_map.105.wout_ref = bf16[4,320,320]{2,1,0:T(8,128)(2,1)S(1)} custom-call(s32[4,1,320]{2,1,0:T(1,128)S(1)} %copy-done, bf16[320,1280]{1,0:T(8,128)(2,1)S(1)} %copy-done.2), custom_call_target="tpu_custom_call" | custom-call | flops 1000000000 | bytes 4000000 | tf_op jit(solution)/shard_map/pallas_call | solution.py:337
  50.7 24.7 %all-to-all-done.qkv_ref = bf16[32,24,640]{2,1,0:T(8,128)(2,1)S(1)} async-done(((bf16[32,24,640]{2,1,0:T(8,128)(2,1)}), bf16[32,24,640]{2,1,0:T(8,128)(2,1)S(1)}, u32[]{:S(2)}, u32[]{:S(2)}) %all-to-all-start) | async-done | bytes 983072 | tf_op jit(solution)/shard_map/all_to_all | solution.py:336
  75.4 1.9 %all-gather.3.cloned.1.call-done = bf16[128,16,640]{2,1,0:T(8,128)(2,1)} async-done(((bf16[32,16,640]{2,1,0:T(8,128)(2,1)}), bf16[128,16,640]{2,1,0:T(8,128)(2,1)}) %all-gather.3.cloned.1.call-update) | async-done | bytes 2621456 | tf_op jit(solution)/shard_map/all_gather | solution.py:332
  77.3 10.7 %shard_map.106 = (bf16[512,1280]{1,0:T(8,128)(2,1)S(1)}, bf16[256,640]{1,0:T(8,128)(2,1)S(1)}, bf16[256,640]{1,0:T(8,128)(2,1)S(1)}, bf16[256,640]{1,0:T(8,128)(2,1)S(1)}, bf16[256,640]{1,0:T(8,128)(2,1)S(1)}) custom-call(s32[1]{0:T(128)} %bitcast.x_ref, bf16[32,24,640]{2,1,0:T(8,128)(2,1)S(1)} %all-to-all-done.qkv_ref, bf16[4,32,16,640]{3,2,1,0:T(8,128)(2,1)} %bitcast.29, ...), custom_call_target="tpu_custom_call" | custom-call | flops 5000000000 | bytes 4000000 | tf_op jit(solution)/shard_map/pallas_call | solution.py:241
  88.0 1.7 %shard_map.109 = bf16[640,1280]{1,0:T(8,128)(2,1)S(1)} custom-call(s32[1]{0:T(128)} %bitcast.16.half_ref, bf16[4,32,16,640]{3,2,1,0:T(8,128)(2,1)S(1)} %bitcast.31, bf16[512,1280]{1,0:T(8,128)(2,1)S(1)} %get-tuple-element.14.grads_ref), custom_call_target="tpu_custom_call" | custom-call | flops 4000000000 | bytes 4000000 | tf_op jit(solution)/shard_map/pallas_call | solution.py:284
  89.7 0.8 collective-permute-start.6
  90.5 0.4 collective-permute-start
  90.8 2.1 %collective-permute-start.1 = (bf16[256,640]{1,0:T(8,128)(2,1)S(1)}, bf16[256,640]{1,0:T(8,128)(2,1)S(1)}, u32[]{:S(2)}, u32[]{:S(2)}) collective-permute-start(bf16[256,640]{1,0:T(8,128)(2,1)S(1)} %get-tuple-element.12), channel_id=1, source_target_pairs={{0,2},{1,3},{2,0},{3,1},{4,6},{5,7},{6,4},{7,5},{8,10},{9,11},{10,... | collective-permute-start | bytes 983048 | tf_op jit(solution)/shard_map/ppermute | solution.py:321
  93.0 1.2 collective-permute-start.2
  94.1 3.6 %shard_map.110 = bf16[640,1280]{1,0:T(8,128)(2,1)} custom-call(s32[1]{0:T(128)} %bitcast.15.half_ref, bf16[4,32,16,640]{3,2,1,0:T(8,128)(2,1)} %bitcast.30, bf16[512,1280]{1,0:T(8,128)(2,1)S(1)} %get-tuple-element.14.grads_ref, bf16[640,1280]{1,0:T(8,128)(2,1)S(1)} %collective-permute-done.6.refs_0_), custom_call_target="tpu_custom_call" | custom-call | flops 4000000000 | bytes 4000000 | tf_op jit(solution)/shard_map/pallas_call | solution.py:284
  97.8 3.4 %collective-permute-done.refs_1_ = bf16[256,640]{1,0:T(8,128)(2,1)S(1)} collective-permute-done((bf16[256,640]{1,0:T(8,128)(2,1)S(1)}, bf16[256,640]{1,0:T(8,128)(2,1)S(1)}, u32[]{:S(2)}, u32[]{:S(2)}) %collective-permute-start) | collective-permute-done | bytes 327712 | tf_op jit(solution)/shard_map/ppermute | solution.py:321
  101.1 6.7 %collective-permute-done.1.refs_2_ = bf16[256,640]{1,0:T(8,128)(2,1)S(1)} collective-permute-done((bf16[256,640]{1,0:T(8,128)(2,1)S(1)}, bf16[256,640]{1,0:T(8,128)(2,1)S(1)}, u32[]{:S(2)}, u32[]{:S(2)}) %collective-permute-start.1) | collective-permute-done | bytes 327712 | tf_op jit(solution)/shard_map/ppermute | solution.py:321
  107.8 0.5 collective-permute-done.2.refs_3_
  108.3 0.2 shard_map.107
  108.4 21.9 %all_to_all.21 = bf16[32,8,640]{2,1,0:T(8,128)(2,1)S(1)} all-to-all(bf16[32,8,640]{2,1,0:T(8,128)(2,1)S(1)} %bitcast.28), channel_id=1, replica_groups=mesh['dp'=2,'z'=8,'yl'=2,'core'=2,'x'=4] {'z','yl','core'}, dimensions={0} | all-to-all | bytes 655360 | tf_op jit(solution)/shard_map/all_to_all | solution.py:347
  130.3 2.4 %collective-permute-start.5 = (bf16[256,640]{1,0:T(8,128)(2,1)S(1)}, bf16[256,640]{1,0:T(8,128)(2,1)S(1)}, u32[]{:S(2)}, u32[]{:S(2)}) collective-permute-start(bf16[256,640]{1,0:T(8,128)(2,1)S(1)} %bitcast.24), channel_id=1, source_target_pairs={{0,3},{1,0},{2,1},{3,2},{4,7},{5,4},{6,5},{7,6},{8,11},{9,8},{10,9... | collective-permute-start | bytes 983048 | tf_op jit(solution)/shard_map/ppermute | solution.py:321
  132.6 0.4 collective-permute-start.4
  133.0 0.2 collective-permute-start.3
  133.2 1.8 %shard_map.111 = bf16[8,20,1280]{2,1,0:T(8,128)(2,1)} custom-call(bf16[160,1280]{1,0:T(8,128)(2,1)} %bitcast.37), custom_call_target="tpu_custom_call" | custom-call | bytes 4000000 | tf_op jit(solution)/shard_map/pallas_call | solution.py:356
  135.0 3.5 %all-to-all-start.3 = ((bf16[8,20,1280]{2,1,0:T(8,128)(2,1)}), bf16[8,20,1280]{2,1,0:T(8,128)(2,1)S(1)}, u32[]{:S(2)}, u32[]{:S(2)}) async-start(bf16[8,20,1280]{2,1,0:T(8,128)(2,1)} %shard_map.111), calls=%async_computation.4 | async-start | bytes 983040 | tf_op jit(solution)/shard_map/all_to_all | solution.py:357
  138.5 0.5 collective-permute-done.5.refs_3_
  139.0 2.8 %collective-permute-done.4.refs_2_ = bf16[256,640]{1,0:T(8,128)(2,1)S(1)} collective-permute-done((bf16[256,640]{1,0:T(8,128)(2,1)S(1)}, bf16[256,640]{1,0:T(8,128)(2,1)S(1)}, u32[]{:S(2)}, u32[]{:S(2)}) %collective-permute-start.4) | collective-permute-done | bytes 327712 | tf_op jit(solution)/shard_map/ppermute | solution.py:321
  141.9 8.9 %collective-permute-done.3.refs_1_ = bf16[256,640]{1,0:T(8,128)(2,1)S(1)} collective-permute-done((bf16[256,640]{1,0:T(8,128)(2,1)S(1)}, bf16[256,640]{1,0:T(8,128)(2,1)S(1)}, u32[]{:S(2)}, u32[]{:S(2)}) %collective-permute-start.3) | collective-permute-done | bytes 327712 | tf_op jit(solution)/shard_map/ppermute | solution.py:321
  150.8 1.7 %shard_map.108 = bf16[2,256,1280]{2,1,0:T(8,128)(2,1)} custom-call(s32[1]{0:T(128)} %bitcast.x_ref, bf16[256,640]{1,0:T(8,128)(2,1)S(1)} %bitcast.27, bf16[256,640]{1,0:T(8,128)(2,1)S(1)} %collective-permute-done.3.refs_1_, bf16[256,640]{1,0:T(8,128)(2,1)S(1)} %collective-permute-done.4.refs_2_, bf16[256,640]{1,0:T(8,128)(2,1)S(1)} %collective-permute-done.5.refs_3_), custom_call_target="tpu_custom_call" | custom-call | flops 40000000000 | bytes 4000000 | tf_op jit(solution)/shard_map/pallas_call | solution.py:349
  152.5 1.1 all-to-all-done.3.in_ref
  153.7 0.8 shard_map.112
  (16 shorter events, 0.1 us)
Async XLA Ops:
  7.2 70.1 %all-gather.3.cloned.1.call-start = ((), (), s32[]{:S(2)}) async-start(), calls=%async_computation.6 | async-start | bytes 3276800 | tf_op jit(solution)/shard_map/all_gather | solution.py:332
  11.1 31.1 %copy-start.3 = (bf16[1,2,256,320]{2,3,1,0:T(8,128)(2,1)S(1)}, bf16[1,2,256,320]{2,3,1,0:T(8,128)(2,1)}, u32[]{:S(2)}) copy-start(bf16[1,2,256,320]{2,3,1,0:T(8,128)(2,1)} %param.8) | copy-start | bytes 983044
  11.1 31.1 %copy-start.4 = (bf16[1,2,256,320]{2,3,1,0:T(8,128)(2,1)S(1)}, bf16[1,2,256,320]{2,3,1,0:T(8,128)(2,1)}, u32[]{:S(2)}) copy-start(bf16[1,2,256,320]{2,3,1,0:T(8,128)(2,1)} %param.9) | copy-start | bytes 983044
  11.2 31.1 %copy-start.5 = (bf16[1,2,256,320]{2,3,1,0:T(8,128)(2,1)S(1)}, bf16[1,2,256,320]{2,3,1,0:T(8,128)(2,1)}, u32[]{:S(2)}) copy-start(bf16[1,2,256,320]{2,3,1,0:T(8,128)(2,1)} %param.10) | copy-start | bytes 983044
  43.5 5.3 %copy-start = (s32[4,1,320]{2,1,0:T(1,128)S(1)}, s32[4,1,320]{2,1,0:T(1,128)}, u32[]{:S(2)}) copy-start(s32[4,1,320]{2,1,0:T(1,128)} %constant.13.clone.order_ref.feat_ref) | copy-start | bytes 15364
  43.5 5.3 %copy-start.2 = (bf16[320,1280]{1,0:T(8,128)(2,1)S(1)}, bf16[320,1280]{1,0:T(8,128)(2,1)}, u32[]{:S(2)}) copy-start(bf16[320,1280]{1,0:T(8,128)(2,1)} %w_ref.1) | copy-start | bytes 2457604
  43.5 31.9 %all-to-all-start = ((bf16[32,24,640]{2,1,0:T(8,128)(2,1)}), bf16[32,24,640]{2,1,0:T(8,128)(2,1)S(1)}, u32[]{:S(2)}, u32[]{:S(2)}) async-start(bf16[32,24,640]{2,1,0:T(8,128)(2,1)} %shard_map.103), calls=%async_computation | async-start | bytes 1966080 | tf_op jit(solution)/shard_map/all_to_all | solution.py:336
  48.6 84.7 %reduce-scatter.2.cloned.1.call-start = ((), (), s32[]{:S(2)}) async-start(), calls=%async_computation.5 | async-start | bytes 2048000 | tf_op jit(solution)/shard_map/reduce_scatter | solution.py:344
  77.3 10.7 %copy-start.1 = (bf16[128,16,640]{2,1,0:T(8,128)(2,1)S(1)}, bf16[128,16,640]{2,1,0:T(8,128)(2,1)}, u32[]{:S(2)}) copy-start(bf16[128,16,640]{2,1,0:T(8,128)(2,1)} %all-gather.3.cloned.1.call-done) | copy-start | bytes 7864324
  89.7 4.4 %collective-permute-start.6 = (bf16[640,1280]{1,0:T(8,128)(2,1)S(1)}, bf16[640,1280]{1,0:T(8,128)(2,1)S(1)}, u32[]{:S(2)}, u32[]{:S(2)}) collective-permute-start(bf16[640,1280]{1,0:T(8,128)(2,1)S(1)} %shard_map.109), channel_id=1, source_target_pairs={{0,4},{4,0},{1,5},{5,1},{2,6},{6,2},{3,7},{7,3},{8,12},{12,8},{9,1... | collective-permute-start | bytes 4915208 | tf_op jit(solution)/shard_map/ppermute | solution.py:342
  90.5 10.7 %collective-permute-start = (bf16[256,640]{1,0:T(8,128)(2,1)S(1)}, bf16[256,640]{1,0:T(8,128)(2,1)S(1)}, u32[]{:S(2)}, u32[]{:S(2)}) collective-permute-start(bf16[256,640]{1,0:T(8,128)(2,1)S(1)} %get-tuple-element.11), channel_id=1, source_target_pairs={{0,1},{1,2},{2,3},{3,0},{4,5},{5,6},{6,7},{7,4},{8,9},{9,10},{10,1... | collective-permute-start | bytes 983048 | tf_op jit(solution)/shard_map/ppermute | solution.py:321
  90.8 17.0 %collective-permute-start.1 = (bf16[256,640]{1,0:T(8,128)(2,1)S(1)}, bf16[256,640]{1,0:T(8,128)(2,1)S(1)}, u32[]{:S(2)}, u32[]{:S(2)}) collective-permute-start(bf16[256,640]{1,0:T(8,128)(2,1)S(1)} %get-tuple-element.12), channel_id=1, source_target_pairs={{0,2},{1,3},{2,0},{3,1},{4,6},{5,7},{6,4},{7,5},{8,10},{9,11},{10,... | collective-permute-start | bytes 983048 | tf_op jit(solution)/shard_map/ppermute | solution.py:321
  93.0 15.3 %collective-permute-start.2 = (bf16[256,640]{1,0:T(8,128)(2,1)S(1)}, bf16[256,640]{1,0:T(8,128)(2,1)S(1)}, u32[]{:S(2)}, u32[]{:S(2)}) collective-permute-start(bf16[256,640]{1,0:T(8,128)(2,1)S(1)} %get-tuple-element.13), channel_id=1, source_target_pairs={{0,3},{1,0},{2,1},{3,2},{4,7},{5,4},{6,5},{7,6},{8,11},{9,8},{10,9... | collective-permute-start | bytes 983048 | tf_op jit(solution)/shard_map/ppermute | solution.py:321
  130.3 8.7 %collective-permute-start.5 = (bf16[256,640]{1,0:T(8,128)(2,1)S(1)}, bf16[256,640]{1,0:T(8,128)(2,1)S(1)}, u32[]{:S(2)}, u32[]{:S(2)}) collective-permute-start(bf16[256,640]{1,0:T(8,128)(2,1)S(1)} %bitcast.24), channel_id=1, source_target_pairs={{0,3},{1,0},{2,1},{3,2},{4,7},{5,4},{6,5},{7,6},{8,11},{9,8},{10,9... | collective-permute-start | bytes 983048 | tf_op jit(solution)/shard_map/ppermute | solution.py:321
  132.6 9.2 %collective-permute-start.4 = (bf16[256,640]{1,0:T(8,128)(2,1)S(1)}, bf16[256,640]{1,0:T(8,128)(2,1)S(1)}, u32[]{:S(2)}, u32[]{:S(2)}) collective-permute-start(bf16[256,640]{1,0:T(8,128)(2,1)S(1)} %bitcast.25), channel_id=1, source_target_pairs={{0,2},{1,3},{2,0},{3,1},{4,6},{5,7},{6,4},{7,5},{8,10},{9,11},{10,... | collective-permute-start | bytes 983048 | tf_op jit(solution)/shard_map/ppermute | solution.py:321
  133.0 17.8 %collective-permute-start.3 = (bf16[256,640]{1,0:T(8,128)(2,1)S(1)}, bf16[256,640]{1,0:T(8,128)(2,1)S(1)}, u32[]{:S(2)}, u32[]{:S(2)}) collective-permute-start(bf16[256,640]{1,0:T(8,128)(2,1)S(1)} %bitcast.26), channel_id=1, source_target_pairs={{0,1},{1,2},{2,3},{3,0},{4,5},{5,6},{6,7},{7,4},{8,9},{9,10},{10,1... | collective-permute-start | bytes 983048 | tf_op jit(solution)/shard_map/ppermute | solution.py:321
  135.0 18.6 %all-to-all-start.3 = ((bf16[8,20,1280]{2,1,0:T(8,128)(2,1)}), bf16[8,20,1280]{2,1,0:T(8,128)(2,1)S(1)}, u32[]{:S(2)}, u32[]{:S(2)}) async-start(bf16[8,20,1280]{2,1,0:T(8,128)(2,1)} %shard_map.111), calls=%async_computation.4 | async-start | bytes 983040 | tf_op jit(solution)/shard_map/all_to_all | solution.py:357
Sparse Core Ops, SparseCore 0:
  42.3 34.9 all-gather.2
  97.9 30.0 reduce-scatter.1

commit v5 on v4

--- a/solution.py
+++ b/solution.py
@@ -30,7 +30,7 @@
 Y = ("dp", "yl")
 BF = jnp.bfloat16
 F32 = jnp.float32
-LIMIT = 48 * 1024 * 1024
+LIMIT = 24 * 1024 * 1024
 
 
 def feature_order():
@@ -149,12 +149,18 @@
     return (p // 4) * BLOCK + f * (BLOCK // 2) + (p % 4) * NT
 
 
-def attend_kernel(x_ref, qkv_ref, gon_ref, wout_ref, wqkv_hbm, grads_ref, *rest):
+def attend_kernel(x_ref, qkv_ref, own_hbm, left_hbm, right_hbm, low_hbm, high_hbm, wout_ref, wqkv_hbm, grads_ref, *rest):
     norm_refs, (wide_s, rows_s, v_s, qkvg_t, g_t, norm_s, go_s, wqkv_s, sems) = rest[:NX], rest[NX:]
+    cols = pl.ds(0, GO)
     copies = [
-        pltpu.make_async_copy(gon_ref.at[at, :, :, pl.ds(0, GO)], go_s.at[at], sems.at[at]) for at in range(NX)
+        pltpu.make_async_copy(hbm.at[:, :, cols], go_s.at[at], sems.at[at])
+        for at, hbm in enumerate((own_hbm, left_hbm, right_hbm))
     ]
-    copies.append(pltpu.make_async_copy(wqkv_hbm, wqkv_s, sems.at[NX]))
+    copies += [
+        pltpu.make_async_copy(hbm.at[:, :, cols], go_s.at[3, pl.ds(i * NT // 2, NT // 2)], sems.at[3 + i])
+        for i, hbm in enumerate((low_hbm, high_hbm))
+    ]
+    copies.append(pltpu.make_async_copy(wqkv_hbm, wqkv_s, sems.at[5]))
     for copy in copies:
         copy.start()
     half = BLOCK // 2
@@ -177,9 +183,11 @@
                     f * W : (f + 1) * W, b * half : (b + 1) * half
                 ]
     acc = jnp.zeros((TOK, W), F32)
-    for at in range(NX):
-        copies[at].wait()
-        acc = acc + dot_nt(go_s[at].reshape(TOK, GO)[:, :W], wout_ref[at])
+    for at, needed, behind in ((0, (0,), 0), (1, (1,), 1), (2, (2,), 3), (3, (3, 4), 2)):
+        for i in needed:
+            copies[i].wait()
+        block = lax.rem(x_ref[0] + NX - behind, NX)
+        acc = acc + dot_nt(go_s[at].reshape(TOK, GO)[:, :W], wout_ref[block])
     wide_s[0] = acc[:, :LANES]
     wide_s[1] = acc[:, LANES : 2 * LANES]
     wide_s[2, :, : W - 2 * LANES] = acc[:, 2 * LANES :]
@@ -223,7 +231,7 @@
                 wide_s[t, pl.ds(f * PT + p, NT, stride=FR * PT), :] = tile[at : at + NT]
     for t in range(TILES):
         grads_ref[:, t * LANES : (t + 1) * LANES] = wide_s[t].astype(BF)
-    copies[NX].wait()
+    copies[5].wait()
     norm = dot(grads_ref[:, : 3 * W], wqkv_s[...])
     for at in range(NX):
         part = norm[:, at * W : (at + 1) * W].reshape(NT, 2 * PT, W)
@@ -242,7 +250,7 @@
         attend_kernel,
         (jax.ShapeDtypeStruct((TOK, 4 * W), BF),) + (jax.ShapeDtypeStruct((TOK // 2, 2 * W), BF),) * NX,
         5_000_000_000,
-        in_specs=[scalar, whole, hbm, whole, hbm],
+        in_specs=[scalar, whole] + [hbm] * 5 + [whole, hbm],
         scratch_shapes=[
             pltpu.VMEM((TILES, TOK, LANES), F32),
             pltpu.VMEM((NT * PT, FR * W), F32),
@@ -252,36 +260,61 @@
             pltpu.VMEM((NX, TOK // 2, 2 * W), BF),
             pltpu.VMEM((NX, NT, 2 * PT, GO), BF),
             pltpu.VMEM((3 * W, D), BF),
-            pltpu.SemaphoreType.DMA((NX + 1,)),
+            pltpu.SemaphoreType.DMA((6,)),
         ],
-    )(x, qkv, gon, w_ordered, w_qkv)
-
-
-def weight_kernel(half_ref, gon_ref, grads_ref, *refs):
-    del half_ref
-    out_ref = refs[-1]
-    gon_t = gon_ref[0].reshape(TOK, 2 * W).astype(F32).T.astype(BF)
-    for rows, cols in ((slice(W, 2 * W), slice(0, 3 * W)), (slice(0, W), slice(3 * W, 4 * W))):
-        total = dot(gon_t[rows], grads_ref[:, cols])
-        if len(refs) == 2:
-            total = total + refs[0][:, cols].astype(F32)
-        out_ref[:, cols] = total.astype(BF)
-
-
-def weight_half(half, gon, grads, *got):
-    block = pl.BlockSpec((W, 4 * W), lambda j, half: (j, 0))
-    spec = pltpu.PrefetchScalarGridSpec(
-        num_scalar_prefetch=1,
-        grid=(2,),
-        in_specs=[
-            pl.BlockSpec((1, NT, 2 * PT, 2 * W), lambda j, half: (half[0] * 2 + j, 0, 0, 0)),
-            pl.BlockSpec((TOK, 4 * W), lambda j, half: (0, 0)),
-        ]
-        + [block] * len(got),
-        out_specs=block,
-    )
-    shape = jax.ShapeDtypeStruct((2 * W, 4 * W), BF)
-    return call(weight_kernel, shape, 4_000_000_000, spec)(half, gon, grads, *got)
+    )(x, qkv, *gon, w_ordered, w_qkv)
+
+
+def weight_kernel(place_ref, own_hbm, left_hbm, right_hbm, low_hbm, high_hbm, grads_ref, *refs):
+    got_refs, (out_hbm, gon_s, out_s, sems, out_sems) = refs[:-5], refs[-5:]
+    near = ((own_hbm, 0), (left_hbm, 3), (right_hbm, 1))
+    for j in range(2):
+        ahead = lax.rem(place_ref[1] * 2 + j + NX - place_ref[0], NX)
+        for hbm, distance in near:
+
+            @pl.when(ahead == distance)
+            def _(hbm=hbm, j=j):
+                pltpu.make_async_copy(hbm, gon_s.at[j], sems.at[j]).start()
+
+        @pl.when(ahead == 2)
+        def _(j=j):
+            for i, hbm in enumerate((low_hbm, high_hbm)):
+                pltpu.make_async_copy(hbm, gon_s.at[j, pl.ds(i * NT // 2, NT // 2)], sems.at[j]).start()
+
+    stores = []
+    for j in range(2):
+        pltpu.make_async_copy(own_hbm, gon_s.at[j], sems.at[j]).wait()
+        gon_t = gon_s[j].reshape(TOK, 2 * W).astype(F32).T.astype(BF)
+        own = slice(j * W, (j + 1) * W)
+        for rows, cols in ((slice(W, 2 * W), slice(0, 3 * W)), (slice(0, W), slice(3 * W, 4 * W))):
+            total = dot(gon_t[rows], grads_ref[:, cols])
+            for got_ref in got_refs:
+                total = total + got_ref[own, cols].astype(F32)
+            out_s[own, cols] = total.astype(BF)
+        rows = pl.ds(j * W, W)
+        stores.append(pltpu.make_async_copy(out_s.at[rows], out_hbm.at[rows], out_sems.at[j]))
+        stores[-1].start()
+    for store in stores:
+        store.wait()
+
+
+def weight_half(place, gon, grads, *got):
+    whole = pl.BlockSpec(memory_space=pltpu.VMEM)
+    hbm = pl.BlockSpec(memory_space=pl.ANY)
+    shape = (2 * W, 4 * W)
+    return call(
+        weight_kernel,
+        jax.ShapeDtypeStruct(shape, BF),
+        4_000_000_000,
+        in_specs=[pl.BlockSpec(memory_space=pltpu.SMEM)] + [hbm] * 5 + [whole] * (1 + len(got)),
+        out_specs=hbm,
+        scratch_shapes=[
+            pltpu.VMEM((2, NT, 2 * PT, 2 * W), BF),
+            pltpu.VMEM(shape, BF),
+            pltpu.SemaphoreType.DMA((2,)),
+            pltpu.SemaphoreType.DMA((2,)),
+        ],
+    )(place, *gon, grads, *got)
 
 
 def add_kernel(*refs):
@@ -329,7 +362,9 @@
     whole = pl.BlockSpec(memory_space=pltpu.VMEM)
     gon = pick(x.reshape(1), order, grad_output[0], normed[0])
     gon = lax.all_to_all(gon, TM, 0, 0, tiled=True)
-    gon = lax.all_gather(gon, "x", axis=0)
+    left, right = shift(gon, 1), shift(gon, NX - 1)
+    low, high = shift(left[: NT // 2], 1), shift(right[NT // 2 :], NX - 1)
+    gon = (gon, left, right, low, high)
     qkv = call(pack_kernel, jax.ShapeDtypeStruct((NT, 3 * PT, FR * W), BF), 30_000_000_000)(
         *[jnp.swapaxes(item[0], 1, 2) for item in (queries, key_vectors, value_vectors)]
     )
@@ -338,9 +373,9 @@
     grads, *parts = attend(x.reshape(1), qkv, gon, w_ordered, jnp.swapaxes(w_qkv, 1, 2).reshape(3 * W, D))
 
     moved = [parts[0]] + [shift(parts[k], k) for k in range(1, NX)]
-    sent = weight_half((1 - core).reshape(1), gon, grads)
+    sent = weight_half(jnp.stack([x, 1 - core]), gon, grads)
     got = lax.ppermute(sent, "core", [(0, 1), (1, 0)])
-    both = weight_half(core.reshape(1), gon, grads, got).reshape(4, D // 8, 4 * W)
+    both = weight_half(jnp.stack([x, core]), gon, grads, got).reshape(4, D // 8, 4 * W)
     quarter = lax.psum_scatter(both, Y, scatter_dimension=0, tiled=True)
 
     own_norm = call(add_kernel, jax.ShapeDtypeStruct((TOK // 2, 2 * W), BF), 40_000_000_000)(*moved)

time: 164 us -> 171 us (1.043)
  blocking collectives: 52.9 us -> 21.7 us
  starting transfers between devices: 16.1 us -> 34.1 us
  waiting for transfers between devices: 50.5 us -> 61.8 us
  local copies, waits for them, and re-layouts: 0.03 us -> 7.24 us
  Pallas kernels: 27.5 us -> 29.7 us
    all_to_all x1 -> x0, blocking collectives: 31 us -> none  [on_device(): gon = lax.all_to_all(gon, TM, 0, 0, tiled=True)]
    all_to_all x1, waiting for transfers between devices: 24.7 us -> 1.45 us  [on_device(): qkv = lax.all_to_all(qkv, TM, 0, 0, tiled=True)]
    all_to_all x0 -> x1, waiting for transfers between devices: none -> 18.3 us  [on_device(): gon = lax.all_to_all(gon, TM, 0, 0, tiled=True)]
    ppermute x6 -> x10, waiting for transfers between devices: 22.8 us -> 40.2 us  [shift(): return lax.ppermute(array, 'x', [(i, (i + k) % NX) for i in range(NX)])]
    all_to_all x0 -> x1, starting transfers between devices: none -> 11.1 us  [on_device(): gon = lax.all_to_all(gon, TM, 0, 0, tiled=True)]
    unnamed x12 -> x20, local copies, waits for them, and re-layouts: 0.03 us -> 5.73 us
    ppermute x6 -> x10, starting transfers between devices: 6.59 us -> 11.5 us  [shift(): return lax.ppermute(array, 'x', [(i, (i + k) % NX) for i in range(NX)])]
    ppermute x1, starting transfers between devices: 0.76 us -> 2.99 us  [on_device(): got = lax.ppermute(sent, 'core', [(0, 1), (1, 0)])]
  transfers between devices with their start and end apart: 11 -> 15, of which waited for: 9 -> 11; matrix products, arithmetic and copies ran while one was open for 0% -> 1% of each run, Pallas kernels for 7% -> 7%
where the time goes in v5:
time: 171 us; the launch traced here: 169 us
  waiting for transfers between devices  61.8 us (36%)
  starting transfers between devices  34.1 us (20%)
  Pallas kernels  29.7 us (17%)
  blocking collectives  21.7 us (13%)
  between operations  14.2 us (8%)
  local copies, waits for them, and re-layouts  7.24 us (4%)
    ppermute x10, waiting for transfers between devices, shift(): return lax.ppermute(array, 'x', [(i, (i + k) % NX) for i in range(NX)])  40.2 us
    all_to_all x1, blocking collectives, on_device(): lax.all_to_all(own_norm.reshape(NT, PT, 2 * W), TM, 0, 0, tiled=True)  21.7 us
    all_to_all x1, waiting for transfers between devices, on_device(): gon = lax.all_to_all(gon, TM, 0, 0, tiled=True)  18.3 us
    ppermute x10, starting transfers between devices, shift(): return lax.ppermute(array, 'x', [(i, (i + k) % NX) for i in range(NX)])  11.5 us
    all_to_all x1, starting transfers between devices, on_device(): gon = lax.all_to_all(gon, TM, 0, 0, tiled=True)  11.1 us
    pallas_call x1, Pallas kernels, attend(): call(attend_kernel, (jax.ShapeDtypeStruct((TOK, 4 * W), BF),) + (jax.Shap...  11 us
    pallas_call x2, Pallas kernels, weight_half(): call(weight_kernel, jax.ShapeDtypeStruct(shape, BF), 4000000000, in_specs...  7.03 us
    unnamed x20, local copies, waits for them, and re-layouts  5.73 us
  transfers between devices with their start and end apart: 15, of which 11 were waited for; matrix products, arithmetic and copies ran while one was open for 1% of the time, Pallas kernels for 7%

profile of v5, /device:TPU:1, one launch (start us, length us, event | category | flops | bytes accessed | tf_op | source)
XLA Modules:
  0.0 168.9 jit_solution(7332870935768335055)
XLA Ops:
  7.2 4.0 %shard_map.104 = bf16[32,16,640]{2,1,0:T(8,128)(2,1)} custom-call(s32[1]{0:T(128)} %bitcast.x_ref, s32[4,1,320]{2,1,0:T(1,128)} %constant.13.clone.order_ref.feat_ref, bf16[2,256,1280]{2,1,0:T(8,128)(2,1)} %bitcast.32, bf16[2,256,1280]{2,1,0:T(8,128)(2,1)} %bitcast.33), custom_call_target="tpu_custom_call" | custom-call | flops 850000000 | bytes 4000000 | tf_op jit(solution)/shard_map/pallas_call | solution.py:115
  11.2 11.1 %all-to-all-start.1 = ((bf16[32,16,640]{2,1,0:T(8,128)(2,1)}), bf16[32,16,640]{2,1,0:T(8,128)(2,1)S(1)}, u32[]{:S(2)}, u32[]{:S(2)}) async-start(bf16[32,16,640]{2,1,0:T(8,128)(2,1)} %shard_map.104), calls=%async_computation.1 | async-start | bytes 1310720 | tf_op jit(solution)/shard_map/all_to_all | solution.py:364
  22.4 1.3 shard_map.103
  23.7 18.3 %all-to-all-done.1.own_hbm = bf16[32,16,640]{2,1,0:T(8,128)(2,1)S(1)} async-done(((bf16[32,16,640]{2,1,0:T(8,128)(2,1)}), bf16[32,16,640]{2,1,0:T(8,128)(2,1)S(1)}, u32[]{:S(2)}, u32[]{:S(2)}) %all-to-all-start.1) | async-done | bytes 655392 | tf_op jit(solution)/shard_map/all_to_all | solution.py:364
  42.0 4.9 %all-to-all-start = ((bf16[32,24,640]{2,1,0:T(8,128)(2,1)}), bf16[32,24,640]{2,1,0:T(8,128)(2,1)S(1)}, u32[]{:S(2)}, u32[]{:S(2)}) async-start(bf16[32,24,640]{2,1,0:T(8,128)(2,1)} %shard_map.103), calls=%async_computation | async-start | bytes 1966080 | tf_op jit(solution)/shard_map/all_to_all | solution.py:371
  46.9 2.6 %collective-permute-start.1 = (bf16[32,16,640]{2,1,0:T(8,128)(2,1)S(1)}, bf16[32,16,640]{2,1,0:T(8,128)(2,1)S(1)}, u32[]{:S(2)}, u32[]{:S(2)}) collective-permute-start(bf16[32,16,640]{2,1,0:T(8,128)(2,1)S(1)} %all-to-all-done.1.own_hbm), channel_id=1, source_target_pairs={{0,3},{1,0},{2,1},{3,2},{4,7},{5,4},{6,5},{7,6},{8,11},{9,8},{10,9... | collective-permute-start | bytes 1966088 | tf_op jit(solution)/shard_map/ppermute | solution.py:354
  49.5 13.8 %collective-permute-done.1.right_hbm = bf16[32,16,640]{2,1,0:T(8,128)(2,1)S(1)} collective-permute-done((bf16[32,16,640]{2,1,0:T(8,128)(2,1)S(1)}, bf16[32,16,640]{2,1,0:T(8,128)(2,1)S(1)}, u32[]{:S(2)}, u32[]{:S(2)}) %collective-permute-start.1) | collective-permute-done | bytes 655392 | tf_op jit(solution)/shard_map/ppermute | solution.py:354
  63.3 0.8 slice.9
  64.0 3.4 %collective-permute-start.3 = (bf16[16,16,640]{2,1,0:T(8,128)(2,1)}, bf16[16,16,640]{2,1,0:T(8,128)(2,1)S(1)}, u32[]{:S(2)}, u32[]{:S(2)}) collective-permute-start(bf16[16,16,640]{2,1,0:T(8,128)(2,1)} %slice.9), channel_id=1, source_target_pairs={{0,3},{1,0},{2,1},{3,2},{4,7},{5,4},{6,5},{7,6},{8,11},{9,8},{10,9... | collective-permute-start | bytes 983048 | tf_op jit(solution)/shard_map/ppermute | solution.py:354
  67.4 0.8 slice.8
  68.2 1.1 copy-done.2
  69.3 1.9 %shard_map.105.wout_ref = bf16[4,320,320]{2,1,0:T(8,128)(2,1)S(1)} custom-call(s32[4,1,320]{2,1,0:T(1,128)S(1)} %copy-done, bf16[320,1280]{1,0:T(8,128)(2,1)S(1)} %copy-done.2), custom_call_target="tpu_custom_call" | custom-call | flops 1000000000 | bytes 4000000 | tf_op jit(solution)/shard_map/pallas_call | solution.py:372
  71.2 1.0 copy-done.6
  72.3 1.4 all-to-all-done.qkv_ref
  73.7 3.8 %collective-permute-done.2.low_hbm = bf16[16,16,640]{2,1,0:T(8,128)(2,1)} collective-permute-done((bf16[16,16,640]{2,1,0:T(8,128)(2,1)}, bf16[16,16,640]{2,1,0:T(8,128)(2,1)}, u32[]{:S(2)}, u32[]{:S(2)}) %collective-permute-start.2) | collective-permute-done | bytes 327712 | tf_op jit(solution)/shard_map/ppermute | solution.py:354
  77.5 1.7 %copy-done.1 = bf16[3,1280,320]{1,2,0:T(8,128)(2,1)S(1)} copy-done((bf16[3,1280,320]{1,2,0:T(8,128)(2,1)S(1)}, bf16[3,1280,320]{1,2,0:T(8,128)(2,1)}, u32[]{:S(2)}) %copy-start.1) | copy-done | bytes 2457624
  79.2 1.2 copy-done.7
  80.4 11.0 %shard_map.106 = (bf16[512,1280]{1,0:T(8,128)(2,1)S(1)}, bf16[256,640]{1,0:T(8,128)(2,1)S(1)}, bf16[256,640]{1,0:T(8,128)(2,1)}, bf16[256,640]{1,0:T(8,128)(2,1)}, bf16[256,640]{1,0:T(8,128)(2,1)}) custom-call(s32[1]{0:T(128)} %bitcast.x_ref, bf16[32,24,640]{2,1,0:T(8,128)(2,1)S(1)} %all-to-all-done.qkv_ref, ...), custom_call_target="tpu_custom_call" | custom-call | flops 5000000000 | bytes 4000000 | tf_op jit(solution)/shard_map/pallas_call | solution.py:249
  92.1 2.9 %shard_map.109 = bf16[640,1280]{1,0:T(8,128)(2,1)S(1)} custom-call(s32[2]{0:T(128)S(1)} %pad_add_fusion.1.place_ref, bf16[32,16,640]{2,1,0:T(8,128)(2,1)S(1)} %all-to-all-done.1.own_hbm, bf16[32,16,640]{2,1,0:T(8,128)(2,1)S(1)} %collective-permute-done.left_hbm, bf16[32,16,640]{2,1,0:T(8,128)(2,1)S(1)} %collective-permute-done.1.right_hbm, ...), custom_call_target="tpu_custom_call" | custom-call | flops 4000000000 | bytes 4000000 | tf_op jit(solution)/shard_map/pallas_call | solution.py:305
  95.0 3.0 %collective-permute-start.10 = (bf16[640,1280]{1,0:T(8,128)(2,1)S(1)}, bf16[640,1280]{1,0:T(8,128)(2,1)S(1)}, u32[]{:S(2)}, u32[]{:S(2)}) collective-permute-start(bf16[640,1280]{1,0:T(8,128)(2,1)S(1)} %shard_map.109), channel_id=1, source_target_pairs={{0,4},{4,0},{1,5},{5,1},{2,6},{6,2},{3,7},{7,3},{8,12},{12,8},{9,1... | collective-permute-start | bytes 4915208 | tf_op jit(solution)/shard_map/ppermute | solution.py:377
  98.4 2.6 %collective-permute-start.6 = (bf16[256,640]{1,0:T(8,128)(2,1)}, bf16[256,640]{1,0:T(8,128)(2,1)S(1)}, u32[]{:S(2)}, u32[]{:S(2)}) collective-permute-start(bf16[256,640]{1,0:T(8,128)(2,1)} %get-tuple-element.13), channel_id=1, source_target_pairs={{0,3},{1,0},{2,1},{3,2},{4,7},{5,4},{6,5},{7,6},{8,11},{9,8},{10,9... | collective-permute-start | bytes 983048 | tf_op jit(solution)/shard_map/ppermute | solution.py:354
  101.1 4.2 %shard_map.110 = bf16[640,1280]{1,0:T(8,128)(2,1)} custom-call(s32[2]{0:T(128)S(1)} %pad_add_fusion.place_ref, bf16[32,16,640]{2,1,0:T(8,128)(2,1)S(1)} %all-to-all-done.1.own_hbm, bf16[32,16,640]{2,1,0:T(8,128)(2,1)S(1)} %collective-permute-done.left_hbm, bf16[32,16,640]{2,1,0:T(8,128)(2,1)S(1)} %collective-permute-done.1.right_hbm, ...), custom_call_target="tpu_custom_call" | custom-call | flops 4000000000 | bytes 4000000 | tf_op jit(solution)/shard_map/pallas_call | solution.py:305
  105.3 10.7 %collective-permute-done.4.refs_1_ = bf16[256,640]{1,0:T(8,128)(2,1)S(1)} collective-permute-done((bf16[256,640]{1,0:T(8,128)(2,1)}, bf16[256,640]{1,0:T(8,128)(2,1)S(1)}, u32[]{:S(2)}, u32[]{:S(2)}) %collective-permute-start.4) | collective-permute-done | bytes 327712 | tf_op jit(solution)/shard_map/ppermute | solution.py:354
  116.5 21.7 %all_to_all.20 = bf16[32,8,640]{2,1,0:T(8,128)(2,1)S(1)} all-to-all(bf16[32,8,640]{2,1,0:T(8,128)(2,1)S(1)} %bitcast.27), channel_id=1, replica_groups=mesh['dp'=2,'z'=8,'yl'=2,'core'=2,'x'=4] {'z','yl','core'}, dimensions={0} | all-to-all | bytes 655360 | tf_op jit(solution)/shard_map/all_to_all | solution.py:382
  138.3 2.1 %collective-permute-start.9 = (bf16[256,640]{1,0:T(8,128)(2,1)S(1)}, bf16[256,640]{1,0:T(8,128)(2,1)S(1)}, u32[]{:S(2)}, u32[]{:S(2)}) collective-permute-start(bf16[256,640]{1,0:T(8,128)(2,1)S(1)} %bitcast.23), channel_id=1, source_target_pairs={{0,3},{1,0},{2,1},{3,2},{4,7},{5,4},{6,5},{7,6},{8,11},{9,8},{10,9... | collective-permute-start | bytes 983048 | tf_op jit(solution)/shard_map/ppermute | solution.py:354
  140.9 1.8 %shard_map.111 = bf16[8,20,1280]{2,1,0:T(8,128)(2,1)} custom-call(bf16[160,1280]{1,0:T(8,128)(2,1)} %bitcast.34), custom_call_target="tpu_custom_call" | custom-call | bytes 4000000 | tf_op jit(solution)/shard_map/pallas_call | solution.py:391
  142.7 3.5 %all-to-all-start.3 = ((bf16[8,20,1280]{2,1,0:T(8,128)(2,1)}), bf16[8,20,1280]{2,1,0:T(8,128)(2,1)S(1)}, u32[]{:S(2)}, u32[]{:S(2)}) async-start(bf16[8,20,1280]{2,1,0:T(8,128)(2,1)} %shard_map.111), calls=%async_computation.4 | async-start | bytes 983040 | tf_op jit(solution)/shard_map/all_to_all | solution.py:392
  146.4 3.1 %collective-permute-done.8.refs_2_ = bf16[256,640]{1,0:T(8,128)(2,1)S(1)} collective-permute-done((bf16[256,640]{1,0:T(8,128)(2,1)S(1)}, bf16[256,640]{1,0:T(8,128)(2,1)S(1)}, u32[]{:S(2)}, u32[]{:S(2)}) %collective-permute-start.8) | collective-permute-done | bytes 327712 | tf_op jit(solution)/shard_map/ppermute | solution.py:354
  149.6 8.3 %collective-permute-done.7.refs_1_ = bf16[256,640]{1,0:T(8,128)(2,1)S(1)} collective-permute-done((bf16[256,640]{1,0:T(8,128)(2,1)S(1)}, bf16[256,640]{1,0:T(8,128)(2,1)S(1)}, u32[]{:S(2)}, u32[]{:S(2)}) %collective-permute-start.7) | collective-permute-done | bytes 327712 | tf_op jit(solution)/shard_map/ppermute | solution.py:354
  157.8 1.7 %shard_map.108 = bf16[2,256,1280]{2,1,0:T(8,128)(2,1)} custom-call(s32[1]{0:T(128)} %bitcast.x_ref, bf16[256,640]{1,0:T(8,128)(2,1)S(1)} %bitcast.26, bf16[256,640]{1,0:T(8,128)(2,1)S(1)} %collective-permute-done.7.refs_1_, bf16[256,640]{1,0:T(8,128)(2,1)S(1)} %collective-permute-done.8.refs_2_, bf16[256,640]{1,0:T(8,128)(2,1)S(1)} %collective-permute-done.9.refs_3_), custom_call_target="tpu_custom_call" | custom-call | flops 40000000000 | bytes 4000000 | tf_op jit(solution)/shard_map/pallas_call | solution.py:384
  159.6 1.8 %all-to-all-done.3.in_ref = bf16[8,20,1280]{2,1,0:T(8,128)(2,1)S(1)} async-done(((bf16[8,20,1280]{2,1,0:T(8,128)(2,1)}), bf16[8,20,1280]{2,1,0:T(8,128)(2,1)S(1)}, u32[]{:S(2)}, u32[]{:S(2)}) %all-to-all-start.3) | async-done | bytes 409632 | tf_op jit(solution)/shard_map/all_to_all | solution.py:392
  161.3 0.8 shard_map.112
  (34 shorter events, 2.7 us)
Async XLA Ops:
  7.2 15.2 %copy-start.3 = (bf16[1,2,256,320]{2,3,1,0:T(8,128)(2,1)S(1)}, bf16[1,2,256,320]{2,3,1,0:T(8,128)(2,1)}, u32[]{:S(2)}) copy-start(bf16[1,2,256,320]{2,3,1,0:T(8,128)(2,1)} %param.8) | copy-start | bytes 983044
  7.2 15.2 %copy-start.4 = (bf16[1,2,256,320]{2,3,1,0:T(8,128)(2,1)S(1)}, bf16[1,2,256,320]{2,3,1,0:T(8,128)(2,1)}, u32[]{:S(2)}) copy-start(bf16[1,2,256,320]{2,3,1,0:T(8,128)(2,1)} %param.9) | copy-start | bytes 983044
  7.2 15.2 %copy-start.5 = (bf16[1,2,256,320]{2,3,1,0:T(8,128)(2,1)S(1)}, bf16[1,2,256,320]{2,3,1,0:T(8,128)(2,1)}, u32[]{:S(2)}) copy-start(bf16[1,2,256,320]{2,3,1,0:T(8,128)(2,1)} %param.10) | copy-start | bytes 983044
  11.2 30.8 %all-to-all-start.1 = ((bf16[32,16,640]{2,1,0:T(8,128)(2,1)}), bf16[32,16,640]{2,1,0:T(8,128)(2,1)S(1)}, u32[]{:S(2)}, u32[]{:S(2)}) async-start(bf16[32,16,640]{2,1,0:T(8,128)(2,1)} %shard_map.104), calls=%async_computation.1 | async-start | bytes 1310720 | tf_op jit(solution)/shard_map/all_to_all | solution.py:364
  23.7 44.5 %copy-start = (s32[4,1,320]{2,1,0:T(1,128)S(1)}, s32[4,1,320]{2,1,0:T(1,128)}, u32[]{:S(2)}) copy-start(s32[4,1,320]{2,1,0:T(1,128)} %constant.13.clone.order_ref.feat_ref) | copy-start | bytes 15364
  42.0 31.7 %all-to-all-start = ((bf16[32,24,640]{2,1,0:T(8,128)(2,1)}), bf16[32,24,640]{2,1,0:T(8,128)(2,1)S(1)}, u32[]{:S(2)}, u32[]{:S(2)}) async-start(bf16[32,24,640]{2,1,0:T(8,128)(2,1)} %shard_map.103), calls=%async_computation | async-start | bytes 1966080 | tf_op jit(solution)/shard_map/all_to_all | solution.py:371
  46.9 94.0 %reduce-scatter.2.cloned.1.call-start = ((), (), s32[]{:S(2)}) async-start(), calls=%async_computation.5 | async-start | bytes 2048000 | tf_op jit(solution)/shard_map/reduce_scatter | solution.py:379
  46.9 16.3 %collective-permute-start.1 = (bf16[32,16,640]{2,1,0:T(8,128)(2,1)S(1)}, bf16[32,16,640]{2,1,0:T(8,128)(2,1)S(1)}, u32[]{:S(2)}, u32[]{:S(2)}) collective-permute-start(bf16[32,16,640]{2,1,0:T(8,128)(2,1)S(1)} %all-to-all-done.1.own_hbm), channel_id=1, source_target_pairs={{0,3},{1,0},{2,1},{3,2},{4,7},{5,4},{6,5},{7,6},{8,11},{9,8},{10,9... | collective-permute-start | bytes 1966088 | tf_op jit(solution)/shard_map/ppermute | solution.py:354
  49.5 17.9 %collective-permute-start = (bf16[32,16,640]{2,1,0:T(8,128)(2,1)S(1)}, bf16[32,16,640]{2,1,0:T(8,128)(2,1)S(1)}, u32[]{:S(2)}, u32[]{:S(2)}) collective-permute-start(bf16[32,16,640]{2,1,0:T(8,128)(2,1)S(1)} %all-to-all-done.1.own_hbm), channel_id=1, source_target_pairs={{0,1},{1,2},{2,3},{3,0},{4,5},{5,6},{6,7},{7,4},{8,9},{9,10},{10,1... | collective-permute-start | bytes 1966088 | tf_op jit(solution)/shard_map/ppermute | solution.py:354
  64.0 9.7 %collective-permute-start.3 = (bf16[16,16,640]{2,1,0:T(8,128)(2,1)}, bf16[16,16,640]{2,1,0:T(8,128)(2,1)S(1)}, u32[]{:S(2)}, u32[]{:S(2)}) collective-permute-start(bf16[16,16,640]{2,1,0:T(8,128)(2,1)} %slice.9), channel_id=1, source_target_pairs={{0,3},{1,0},{2,1},{3,2},{4,7},{5,4},{6,5},{7,6},{8,11},{9,8},{10,9... | collective-permute-start | bytes 983048 | tf_op jit(solution)/shard_map/ppermute | solution.py:354
  68.2 9.3 %collective-permute-start.2 = (bf16[16,16,640]{2,1,0:T(8,128)(2,1)}, bf16[16,16,640]{2,1,0:T(8,128)(2,1)}, u32[]{:S(2)}, u32[]{:S(2)}) collective-permute-start(bf16[16,16,640]{2,1,0:T(8,128)(2,1)} %slice.8), channel_id=1, source_target_pairs={{0,1},{1,2},{2,3},{3,0},{4,5},{5,6},{6,7},{7,4},{8,9},{9,10},{10,1... | collective-permute-start | bytes 983048 | tf_op jit(solution)/shard_map/ppermute | solution.py:354
  68.2 1.1 copy-start.2
  71.2 1.0 copy-start.6
  77.5 1.7 %copy-start.1 = (bf16[3,1280,320]{1,2,0:T(8,128)(2,1)S(1)}, bf16[3,1280,320]{1,2,0:T(8,128)(2,1)}, u32[]{:S(2)}) copy-start(bf16[3,1280,320]{1,2,0:T(8,128)(2,1)} %param.13) | copy-start | bytes 7372804
  79.2 1.2 copy-start.7
  91.4 0.7 copy-start.8
  95.0 6.1 %collective-permute-start.10 = (bf16[640,1280]{1,0:T(8,128)(2,1)S(1)}, bf16[640,1280]{1,0:T(8,128)(2,1)S(1)}, u32[]{:S(2)}, u32[]{:S(2)}) collective-permute-start(bf16[640,1280]{1,0:T(8,128)(2,1)S(1)} %shard_map.109), channel_id=1, source_target_pairs={{0,4},{4,0},{1,5},{5,1},{2,6},{6,2},{3,7},{7,3},{8,12},{12,8},{9,1... | collective-permute-start | bytes 4915208 | tf_op jit(solution)/shard_map/ppermute | solution.py:377
  98.1 18.0 %collective-permute-start.4 = (bf16[256,640]{1,0:T(8,128)(2,1)}, bf16[256,640]{1,0:T(8,128)(2,1)S(1)}, u32[]{:S(2)}, u32[]{:S(2)}) collective-permute-start(bf16[256,640]{1,0:T(8,128)(2,1)} %get-tuple-element.11), channel_id=1, source_target_pairs={{0,1},{1,2},{2,3},{3,0},{4,5},{5,6},{6,7},{7,4},{8,9},{9,10},{10,1... | collective-permute-start | bytes 983048 | tf_op jit(solution)/shard_map/ppermute | solution.py:354
  98.3 17.7 %collective-permute-start.5 = (bf16[256,640]{1,0:T(8,128)(2,1)}, bf16[256,640]{1,0:T(8,128)(2,1)S(1)}, u32[]{:S(2)}, u32[]{:S(2)}) collective-permute-start(bf16[256,640]{1,0:T(8,128)(2,1)} %get-tuple-element.12), channel_id=1, source_target_pairs={{0,2},{1,3},{2,0},{3,1},{4,6},{5,7},{6,4},{7,5},{8,10},{9,11},{10,... | collective-permute-start | bytes 983048 | tf_op jit(solution)/shard_map/ppermute | solution.py:354
  98.4 17.9 %collective-permute-start.6 = (bf16[256,640]{1,0:T(8,128)(2,1)}, bf16[256,640]{1,0:T(8,128)(2,1)S(1)}, u32[]{:S(2)}, u32[]{:S(2)}) collective-permute-start(bf16[256,640]{1,0:T(8,128)(2,1)} %get-tuple-element.13), channel_id=1, source_target_pairs={{0,3},{1,0},{2,1},{3,2},{4,7},{5,4},{6,5},{7,6},{8,11},{9,8},{10,9... | collective-permute-start | bytes 983048 | tf_op jit(solution)/shard_map/ppermute | solution.py:354
  105.3 11.1 %copy-start.9 = (bf16[256,640]{1,0:T(8,128)(2,1)S(1)}, bf16[256,640]{1,0:T(8,128)(2,1)}, u32[]{:S(2)}) copy-start(bf16[256,640]{1,0:T(8,128)(2,1)} %copy-done.8) | copy-start | bytes 983044
  138.3 8.2 %collective-permute-start.9 = (bf16[256,640]{1,0:T(8,128)(2,1)S(1)}, bf16[256,640]{1,0:T(8,128)(2,1)S(1)}, u32[]{:S(2)}, u32[]{:S(2)}) collective-permute-start(bf16[256,640]{1,0:T(8,128)(2,1)S(1)} %bitcast.23), channel_id=1, source_target_pairs={{0,3},{1,0},{2,1},{3,2},{4,7},{5,4},{6,5},{7,6},{8,11},{9,8},{10,9... | collective-permute-start | bytes 983048 | tf_op jit(solution)/shard_map/ppermute | solution.py:354
  140.3 9.2 %collective-permute-start.8 = (bf16[256,640]{1,0:T(8,128)(2,1)S(1)}, bf16[256,640]{1,0:T(8,128)(2,1)S(1)}, u32[]{:S(2)}, u32[]{:S(2)}) collective-permute-start(bf16[256,640]{1,0:T(8,128)(2,1)S(1)} %bitcast.24), channel_id=1, source_target_pairs={{0,2},{1,3},{2,0},{3,1},{4,6},{5,7},{6,4},{7,5},{8,10},{9,11},{10,... | collective-permute-start | bytes 983048 | tf_op jit(solution)/shard_map/ppermute | solution.py:354
  140.3 17.5 %collective-permute-start.7 = (bf16[256,640]{1,0:T(8,128)(2,1)S(1)}, bf16[256,640]{1,0:T(8,128)(2,1)S(1)}, u32[]{:S(2)}, u32[]{:S(2)}) collective-permute-start(bf16[256,640]{1,0:T(8,128)(2,1)S(1)} %bitcast.25), channel_id=1, source_target_pairs={{0,1},{1,2},{2,3},{3,0},{4,5},{5,6},{6,7},{7,4},{8,9},{9,10},{10,1... | collective-permute-start | bytes 983048 | tf_op jit(solution)/shard_map/ppermute | solution.py:354
  142.7 18.6 %all-to-all-start.3 = ((bf16[8,20,1280]{2,1,0:T(8,128)(2,1)}), bf16[8,20,1280]{2,1,0:T(8,128)(2,1)S(1)}, u32[]{:S(2)}, u32[]{:S(2)}) async-start(bf16[8,20,1280]{2,1,0:T(8,128)(2,1)} %shard_map.111), calls=%async_computation.4 | async-start | bytes 983040 | tf_op jit(solution)/shard_map/all_to_all | solution.py:392
Sparse Core Ops, SparseCore 0:
  105.4 30.9 reduce-scatter.1

commit v6 on v4

--- a/solution.py
+++ b/solution.py
@@ -281,7 +281,7 @@
         out_specs=block,
     )
     shape = jax.ShapeDtypeStruct((2 * W, 4 * W), BF)
-    return call(weight_kernel, shape, 4_000_000_000, spec)(half, gon, grads, *got)
+    return call(weight_kernel, shape, 4_000_000_000, spec, 20 * 1024 * 1024)(half, gon, grads, *got)
 
 
 def add_kernel(*refs):

time: 164 us -> 164 us (level)
  transfers between devices with their start and end apart: 11 -> 11, of which waited for: 9 -> 9; matrix products, arithmetic and copies ran while one was open for 0% -> 0% of each run, Pallas kernels for 7% -> 6%
where the time goes in v6:
time: 164 us; the launch traced here: 161 us
  blocking collectives  52.9 us (32%)
  waiting for transfers between devices  51.5 us (31%)
  Pallas kernels  26.5 us (16%)
  starting transfers between devices  16.1 us (10%)
  between operations  14.2 us (9%)
    all_to_all x1, blocking collectives, on_device(): gon = lax.all_to_all(gon, TM, 0, 0, tiled=True)  31 us
    all_to_all x1, waiting for transfers between devices, on_device(): qkv = lax.all_to_all(qkv, TM, 0, 0, tiled=True)  24.7 us
    ppermute x6, waiting for transfers between devices, shift(): return lax.ppermute(array, 'x', [(i, (i + k) % NX) for i in range(NX)])  23.8 us
    all_to_all x1, blocking collectives, on_device(): lax.all_to_all(own_norm.reshape(NT, PT, 2 * W), TM, 0, 0, tiled=True)  21.9 us
    pallas_call x1, Pallas kernels, attend(): call(attend_kernel, (jax.ShapeDtypeStruct((TOK, 4 * W), BF),) + (jax.Shap...  10.7 us
    ppermute x6, starting transfers between devices, shift(): return lax.ppermute(array, 'x', [(i, (i + k) % NX) for i in range(NX)])  6.59 us
    all_to_all x1, starting transfers between devices, on_device(): qkv = lax.all_to_all(qkv, TM, 0, 0, tiled=True)  5.06 us
    pallas_call x2, Pallas kernels, weight_half(): call(weight_kernel, shape, 4000000000, spec, 20 * 1024 * 1024)  4.3 us
  transfers between devices with their start and end apart: 11, of which 9 were waited for; matrix products, arithmetic and copies ran while one was open for 0% of the time, Pallas kernels for 6%

profile of v6, /device:TPU:1, one launch (start us, length us, event | category | flops | bytes accessed | tf_op | source)
XLA Modules:
  0.0 161.2 jit_solution(2095245207729869150)
XLA Ops:
  7.2 0.0 all-gather.3.cloned.1.call-start
  7.2 3.9 %shard_map.104 = bf16[32,16,640]{2,1,0:T(8,128)(2,1)} custom-call(s32[1]{0:T(128)} %bitcast.x_ref, s32[4,1,320]{2,1,0:T(1,128)} %constant.13.clone.order_ref.feat_ref, bf16[2,256,1280]{2,1,0:T(8,128)(2,1)} %bitcast.35, bf16[2,256,1280]{2,1,0:T(8,128)(2,1)} %bitcast.36), custom_call_target="tpu_custom_call" | custom-call | flops 850000000 | bytes 4000000 | tf_op jit(solution)/shard_map/pallas_call | solution.py:115
  11.2 31.0 %all_to_all.20 = bf16[32,16,640]{2,1,0:T(8,128)(2,1)} all-to-all(bf16[32,16,640]{2,1,0:T(8,128)(2,1)} %shard_map.104), channel_id=1, replica_groups=mesh['dp'=2,'z'=8,'yl'=2,'core'=2,'x'=4] {'z','yl','core'}, dimensions={0} | all-to-all | bytes 1310720 | tf_op jit(solution)/shard_map/all_to_all | solution.py:331
  42.2 1.3 shard_map.103
  43.5 5.1 %all-to-all-start = ((bf16[32,24,640]{2,1,0:T(8,128)(2,1)}), bf16[32,24,640]{2,1,0:T(8,128)(2,1)S(1)}, u32[]{:S(2)}, u32[]{:S(2)}) async-start(bf16[32,24,640]{2,1,0:T(8,128)(2,1)} %shard_map.103), calls=%async_computation | async-start | bytes 1966080 | tf_op jit(solution)/shard_map/all_to_all | solution.py:336
  48.6 0.2 reduce-scatter.2.cloned.1.call-start
  48.8 1.9 %shard_map.105.wout_ref = bf16[4,320,320]{2,1,0:T(8,128)(2,1)S(1)} custom-call(s32[4,1,320]{2,1,0:T(1,128)S(1)} %copy-done, bf16[320,1280]{1,0:T(8,128)(2,1)S(1)} %copy-done.2), custom_call_target="tpu_custom_call" | custom-call | flops 1000000000 | bytes 4000000 | tf_op jit(solution)/shard_map/pallas_call | solution.py:337
  50.7 24.7 %all-to-all-done.qkv_ref = bf16[32,24,640]{2,1,0:T(8,128)(2,1)S(1)} async-done(((bf16[32,24,640]{2,1,0:T(8,128)(2,1)}), bf16[32,24,640]{2,1,0:T(8,128)(2,1)S(1)}, u32[]{:S(2)}, u32[]{:S(2)}) %all-to-all-start) | async-done | bytes 983072 | tf_op jit(solution)/shard_map/all_to_all | solution.py:336
  75.4 1.9 %all-gather.3.cloned.1.call-done = bf16[128,16,640]{2,1,0:T(8,128)(2,1)} async-done(((bf16[32,16,640]{2,1,0:T(8,128)(2,1)}), bf16[128,16,640]{2,1,0:T(8,128)(2,1)}) %all-gather.3.cloned.1.call-update) | async-done | bytes 2621456 | tf_op jit(solution)/shard_map/all_gather | solution.py:332
  77.3 10.7 %shard_map.106 = (bf16[512,1280]{1,0:T(8,128)(2,1)S(1)}, bf16[256,640]{1,0:T(8,128)(2,1)S(1)}, bf16[256,640]{1,0:T(8,128)(2,1)S(1)}, bf16[256,640]{1,0:T(8,128)(2,1)S(1)}, bf16[256,640]{1,0:T(8,128)(2,1)S(1)}) custom-call(s32[1]{0:T(128)} %bitcast.x_ref, bf16[32,24,640]{2,1,0:T(8,128)(2,1)S(1)} %all-to-all-done.qkv_ref, bf16[4,32,16,640]{3,2,1,0:T(8,128)(2,1)} %bitcast.29, ...), custom_call_target="tpu_custom_call" | custom-call | flops 5000000000 | bytes 4000000 | tf_op jit(solution)/shard_map/pallas_call | solution.py:241
  88.0 1.7 %shard_map.109 = bf16[640,1280]{1,0:T(8,128)(2,1)S(1)} custom-call(s32[1]{0:T(128)} %bitcast.16.half_ref, bf16[4,32,16,640]{3,2,1,0:T(8,128)(2,1)S(1)} %bitcast.30, bf16[512,1280]{1,0:T(8,128)(2,1)S(1)} %get-tuple-element.14.grads_ref), custom_call_target="tpu_custom_call" | custom-call | flops 4000000000 | bytes 4000000 | tf_op jit(solution)/shard_map/pallas_call | solution.py:284
  89.7 0.8 collective-permute-start.6
  90.5 0.4 collective-permute-start
  90.8 2.1 %collective-permute-start.1 = (bf16[256,640]{1,0:T(8,128)(2,1)S(1)}, bf16[256,640]{1,0:T(8,128)(2,1)S(1)}, u32[]{:S(2)}, u32[]{:S(2)}) collective-permute-start(bf16[256,640]{1,0:T(8,128)(2,1)S(1)} %get-tuple-element.12), channel_id=1, source_target_pairs={{0,2},{1,3},{2,0},{3,1},{4,6},{5,7},{6,4},{7,5},{8,10},{9,11},{10,... | collective-permute-start | bytes 983048 | tf_op jit(solution)/shard_map/ppermute | solution.py:321
  93.0 1.2 collective-permute-start.2
  94.1 2.6 %shard_map.110 = bf16[640,1280]{1,0:T(8,128)(2,1)} custom-call(s32[1]{0:T(128)} %bitcast.15.half_ref, bf16[4,32,16,640]{3,2,1,0:T(8,128)(2,1)S(1)} %bitcast.31, bf16[512,1280]{1,0:T(8,128)(2,1)S(1)} %get-tuple-element.14.grads_ref, bf16[640,1280]{1,0:T(8,128)(2,1)S(1)} %collective-permute-done.6.refs_0_), custom_call_target="tpu_custom_call" | custom-call | flops 4000000000 | bytes 4000000 | tf_op jit(solution)/shard_map/pallas_call | solution.py:284
  96.8 4.4 %collective-permute-done.refs_1_ = bf16[256,640]{1,0:T(8,128)(2,1)S(1)} collective-permute-done((bf16[256,640]{1,0:T(8,128)(2,1)S(1)}, bf16[256,640]{1,0:T(8,128)(2,1)S(1)}, u32[]{:S(2)}, u32[]{:S(2)}) %collective-permute-start) | collective-permute-done | bytes 327712 | tf_op jit(solution)/shard_map/ppermute | solution.py:321
  101.1 6.7 %collective-permute-done.1.refs_2_ = bf16[256,640]{1,0:T(8,128)(2,1)S(1)} collective-permute-done((bf16[256,640]{1,0:T(8,128)(2,1)S(1)}, bf16[256,640]{1,0:T(8,128)(2,1)S(1)}, u32[]{:S(2)}, u32[]{:S(2)}) %collective-permute-start.1) | collective-permute-done | bytes 327712 | tf_op jit(solution)/shard_map/ppermute | solution.py:321
  107.8 0.5 collective-permute-done.2.refs_3_
  108.3 0.2 shard_map.107
  108.4 21.9 %all_to_all.21 = bf16[32,8,640]{2,1,0:T(8,128)(2,1)S(1)} all-to-all(bf16[32,8,640]{2,1,0:T(8,128)(2,1)S(1)} %bitcast.28), channel_id=1, replica_groups=mesh['dp'=2,'z'=8,'yl'=2,'core'=2,'x'=4] {'z','yl','core'}, dimensions={0} | all-to-all | bytes 655360 | tf_op jit(solution)/shard_map/all_to_all | solution.py:347
  130.3 2.4 %collective-permute-start.5 = (bf16[256,640]{1,0:T(8,128)(2,1)S(1)}, bf16[256,640]{1,0:T(8,128)(2,1)S(1)}, u32[]{:S(2)}, u32[]{:S(2)}) collective-permute-start(bf16[256,640]{1,0:T(8,128)(2,1)S(1)} %bitcast.24), channel_id=1, source_target_pairs={{0,3},{1,0},{2,1},{3,2},{4,7},{5,4},{6,5},{7,6},{8,11},{9,8},{10,9... | collective-permute-start | bytes 983048 | tf_op jit(solution)/shard_map/ppermute | solution.py:321
  132.6 0.4 collective-permute-start.4
  133.0 0.2 collective-permute-start.3
  133.2 1.8 %shard_map.111 = bf16[8,20,1280]{2,1,0:T(8,128)(2,1)} custom-call(bf16[160,1280]{1,0:T(8,128)(2,1)} %bitcast.37), custom_call_target="tpu_custom_call" | custom-call | bytes 4000000 | tf_op jit(solution)/shard_map/pallas_call | solution.py:356
  135.0 3.5 %all-to-all-start.3 = ((bf16[8,20,1280]{2,1,0:T(8,128)(2,1)}), bf16[8,20,1280]{2,1,0:T(8,128)(2,1)S(1)}, u32[]{:S(2)}, u32[]{:S(2)}) async-start(bf16[8,20,1280]{2,1,0:T(8,128)(2,1)} %shard_map.111), calls=%async_computation.4 | async-start | bytes 983040 | tf_op jit(solution)/shard_map/all_to_all | solution.py:357
  138.5 0.5 collective-permute-done.5.refs_3_
  139.0 2.8 %collective-permute-done.4.refs_2_ = bf16[256,640]{1,0:T(8,128)(2,1)S(1)} collective-permute-done((bf16[256,640]{1,0:T(8,128)(2,1)S(1)}, bf16[256,640]{1,0:T(8,128)(2,1)S(1)}, u32[]{:S(2)}, u32[]{:S(2)}) %collective-permute-start.4) | collective-permute-done | bytes 327712 | tf_op jit(solution)/shard_map/ppermute | solution.py:321
  141.9 8.9 %collective-permute-done.3.refs_1_ = bf16[256,640]{1,0:T(8,128)(2,1)S(1)} collective-permute-done((bf16[256,640]{1,0:T(8,128)(2,1)S(1)}, bf16[256,640]{1,0:T(8,128)(2,1)S(1)}, u32[]{:S(2)}, u32[]{:S(2)}) %collective-permute-start.3) | collective-permute-done | bytes 327712 | tf_op jit(solution)/shard_map/ppermute | solution.py:321
  150.8 1.7 %shard_map.108 = bf16[2,256,1280]{2,1,0:T(8,128)(2,1)} custom-call(s32[1]{0:T(128)} %bitcast.x_ref, bf16[256,640]{1,0:T(8,128)(2,1)S(1)} %bitcast.27, bf16[256,640]{1,0:T(8,128)(2,1)S(1)} %collective-permute-done.3.refs_1_, bf16[256,640]{1,0:T(8,128)(2,1)S(1)} %collective-permute-done.4.refs_2_, bf16[256,640]{1,0:T(8,128)(2,1)S(1)} %collective-permute-done.5.refs_3_), custom_call_target="tpu_custom_call" | custom-call | flops 40000000000 | bytes 4000000 | tf_op jit(solution)/shard_map/pallas_call | solution.py:349
  152.5 1.1 all-to-all-done.3.in_ref
  153.7 0.8 shard_map.112
  (16 shorter events, 0.1 us)
Async XLA Ops:
  7.2 70.1 %all-gather.3.cloned.1.call-start = ((), (), s32[]{:S(2)}) async-start(), calls=%async_computation.6 | async-start | bytes 3276800 | tf_op jit(solution)/shard_map/all_gather | solution.py:332
  11.1 31.1 %copy-start.3 = (bf16[1,2,256,320]{2,3,1,0:T(8,128)(2,1)S(1)}, bf16[1,2,256,320]{2,3,1,0:T(8,128)(2,1)}, u32[]{:S(2)}) copy-start(bf16[1,2,256,320]{2,3,1,0:T(8,128)(2,1)} %param.8) | copy-start | bytes 983044
  11.1 31.1 %copy-start.4 = (bf16[1,2,256,320]{2,3,1,0:T(8,128)(2,1)S(1)}, bf16[1,2,256,320]{2,3,1,0:T(8,128)(2,1)}, u32[]{:S(2)}) copy-start(bf16[1,2,256,320]{2,3,1,0:T(8,128)(2,1)} %param.9) | copy-start | bytes 983044
  11.2 31.1 %copy-start.5 = (bf16[1,2,256,320]{2,3,1,0:T(8,128)(2,1)S(1)}, bf16[1,2,256,320]{2,3,1,0:T(8,128)(2,1)}, u32[]{:S(2)}) copy-start(bf16[1,2,256,320]{2,3,1,0:T(8,128)(2,1)} %param.10) | copy-start | bytes 983044
  43.5 5.3 %copy-start = (s32[4,1,320]{2,1,0:T(1,128)S(1)}, s32[4,1,320]{2,1,0:T(1,128)}, u32[]{:S(2)}) copy-start(s32[4,1,320]{2,1,0:T(1,128)} %constant.13.clone.order_ref.feat_ref) | copy-start | bytes 15364
  43.5 5.3 %copy-start.2 = (bf16[320,1280]{1,0:T(8,128)(2,1)S(1)}, bf16[320,1280]{1,0:T(8,128)(2,1)}, u32[]{:S(2)}) copy-start(bf16[320,1280]{1,0:T(8,128)(2,1)} %w_ref.1) | copy-start | bytes 2457604
  43.5 31.9 %all-to-all-start = ((bf16[32,24,640]{2,1,0:T(8,128)(2,1)}), bf16[32,24,640]{2,1,0:T(8,128)(2,1)S(1)}, u32[]{:S(2)}, u32[]{:S(2)}) async-start(bf16[32,24,640]{2,1,0:T(8,128)(2,1)} %shard_map.103), calls=%async_computation | async-start | bytes 1966080 | tf_op jit(solution)/shard_map/all_to_all | solution.py:336
  48.6 84.7 %reduce-scatter.2.cloned.1.call-start = ((), (), s32[]{:S(2)}) async-start(), calls=%async_computation.5 | async-start | bytes 2048000 | tf_op jit(solution)/shard_map/reduce_scatter | solution.py:344
  77.3 10.7 %copy-start.1 = (bf16[128,16,640]{2,1,0:T(8,128)(2,1)S(1)}, bf16[128,16,640]{2,1,0:T(8,128)(2,1)}, u32[]{:S(2)}) copy-start(bf16[128,16,640]{2,1,0:T(8,128)(2,1)} %all-gather.3.cloned.1.call-done) | copy-start | bytes 7864324
  89.7 4.4 %collective-permute-start.6 = (bf16[640,1280]{1,0:T(8,128)(2,1)S(1)}, bf16[640,1280]{1,0:T(8,128)(2,1)S(1)}, u32[]{:S(2)}, u32[]{:S(2)}) collective-permute-start(bf16[640,1280]{1,0:T(8,128)(2,1)S(1)} %shard_map.109), channel_id=1, source_target_pairs={{0,4},{4,0},{1,5},{5,1},{2,6},{6,2},{3,7},{7,3},{8,12},{12,8},{9,1... | collective-permute-start | bytes 4915208 | tf_op jit(solution)/shard_map/ppermute | solution.py:342
  90.5 10.7 %collective-permute-start = (bf16[256,640]{1,0:T(8,128)(2,1)S(1)}, bf16[256,640]{1,0:T(8,128)(2,1)S(1)}, u32[]{:S(2)}, u32[]{:S(2)}) collective-permute-start(bf16[256,640]{1,0:T(8,128)(2,1)S(1)} %get-tuple-element.11), channel_id=1, source_target_pairs={{0,1},{1,2},{2,3},{3,0},{4,5},{5,6},{6,7},{7,4},{8,9},{9,10},{10,1... | collective-permute-start | bytes 983048 | tf_op jit(solution)/shard_map/ppermute | solution.py:321
  90.8 17.0 %collective-permute-start.1 = (bf16[256,640]{1,0:T(8,128)(2,1)S(1)}, bf16[256,640]{1,0:T(8,128)(2,1)S(1)}, u32[]{:S(2)}, u32[]{:S(2)}) collective-permute-start(bf16[256,640]{1,0:T(8,128)(2,1)S(1)} %get-tuple-element.12), channel_id=1, source_target_pairs={{0,2},{1,3},{2,0},{3,1},{4,6},{5,7},{6,4},{7,5},{8,10},{9,11},{10,... | collective-permute-start | bytes 983048 | tf_op jit(solution)/shard_map/ppermute | solution.py:321
  93.0 15.3 %collective-permute-start.2 = (bf16[256,640]{1,0:T(8,128)(2,1)S(1)}, bf16[256,640]{1,0:T(8,128)(2,1)S(1)}, u32[]{:S(2)}, u32[]{:S(2)}) collective-permute-start(bf16[256,640]{1,0:T(8,128)(2,1)S(1)} %get-tuple-element.13), channel_id=1, source_target_pairs={{0,3},{1,0},{2,1},{3,2},{4,7},{5,4},{6,5},{7,6},{8,11},{9,8},{10,9... | collective-permute-start | bytes 983048 | tf_op jit(solution)/shard_map/ppermute | solution.py:321
  130.3 8.7 %collective-permute-start.5 = (bf16[256,640]{1,0:T(8,128)(2,1)S(1)}, bf16[256,640]{1,0:T(8,128)(2,1)S(1)}, u32[]{:S(2)}, u32[]{:S(2)}) collective-permute-start(bf16[256,640]{1,0:T(8,128)(2,1)S(1)} %bitcast.24), channel_id=1, source_target_pairs={{0,3},{1,0},{2,1},{3,2},{4,7},{5,4},{6,5},{7,6},{8,11},{9,8},{10,9... | collective-permute-start | bytes 983048 | tf_op jit(solution)/shard_map/ppermute | solution.py:321
  132.6 9.2 %collective-permute-start.4 = (bf16[256,640]{1,0:T(8,128)(2,1)S(1)}, bf16[256,640]{1,0:T(8,128)(2,1)S(1)}, u32[]{:S(2)}, u32[]{:S(2)}) collective-permute-start(bf16[256,640]{1,0:T(8,128)(2,1)S(1)} %bitcast.25), channel_id=1, source_target_pairs={{0,2},{1,3},{2,0},{3,1},{4,6},{5,7},{6,4},{7,5},{8,10},{9,11},{10,... | collective-permute-start | bytes 983048 | tf_op jit(solution)/shard_map/ppermute | solution.py:321
  133.0 17.8 %collective-permute-start.3 = (bf16[256,640]{1,0:T(8,128)(2,1)S(1)}, bf16[256,640]{1,0:T(8,128)(2,1)S(1)}, u32[]{:S(2)}, u32[]{:S(2)}) collective-permute-start(bf16[256,640]{1,0:T(8,128)(2,1)S(1)} %bitcast.26), channel_id=1, source_target_pairs={{0,1},{1,2},{2,3},{3,0},{4,5},{5,6},{6,7},{7,4},{8,9},{9,10},{10,1... | collective-permute-start | bytes 983048 | tf_op jit(solution)/shard_map/ppermute | solution.py:321
  135.0 18.6 %all-to-all-start.3 = ((bf16[8,20,1280]{2,1,0:T(8,128)(2,1)}), bf16[8,20,1280]{2,1,0:T(8,128)(2,1)S(1)}, u32[]{:S(2)}, u32[]{:S(2)}) async-start(bf16[8,20,1280]{2,1,0:T(8,128)(2,1)} %shard_map.111), calls=%async_computation.4 | async-start | bytes 983040 | tf_op jit(solution)/shard_map/all_to_all | solution.py:357
Sparse Core Ops, SparseCore 0:
  42.3 34.9 all-gather.2
  96.9 28.5 reduce-scatter.1

commit v7 on v6

--- a/solution.py
+++ b/solution.py
@@ -75,7 +75,7 @@
     return jnp.where(places == feat, 1.0, 0.0).astype(BF)
 
 
-def pick_kernel(x_ref, order_ref, go_hbm, n_hbm, out_hbm, rows_s, out_s, sems, out_sems):
+def pick_kernel(x_ref, go_hbm, n_hbm, out_hbm, rows_s, out_s, sems, out_sems):
     part = NT * PT // STEPS
     first = lax.rem(x_ref[0], 2) * (D // 2)
     fetches = [
@@ -93,7 +93,11 @@
     for group in fetches:
         for fetch in group:
             fetch.start()
-    pick = one_hot(order_ref[x_ref[0]] - first, D // 2)
+    at = lax.broadcasted_iota(jnp.int32, (1, W), 1)
+    low = (at >= W // 2).astype(jnp.int32)
+    z = sum((at - low * (W // 2) >= 20 * k).astype(jnp.int32) for k in range(1, 8))
+    start = z * 80 + low * 40 + lax.div(x_ref[0], 2) * 20
+    pick = one_hot(start + at - low * (W // 2) - z * 20, D // 2)
     chunks = NT // STEPS
     stores = []
     for i in range(STEPS):
@@ -109,7 +113,7 @@
         store.wait()
 
 
-def pick(x, order, grad_output, normed):
+def pick(x, grad_output, normed):
     hbm = pl.BlockSpec(memory_space=pl.ANY)
     shape = (NT, 2 * PT, 2 * W)
     return call(
@@ -119,7 +123,6 @@
         limit=60 * 1024 * 1024,
         in_specs=[
             pl.BlockSpec(memory_space=pltpu.SMEM),
-            pl.BlockSpec(memory_space=pltpu.VMEM),
             hbm,
             hbm,
         ],
@@ -130,7 +133,7 @@
             pltpu.SemaphoreType.DMA((2 * STEPS * FR,)),
             pltpu.SemaphoreType.DMA((STEPS,)),
         ],
-    )(x, order, grad_output, normed)
+    )(x, grad_output, normed)
 
 
 def pack_kernel(q_ref, k_ref, v_ref, out_ref):
@@ -327,7 +330,7 @@
     core = lax.axis_index("core")
     scalar = pl.BlockSpec(memory_space=pltpu.SMEM)
     whole = pl.BlockSpec(memory_space=pltpu.VMEM)
-    gon = pick(x.reshape(1), order, grad_output[0], normed[0])
+    gon = pick(x.reshape(1), grad_output[0], normed[0])
     gon = lax.all_to_all(gon, TM, 0, 0, tiled=True)
     gon = lax.all_gather(gon, "x", axis=0)
     qkv = call(pack_kernel, jax.ShapeDtypeStruct((NT, 3 * PT, FR * W), BF), 30_000_000_000)(

time: 164 us -> 163 us (level)
  no operation moved by 1% of the time
where the time goes in v7:
time: 163 us; the launch traced here: 161 us
  blocking collectives  52.9 us (32%)
  waiting for transfers between devices  51.5 us (32%)
  Pallas kernels  25.8 us (16%)
  starting transfers between devices  16.1 us (10%)
  between operations  14.2 us (9%)
    all_to_all x1, blocking collectives, on_device(): gon = lax.all_to_all(gon, TM, 0, 0, tiled=True)  31 us
    all_to_all x1, waiting for transfers between devices, on_device(): qkv = lax.all_to_all(qkv, TM, 0, 0, tiled=True)  24.7 us
    ppermute x6, waiting for transfers between devices, shift(): return lax.ppermute(array, 'x', [(i, (i + k) % NX) for i in range(NX)])  23.8 us
    all_to_all x1, blocking collectives, on_device(): lax.all_to_all(own_norm.reshape(NT, PT, 2 * W), TM, 0, 0, tiled=True)  21.9 us
    pallas_call x1, Pallas kernels, attend(): call(attend_kernel, (jax.ShapeDtypeStruct((TOK, 4 * W), BF),) + (jax.Shap...  10.7 us
    ppermute x6, starting transfers between devices, shift(): return lax.ppermute(array, 'x', [(i, (i + k) % NX) for i in range(NX)])  6.59 us
    all_to_all x1, starting transfers between devices, on_device(): qkv = lax.all_to_all(qkv, TM, 0, 0, tiled=True)  5.06 us
    pallas_call x2, Pallas kernels, weight_half(): call(weight_kernel, shape, 4000000000, spec, 20 * 1024 * 1024)  4.3 us
  transfers between devices with their start and end apart: 11, of which 9 were waited for; matrix products, arithmetic and copies ran while one was open for 0% of the time, Pallas kernels for 6%

profile of v7, /device:TPU:1, one launch (start us, length us, event | category | flops | bytes accessed | tf_op | source)
XLA Modules:
  0.0 160.6 jit_solution(10888244852080511389)
XLA Ops:
  7.2 0.0 all-gather.3.cloned.1.call-start
  7.2 3.2 %shard_map.104 = bf16[32,16,640]{2,1,0:T(8,128)(2,1)} custom-call(s32[1]{0:T(128)} %bitcast.x_ref, bf16[2,256,1280]{2,1,0:T(8,128)(2,1)} %bitcast.35, bf16[2,256,1280]{2,1,0:T(8,128)(2,1)} %bitcast.36), custom_call_target="tpu_custom_call" | custom-call | flops 850000000 | bytes 4000000 | tf_op jit(solution)/shard_map/pallas_call | solution.py:119
  10.5 31.0 %all_to_all.20 = bf16[32,16,640]{2,1,0:T(8,128)(2,1)} all-to-all(bf16[32,16,640]{2,1,0:T(8,128)(2,1)} %shard_map.104), channel_id=1, replica_groups=mesh['dp'=2,'z'=8,'yl'=2,'core'=2,'x'=4] {'z','yl','core'}, dimensions={0} | all-to-all | bytes 1310720 | tf_op jit(solution)/shard_map/all_to_all | solution.py:334
  41.5 1.3 shard_map.103
  42.8 5.1 %all-to-all-start = ((bf16[32,24,640]{2,1,0:T(8,128)(2,1)}), bf16[32,24,640]{2,1,0:T(8,128)(2,1)S(1)}, u32[]{:S(2)}, u32[]{:S(2)}) async-start(bf16[32,24,640]{2,1,0:T(8,128)(2,1)} %shard_map.103), calls=%async_computation | async-start | bytes 1966080 | tf_op jit(solution)/shard_map/all_to_all | solution.py:339
  47.9 0.2 reduce-scatter.2.cloned.1.call-start
  48.1 1.9 %shard_map.105.wout_ref = bf16[4,320,320]{2,1,0:T(8,128)(2,1)S(1)} custom-call(s32[4,1,320]{2,1,0:T(1,128)S(1)} %copy-done.5, bf16[320,1280]{1,0:T(8,128)(2,1)S(1)} %copy-done.1), custom_call_target="tpu_custom_call" | custom-call | flops 1000000000 | bytes 4000000 | tf_op jit(solution)/shard_map/pallas_call | solution.py:340
  50.0 24.7 %all-to-all-done.qkv_ref = bf16[32,24,640]{2,1,0:T(8,128)(2,1)S(1)} async-done(((bf16[32,24,640]{2,1,0:T(8,128)(2,1)}), bf16[32,24,640]{2,1,0:T(8,128)(2,1)S(1)}, u32[]{:S(2)}, u32[]{:S(2)}) %all-to-all-start) | async-done | bytes 983072 | tf_op jit(solution)/shard_map/all_to_all | solution.py:339
  74.7 1.9 %all-gather.3.cloned.1.call-done = bf16[128,16,640]{2,1,0:T(8,128)(2,1)} async-done(((bf16[32,16,640]{2,1,0:T(8,128)(2,1)}), bf16[128,16,640]{2,1,0:T(8,128)(2,1)}) %all-gather.3.cloned.1.call-update) | async-done | bytes 2621456 | tf_op jit(solution)/shard_map/all_gather | solution.py:335
  76.6 10.7 %shard_map.106 = (bf16[512,1280]{1,0:T(8,128)(2,1)S(1)}, bf16[256,640]{1,0:T(8,128)(2,1)S(1)}, bf16[256,640]{1,0:T(8,128)(2,1)S(1)}, bf16[256,640]{1,0:T(8,128)(2,1)S(1)}, bf16[256,640]{1,0:T(8,128)(2,1)S(1)}) custom-call(s32[1]{0:T(128)} %bitcast.x_ref, bf16[32,24,640]{2,1,0:T(8,128)(2,1)S(1)} %all-to-all-done.qkv_ref, bf16[4,32,16,640]{3,2,1,0:T(8,128)(2,1)} %bitcast.29, ...), custom_call_target="tpu_custom_call" | custom-call | flops 5000000000 | bytes 4000000 | tf_op jit(solution)/shard_map/pallas_call | solution.py:244
  87.3 1.7 %shard_map.109 = bf16[640,1280]{1,0:T(8,128)(2,1)S(1)} custom-call(s32[1]{0:T(128)} %bitcast.16.half_ref, bf16[4,32,16,640]{3,2,1,0:T(8,128)(2,1)S(1)} %bitcast.30, bf16[512,1280]{1,0:T(8,128)(2,1)S(1)} %get-tuple-element.14.grads_ref), custom_call_target="tpu_custom_call" | custom-call | flops 4000000000 | bytes 4000000 | tf_op jit(solution)/shard_map/pallas_call | solution.py:287
  89.0 0.8 collective-permute-start.6
  89.8 0.4 collective-permute-start
  90.1 2.1 %collective-permute-start.1 = (bf16[256,640]{1,0:T(8,128)(2,1)S(1)}, bf16[256,640]{1,0:T(8,128)(2,1)S(1)}, u32[]{:S(2)}, u32[]{:S(2)}) collective-permute-start(bf16[256,640]{1,0:T(8,128)(2,1)S(1)} %get-tuple-element.12), channel_id=1, source_target_pairs={{0,2},{1,3},{2,0},{3,1},{4,6},{5,7},{6,4},{7,5},{8,10},{9,11},{10,... | collective-permute-start | bytes 983048 | tf_op jit(solution)/shard_map/ppermute | solution.py:324
  92.3 1.2 collective-permute-start.2
  93.4 2.6 %shard_map.110 = bf16[640,1280]{1,0:T(8,128)(2,1)} custom-call(s32[1]{0:T(128)} %bitcast.15.half_ref, bf16[4,32,16,640]{3,2,1,0:T(8,128)(2,1)S(1)} %bitcast.31, bf16[512,1280]{1,0:T(8,128)(2,1)S(1)} %get-tuple-element.14.grads_ref, bf16[640,1280]{1,0:T(8,128)(2,1)S(1)} %collective-permute-done.6.refs_0_), custom_call_target="tpu_custom_call" | custom-call | flops 4000000000 | bytes 4000000 | tf_op jit(solution)/shard_map/pallas_call | solution.py:287
  96.1 4.4 %collective-permute-done.refs_1_ = bf16[256,640]{1,0:T(8,128)(2,1)S(1)} collective-permute-done((bf16[256,640]{1,0:T(8,128)(2,1)S(1)}, bf16[256,640]{1,0:T(8,128)(2,1)S(1)}, u32[]{:S(2)}, u32[]{:S(2)}) %collective-permute-start) | collective-permute-done | bytes 327712 | tf_op jit(solution)/shard_map/ppermute | solution.py:324
  100.4 6.7 %collective-permute-done.1.refs_2_ = bf16[256,640]{1,0:T(8,128)(2,1)S(1)} collective-permute-done((bf16[256,640]{1,0:T(8,128)(2,1)S(1)}, bf16[256,640]{1,0:T(8,128)(2,1)S(1)}, u32[]{:S(2)}, u32[]{:S(2)}) %collective-permute-start.1) | collective-permute-done | bytes 327712 | tf_op jit(solution)/shard_map/ppermute | solution.py:324
  107.1 0.5 collective-permute-done.2.refs_3_
  107.6 0.2 shard_map.107
  107.7 21.9 %all_to_all.21 = bf16[32,8,640]{2,1,0:T(8,128)(2,1)S(1)} all-to-all(bf16[32,8,640]{2,1,0:T(8,128)(2,1)S(1)} %bitcast.28), channel_id=1, replica_groups=mesh['dp'=2,'z'=8,'yl'=2,'core'=2,'x'=4] {'z','yl','core'}, dimensions={0} | all-to-all | bytes 655360 | tf_op jit(solution)/shard_map/all_to_all | solution.py:350
  129.6 2.4 %collective-permute-start.5 = (bf16[256,640]{1,0:T(8,128)(2,1)S(1)}, bf16[256,640]{1,0:T(8,128)(2,1)S(1)}, u32[]{:S(2)}, u32[]{:S(2)}) collective-permute-start(bf16[256,640]{1,0:T(8,128)(2,1)S(1)} %bitcast.24), channel_id=1, source_target_pairs={{0,3},{1,0},{2,1},{3,2},{4,7},{5,4},{6,5},{7,6},{8,11},{9,8},{10,9... | collective-permute-start | bytes 983048 | tf_op jit(solution)/shard_map/ppermute | solution.py:324
  132.0 0.4 collective-permute-start.4
  132.3 0.2 collective-permute-start.3
  132.5 1.8 %shard_map.111 = bf16[8,20,1280]{2,1,0:T(8,128)(2,1)} custom-call(bf16[160,1280]{1,0:T(8,128)(2,1)} %bitcast.37), custom_call_target="tpu_custom_call" | custom-call | bytes 4000000 | tf_op jit(solution)/shard_map/pallas_call | solution.py:359
  134.4 3.5 %all-to-all-start.3 = ((bf16[8,20,1280]{2,1,0:T(8,128)(2,1)}), bf16[8,20,1280]{2,1,0:T(8,128)(2,1)S(1)}, u32[]{:S(2)}, u32[]{:S(2)}) async-start(bf16[8,20,1280]{2,1,0:T(8,128)(2,1)} %shard_map.111), calls=%async_computation.4 | async-start | bytes 983040 | tf_op jit(solution)/shard_map/all_to_all | solution.py:360
  137.8 0.5 collective-permute-done.5.refs_3_
  138.3 2.8 %collective-permute-done.4.refs_2_ = bf16[256,640]{1,0:T(8,128)(2,1)S(1)} collective-permute-done((bf16[256,640]{1,0:T(8,128)(2,1)S(1)}, bf16[256,640]{1,0:T(8,128)(2,1)S(1)}, u32[]{:S(2)}, u32[]{:S(2)}) %collective-permute-start.4) | collective-permute-done | bytes 327712 | tf_op jit(solution)/shard_map/ppermute | solution.py:324
  141.2 8.9 %collective-permute-done.3.refs_1_ = bf16[256,640]{1,0:T(8,128)(2,1)S(1)} collective-permute-done((bf16[256,640]{1,0:T(8,128)(2,1)S(1)}, bf16[256,640]{1,0:T(8,128)(2,1)S(1)}, u32[]{:S(2)}, u32[]{:S(2)}) %collective-permute-start.3) | collective-permute-done | bytes 327712 | tf_op jit(solution)/shard_map/ppermute | solution.py:324
  150.1 1.7 %shard_map.108 = bf16[2,256,1280]{2,1,0:T(8,128)(2,1)} custom-call(s32[1]{0:T(128)} %bitcast.x_ref, bf16[256,640]{1,0:T(8,128)(2,1)S(1)} %bitcast.27, bf16[256,640]{1,0:T(8,128)(2,1)S(1)} %collective-permute-done.3.refs_1_, bf16[256,640]{1,0:T(8,128)(2,1)S(1)} %collective-permute-done.4.refs_2_, bf16[256,640]{1,0:T(8,128)(2,1)S(1)} %collective-permute-done.5.refs_3_), custom_call_target="tpu_custom_call" | custom-call | flops 40000000000 | bytes 4000000 | tf_op jit(solution)/shard_map/pallas_call | solution.py:352
  151.8 1.1 all-to-all-done.3.in_ref
  153.0 0.8 shard_map.112
  (16 shorter events, 0.1 us)
Async XLA Ops:
  7.2 69.4 %all-gather.3.cloned.1.call-start = ((), (), s32[]{:S(2)}) async-start(), calls=%async_computation.6 | async-start | bytes 3276800 | tf_op jit(solution)/shard_map/all_gather | solution.py:335
  10.4 31.1 %copy-start.2 = (bf16[1,2,256,320]{2,3,1,0:T(8,128)(2,1)S(1)}, bf16[1,2,256,320]{2,3,1,0:T(8,128)(2,1)}, u32[]{:S(2)}) copy-start(bf16[1,2,256,320]{2,3,1,0:T(8,128)(2,1)} %param.8) | copy-start | bytes 983044
  10.4 31.1 %copy-start.3 = (bf16[1,2,256,320]{2,3,1,0:T(8,128)(2,1)S(1)}, bf16[1,2,256,320]{2,3,1,0:T(8,128)(2,1)}, u32[]{:S(2)}) copy-start(bf16[1,2,256,320]{2,3,1,0:T(8,128)(2,1)} %param.9) | copy-start | bytes 983044
  10.5 31.1 %copy-start.4 = (bf16[1,2,256,320]{2,3,1,0:T(8,128)(2,1)S(1)}, bf16[1,2,256,320]{2,3,1,0:T(8,128)(2,1)}, u32[]{:S(2)}) copy-start(bf16[1,2,256,320]{2,3,1,0:T(8,128)(2,1)} %param.10) | copy-start | bytes 983044
  42.8 5.3 %copy-start.1 = (bf16[320,1280]{1,0:T(8,128)(2,1)S(1)}, bf16[320,1280]{1,0:T(8,128)(2,1)}, u32[]{:S(2)}) copy-start(bf16[320,1280]{1,0:T(8,128)(2,1)} %w_ref.1) | copy-start | bytes 2457604
  42.8 5.3 %copy-start.5 = (s32[4,1,320]{2,1,0:T(1,128)S(1)}, s32[4,1,320]{2,1,0:T(1,128)}, u32[]{:S(2)}) copy-start(s32[4,1,320]{2,1,0:T(1,128)} %constant.13.clone.feat_ref) | copy-start | bytes 15364
  42.8 31.9 %all-to-all-start = ((bf16[32,24,640]{2,1,0:T(8,128)(2,1)}), bf16[32,24,640]{2,1,0:T(8,128)(2,1)S(1)}, u32[]{:S(2)}, u32[]{:S(2)}) async-start(bf16[32,24,640]{2,1,0:T(8,128)(2,1)} %shard_map.103), calls=%async_computation | async-start | bytes 1966080 | tf_op jit(solution)/shard_map/all_to_all | solution.py:339
  47.9 84.7 %reduce-scatter.2.cloned.1.call-start = ((), (), s32[]{:S(2)}) async-start(), calls=%async_computation.5 | async-start | bytes 2048000 | tf_op jit(solution)/shard_map/reduce_scatter | solution.py:347
  76.6 10.7 %copy-start = (bf16[128,16,640]{2,1,0:T(8,128)(2,1)S(1)}, bf16[128,16,640]{2,1,0:T(8,128)(2,1)}, u32[]{:S(2)}) copy-start(bf16[128,16,640]{2,1,0:T(8,128)(2,1)} %all-gather.3.cloned.1.call-done) | copy-start | bytes 7864324
  89.0 4.4 %collective-permute-start.6 = (bf16[640,1280]{1,0:T(8,128)(2,1)S(1)}, bf16[640,1280]{1,0:T(8,128)(2,1)S(1)}, u32[]{:S(2)}, u32[]{:S(2)}) collective-permute-start(bf16[640,1280]{1,0:T(8,128)(2,1)S(1)} %shard_map.109), channel_id=1, source_target_pairs={{0,4},{4,0},{1,5},{5,1},{2,6},{6,2},{3,7},{7,3},{8,12},{12,8},{9,1... | collective-permute-start | bytes 4915208 | tf_op jit(solution)/shard_map/ppermute | solution.py:345
  89.8 10.7 %collective-permute-start = (bf16[256,640]{1,0:T(8,128)(2,1)S(1)}, bf16[256,640]{1,0:T(8,128)(2,1)S(1)}, u32[]{:S(2)}, u32[]{:S(2)}) collective-permute-start(bf16[256,640]{1,0:T(8,128)(2,1)S(1)} %get-tuple-element.11), channel_id=1, source_target_pairs={{0,1},{1,2},{2,3},{3,0},{4,5},{5,6},{6,7},{7,4},{8,9},{9,10},{10,1... | collective-permute-start | bytes 983048 | tf_op jit(solution)/shard_map/ppermute | solution.py:324
  90.1 17.0 %collective-permute-start.1 = (bf16[256,640]{1,0:T(8,128)(2,1)S(1)}, bf16[256,640]{1,0:T(8,128)(2,1)S(1)}, u32[]{:S(2)}, u32[]{:S(2)}) collective-permute-start(bf16[256,640]{1,0:T(8,128)(2,1)S(1)} %get-tuple-element.12), channel_id=1, source_target_pairs={{0,2},{1,3},{2,0},{3,1},{4,6},{5,7},{6,4},{7,5},{8,10},{9,11},{10,... | collective-permute-start | bytes 983048 | tf_op jit(solution)/shard_map/ppermute | solution.py:324
  92.3 15.3 %collective-permute-start.2 = (bf16[256,640]{1,0:T(8,128)(2,1)S(1)}, bf16[256,640]{1,0:T(8,128)(2,1)S(1)}, u32[]{:S(2)}, u32[]{:S(2)}) collective-permute-start(bf16[256,640]{1,0:T(8,128)(2,1)S(1)} %get-tuple-element.13), channel_id=1, source_target_pairs={{0,3},{1,0},{2,1},{3,2},{4,7},{5,4},{6,5},{7,6},{8,11},{9,8},{10,9... | collective-permute-start | bytes 983048 | tf_op jit(solution)/shard_map/ppermute | solution.py:324
  129.6 8.7 %collective-permute-start.5 = (bf16[256,640]{1,0:T(8,128)(2,1)S(1)}, bf16[256,640]{1,0:T(8,128)(2,1)S(1)}, u32[]{:S(2)}, u32[]{:S(2)}) collective-permute-start(bf16[256,640]{1,0:T(8,128)(2,1)S(1)} %bitcast.24), channel_id=1, source_target_pairs={{0,3},{1,0},{2,1},{3,2},{4,7},{5,4},{6,5},{7,6},{8,11},{9,8},{10,9... | collective-permute-start | bytes 983048 | tf_op jit(solution)/shard_map/ppermute | solution.py:324
  132.0 9.2 %collective-permute-start.4 = (bf16[256,640]{1,0:T(8,128)(2,1)S(1)}, bf16[256,640]{1,0:T(8,128)(2,1)S(1)}, u32[]{:S(2)}, u32[]{:S(2)}) collective-permute-start(bf16[256,640]{1,0:T(8,128)(2,1)S(1)} %bitcast.25), channel_id=1, source_target_pairs={{0,2},{1,3},{2,0},{3,1},{4,6},{5,7},{6,4},{7,5},{8,10},{9,11},{10,... | collective-permute-start | bytes 983048 | tf_op jit(solution)/shard_map/ppermute | solution.py:324
  132.3 17.8 %collective-permute-start.3 = (bf16[256,640]{1,0:T(8,128)(2,1)S(1)}, bf16[256,640]{1,0:T(8,128)(2,1)S(1)}, u32[]{:S(2)}, u32[]{:S(2)}) collective-permute-start(bf16[256,640]{1,0:T(8,128)(2,1)S(1)} %bitcast.26), channel_id=1, source_target_pairs={{0,1},{1,2},{2,3},{3,0},{4,5},{5,6},{6,7},{7,4},{8,9},{9,10},{10,1... | collective-permute-start | bytes 983048 | tf_op jit(solution)/shard_map/ppermute | solution.py:324
  134.4 18.6 %all-to-all-start.3 = ((bf16[8,20,1280]{2,1,0:T(8,128)(2,1)}), bf16[8,20,1280]{2,1,0:T(8,128)(2,1)S(1)}, u32[]{:S(2)}, u32[]{:S(2)}) async-start(bf16[8,20,1280]{2,1,0:T(8,128)(2,1)} %shard_map.111), calls=%async_computation.4 | async-start | bytes 983040 | tf_op jit(solution)/shard_map/all_to_all | solution.py:360
Sparse Core Ops, SparseCore 0:
  41.6 34.9 all-gather.2
  96.2 28.5 reduce-scatter.1

commit v8 on v7

--- a/solution.py
+++ b/solution.py
@@ -332,7 +332,7 @@
     whole = pl.BlockSpec(memory_space=pltpu.VMEM)
     gon = pick(x.reshape(1), grad_output[0], normed[0])
     gon = lax.all_to_all(gon, TM, 0, 0, tiled=True)
-    gon = lax.all_gather(gon, "x", axis=0)
+    gon = lax.all_gather(gon.reshape(TOK, 2 * W), "x", axis=0, tiled=True).reshape(NX, NT, 2 * PT, 2 * W)
     qkv = call(pack_kernel, jax.ShapeDtypeStruct((NT, 3 * PT, FR * W), BF), 30_000_000_000)(
         *[jnp.swapaxes(item[0], 1, 2) for item in (queries, key_vectors, value_vectors)]
     )

time: 163 us -> 163 us (level)
  no operation moved by 1% of the time
where the time goes in v8:
time: 163 us; the launch traced here: 161 us
  blocking collectives  52.9 us (32%)
  waiting for transfers between devices  51.5 us (32%)
  Pallas kernels  25.8 us (16%)
  starting transfers between devices  16.1 us (10%)
  between operations  14.2 us (9%)
    all_to_all x1, blocking collectives, on_device(): gon = lax.all_to_all(gon, TM, 0, 0, tiled=True)  31 us
    all_to_all x1, waiting for transfers between devices, on_device(): qkv = lax.all_to_all(qkv, TM, 0, 0, tiled=True)  24.7 us
    ppermute x6, waiting for transfers between devices, shift(): return lax.ppermute(array, 'x', [(i, (i + k) % NX) for i in range(NX)])  23.8 us
    all_to_all x1, blocking collectives, on_device(): lax.all_to_all(own_norm.reshape(NT, PT, 2 * W), TM, 0, 0, tiled=True)  21.9 us
    pallas_call x1, Pallas kernels, attend(): call(attend_kernel, (jax.ShapeDtypeStruct((TOK, 4 * W), BF),) + (jax.Shap...  10.7 us
    ppermute x6, starting transfers between devices, shift(): return lax.ppermute(array, 'x', [(i, (i + k) % NX) for i in range(NX)])  6.59 us
    all_to_all x1, starting transfers between devices, on_device(): qkv = lax.all_to_all(qkv, TM, 0, 0, tiled=True)  5.06 us
    pallas_call x2, Pallas kernels, weight_half(): call(weight_kernel, shape, 4000000000, spec, 20 * 1024 * 1024)  4.3 us
  transfers between devices with their start and end apart: 11, of which 9 were waited for; matrix products, arithmetic and copies ran while one was open for 0% of the time, Pallas kernels for 6%

profile of v8, /device:TPU:1, one launch (start us, length us, event | category | flops | bytes accessed | tf_op | source)
XLA Modules:
  0.0 160.6 jit_solution(12834146056338362971)
XLA Ops:
  7.2 0.0 all-gather.2.cloned.1.call-start
  7.2 3.2 %shard_map.104 = bf16[32,16,640]{2,1,0:T(8,128)(2,1)} custom-call(s32[1]{0:T(128)} %bitcast.x_ref, bf16[2,256,1280]{2,1,0:T(8,128)(2,1)} %bitcast.37, bf16[2,256,1280]{2,1,0:T(8,128)(2,1)} %bitcast.38), custom_call_target="tpu_custom_call" | custom-call | flops 850000000 | bytes 4000000 | tf_op jit(solution)/shard_map/pallas_call | solution.py:119
  10.5 31.0 %all_to_all.20 = bf16[32,16,640]{2,1,0:T(8,128)(2,1)} all-to-all(bf16[32,16,640]{2,1,0:T(8,128)(2,1)} %shard_map.104), channel_id=1, replica_groups=mesh['dp'=2,'z'=8,'yl'=2,'core'=2,'x'=4] {'z','yl','core'}, dimensions={0} | all-to-all | bytes 1310720 | tf_op jit(solution)/shard_map/all_to_all | solution.py:334
  41.5 1.3 shard_map.103
  42.8 5.1 %all-to-all-start = ((bf16[32,24,640]{2,1,0:T(8,128)(2,1)}), bf16[32,24,640]{2,1,0:T(8,128)(2,1)S(1)}, u32[]{:S(2)}, u32[]{:S(2)}) async-start(bf16[32,24,640]{2,1,0:T(8,128)(2,1)} %shard_map.103), calls=%async_computation | async-start | bytes 1966080 | tf_op jit(solution)/shard_map/all_to_all | solution.py:339
  47.9 0.2 reduce-scatter.2.cloned.1.call-start
  48.1 1.9 %shard_map.105.wout_ref = bf16[4,320,320]{2,1,0:T(8,128)(2,1)S(1)} custom-call(s32[4,1,320]{2,1,0:T(1,128)S(1)} %copy-done.5, bf16[320,1280]{1,0:T(8,128)(2,1)S(1)} %copy-done.1), custom_call_target="tpu_custom_call" | custom-call | flops 1000000000 | bytes 4000000 | tf_op jit(solution)/shard_map/pallas_call | solution.py:340
  50.0 24.7 %all-to-all-done.qkv_ref = bf16[32,24,640]{2,1,0:T(8,128)(2,1)S(1)} async-done(((bf16[32,24,640]{2,1,0:T(8,128)(2,1)}), bf16[32,24,640]{2,1,0:T(8,128)(2,1)S(1)}, u32[]{:S(2)}, u32[]{:S(2)}) %all-to-all-start) | async-done | bytes 983072 | tf_op jit(solution)/shard_map/all_to_all | solution.py:339
  74.7 1.9 %all-gather.2.cloned.1.call-done = bf16[2048,640]{1,0:T(8,128)(2,1)} async-done(((bf16[512,640]{1,0:T(8,128)(2,1)}), bf16[2048,640]{1,0:T(8,128)(2,1)}) %all-gather.2.cloned.1.call-update) | async-done | bytes 2621456 | tf_op jit(solution)/shard_map/all_gather | solution.py:335
  76.6 10.7 %shard_map.106 = (bf16[512,1280]{1,0:T(8,128)(2,1)S(1)}, bf16[256,640]{1,0:T(8,128)(2,1)S(1)}, bf16[256,640]{1,0:T(8,128)(2,1)S(1)}, bf16[256,640]{1,0:T(8,128)(2,1)S(1)}, bf16[256,640]{1,0:T(8,128)(2,1)S(1)}) custom-call(s32[1]{0:T(128)} %bitcast.x_ref, bf16[32,24,640]{2,1,0:T(8,128)(2,1)S(1)} %all-to-all-done.qkv_ref, bf16[4,32,16,640]{3,2,1,0:T(8,128)(2,1)} %bitcast.30, ...), custom_call_target="tpu_custom_call" | custom-call | flops 5000000000 | bytes 4000000 | tf_op jit(solution)/shard_map/pallas_call | solution.py:244
  87.3 1.7 %shard_map.109 = bf16[640,1280]{1,0:T(8,128)(2,1)S(1)} custom-call(s32[1]{0:T(128)} %bitcast.17.half_ref, bf16[4,32,16,640]{3,2,1,0:T(8,128)(2,1)S(1)} %bitcast.31, bf16[512,1280]{1,0:T(8,128)(2,1)S(1)} %get-tuple-element.14.grads_ref), custom_call_target="tpu_custom_call" | custom-call | flops 4000000000 | bytes 4000000 | tf_op jit(solution)/shard_map/pallas_call | solution.py:287
  89.0 0.8 collective-permute-start.6
  89.8 0.4 collective-permute-start
  90.1 2.1 %collective-permute-start.1 = (bf16[256,640]{1,0:T(8,128)(2,1)S(1)}, bf16[256,640]{1,0:T(8,128)(2,1)S(1)}, u32[]{:S(2)}, u32[]{:S(2)}) collective-permute-start(bf16[256,640]{1,0:T(8,128)(2,1)S(1)} %get-tuple-element.12), channel_id=1, source_target_pairs={{0,2},{1,3},{2,0},{3,1},{4,6},{5,7},{6,4},{7,5},{8,10},{9,11},{10,... | collective-permute-start | bytes 983048 | tf_op jit(solution)/shard_map/ppermute | solution.py:324
  92.3 1.2 collective-permute-start.2
  93.4 2.6 %shard_map.110 = bf16[640,1280]{1,0:T(8,128)(2,1)} custom-call(s32[1]{0:T(128)} %bitcast.16.half_ref, bf16[4,32,16,640]{3,2,1,0:T(8,128)(2,1)S(1)} %bitcast.32, bf16[512,1280]{1,0:T(8,128)(2,1)S(1)} %get-tuple-element.14.grads_ref, bf16[640,1280]{1,0:T(8,128)(2,1)S(1)} %collective-permute-done.6.refs_0_), custom_call_target="tpu_custom_call" | custom-call | flops 4000000000 | bytes 4000000 | tf_op jit(solution)/shard_map/pallas_call | solution.py:287
  96.1 4.4 %collective-permute-done.refs_1_ = bf16[256,640]{1,0:T(8,128)(2,1)S(1)} collective-permute-done((bf16[256,640]{1,0:T(8,128)(2,1)S(1)}, bf16[256,640]{1,0:T(8,128)(2,1)S(1)}, u32[]{:S(2)}, u32[]{:S(2)}) %collective-permute-start) | collective-permute-done | bytes 327712 | tf_op jit(solution)/shard_map/ppermute | solution.py:324
  100.4 6.7 %collective-permute-done.1.refs_2_ = bf16[256,640]{1,0:T(8,128)(2,1)S(1)} collective-permute-done((bf16[256,640]{1,0:T(8,128)(2,1)S(1)}, bf16[256,640]{1,0:T(8,128)(2,1)S(1)}, u32[]{:S(2)}, u32[]{:S(2)}) %collective-permute-start.1) | collective-permute-done | bytes 327712 | tf_op jit(solution)/shard_map/ppermute | solution.py:324
  107.1 0.5 collective-permute-done.2.refs_3_
  107.6 0.2 shard_map.107
  107.7 21.9 %all_to_all.21 = bf16[32,8,640]{2,1,0:T(8,128)(2,1)S(1)} all-to-all(bf16[32,8,640]{2,1,0:T(8,128)(2,1)S(1)} %bitcast.29), channel_id=1, replica_groups=mesh['dp'=2,'z'=8,'yl'=2,'core'=2,'x'=4] {'z','yl','core'}, dimensions={0} | all-to-all | bytes 655360 | tf_op jit(solution)/shard_map/all_to_all | solution.py:350
  129.6 2.4 %collective-permute-start.5 = (bf16[256,640]{1,0:T(8,128)(2,1)S(1)}, bf16[256,640]{1,0:T(8,128)(2,1)S(1)}, u32[]{:S(2)}, u32[]{:S(2)}) collective-permute-start(bf16[256,640]{1,0:T(8,128)(2,1)S(1)} %bitcast.25), channel_id=1, source_target_pairs={{0,3},{1,0},{2,1},{3,2},{4,7},{5,4},{6,5},{7,6},{8,11},{9,8},{10,9... | collective-permute-start | bytes 983048 | tf_op jit(solution)/shard_map/ppermute | solution.py:324
  132.0 0.4 collective-permute-start.4
  132.3 0.2 collective-permute-start.3
  132.5 1.8 %shard_map.111 = bf16[8,20,1280]{2,1,0:T(8,128)(2,1)} custom-call(bf16[160,1280]{1,0:T(8,128)(2,1)} %bitcast.39), custom_call_target="tpu_custom_call" | custom-call | bytes 4000000 | tf_op jit(solution)/shard_map/pallas_call | solution.py:359
  134.4 3.5 %all-to-all-start.3 = ((bf16[8,20,1280]{2,1,0:T(8,128)(2,1)}), bf16[8,20,1280]{2,1,0:T(8,128)(2,1)S(1)}, u32[]{:S(2)}, u32[]{:S(2)}) async-start(bf16[8,20,1280]{2,1,0:T(8,128)(2,1)} %shard_map.111), calls=%async_computation.4 | async-start | bytes 983040 | tf_op jit(solution)/shard_map/all_to_all | solution.py:360
  137.8 0.5 collective-permute-done.5.refs_3_
  138.3 2.8 %collective-permute-done.4.refs_2_ = bf16[256,640]{1,0:T(8,128)(2,1)S(1)} collective-permute-done((bf16[256,640]{1,0:T(8,128)(2,1)S(1)}, bf16[256,640]{1,0:T(8,128)(2,1)S(1)}, u32[]{:S(2)}, u32[]{:S(2)}) %collective-permute-start.4) | collective-permute-done | bytes 327712 | tf_op jit(solution)/shard_map/ppermute | solution.py:324
  141.2 8.9 %collective-permute-done.3.refs_1_ = bf16[256,640]{1,0:T(8,128)(2,1)S(1)} collective-permute-done((bf16[256,640]{1,0:T(8,128)(2,1)S(1)}, bf16[256,640]{1,0:T(8,128)(2,1)S(1)}, u32[]{:S(2)}, u32[]{:S(2)}) %collective-permute-start.3) | collective-permute-done | bytes 327712 | tf_op jit(solution)/shard_map/ppermute | solution.py:324
  150.1 1.7 %shard_map.108 = bf16[2,256,1280]{2,1,0:T(8,128)(2,1)} custom-call(s32[1]{0:T(128)} %bitcast.x_ref, bf16[256,640]{1,0:T(8,128)(2,1)S(1)} %bitcast.28, bf16[256,640]{1,0:T(8,128)(2,1)S(1)} %collective-permute-done.3.refs_1_, bf16[256,640]{1,0:T(8,128)(2,1)S(1)} %collective-permute-done.4.refs_2_, bf16[256,640]{1,0:T(8,128)(2,1)S(1)} %collective-permute-done.5.refs_3_), custom_call_target="tpu_custom_call" | custom-call | flops 40000000000 | bytes 4000000 | tf_op jit(solution)/shard_map/pallas_call | solution.py:352
  151.8 1.1 all-to-all-done.3.in_ref
  153.0 0.8 shard_map.112
  (16 shorter events, 0.1 us)
Async XLA Ops:
  7.2 69.4 %all-gather.2.cloned.1.call-start = ((), (), s32[]{:S(2)}) async-start(), calls=%async_computation.5 | async-start | bytes 3276800 | tf_op jit(solution)/shard_map/all_gather | solution.py:335
  10.4 31.1 %copy-start.2 = (bf16[1,2,256,320]{2,3,1,0:T(8,128)(2,1)S(1)}, bf16[1,2,256,320]{2,3,1,0:T(8,128)(2,1)}, u32[]{:S(2)}) copy-start(bf16[1,2,256,320]{2,3,1,0:T(8,128)(2,1)} %param.8) | copy-start | bytes 983044
  10.4 31.1 %copy-start.3 = (bf16[1,2,256,320]{2,3,1,0:T(8,128)(2,1)S(1)}, bf16[1,2,256,320]{2,3,1,0:T(8,128)(2,1)}, u32[]{:S(2)}) copy-start(bf16[1,2,256,320]{2,3,1,0:T(8,128)(2,1)} %param.9) | copy-start | bytes 983044
  10.5 31.1 %copy-start.4 = (bf16[1,2,256,320]{2,3,1,0:T(8,128)(2,1)S(1)}, bf16[1,2,256,320]{2,3,1,0:T(8,128)(2,1)}, u32[]{:S(2)}) copy-start(bf16[1,2,256,320]{2,3,1,0:T(8,128)(2,1)} %param.10) | copy-start | bytes 983044
  42.8 5.3 %copy-start.1 = (bf16[320,1280]{1,0:T(8,128)(2,1)S(1)}, bf16[320,1280]{1,0:T(8,128)(2,1)}, u32[]{:S(2)}) copy-start(bf16[320,1280]{1,0:T(8,128)(2,1)} %w_ref.1) | copy-start | bytes 2457604
  42.8 5.3 %copy-start.5 = (s32[4,1,320]{2,1,0:T(1,128)S(1)}, s32[4,1,320]{2,1,0:T(1,128)}, u32[]{:S(2)}) copy-start(s32[4,1,320]{2,1,0:T(1,128)} %constant.13.clone.feat_ref) | copy-start | bytes 15364
  42.8 31.9 %all-to-all-start = ((bf16[32,24,640]{2,1,0:T(8,128)(2,1)}), bf16[32,24,640]{2,1,0:T(8,128)(2,1)S(1)}, u32[]{:S(2)}, u32[]{:S(2)}) async-start(bf16[32,24,640]{2,1,0:T(8,128)(2,1)} %shard_map.103), calls=%async_computation | async-start | bytes 1966080 | tf_op jit(solution)/shard_map/all_to_all | solution.py:339
  47.9 84.7 %reduce-scatter.2.cloned.1.call-start = ((), (), s32[]{:S(2)}) async-start(), calls=%async_computation.6 | async-start | bytes 2048000 | tf_op jit(solution)/shard_map/reduce_scatter | solution.py:347
  76.6 10.7 %copy-start = (bf16[2048,640]{1,0:T(8,128)(2,1)S(1)}, bf16[2048,640]{1,0:T(8,128)(2,1)}, u32[]{:S(2)}) copy-start(bf16[2048,640]{1,0:T(8,128)(2,1)} %all-gather.2.cloned.1.call-done) | copy-start | bytes 7864324
  89.0 4.4 %collective-permute-start.6 = (bf16[640,1280]{1,0:T(8,128)(2,1)S(1)}, bf16[640,1280]{1,0:T(8,128)(2,1)S(1)}, u32[]{:S(2)}, u32[]{:S(2)}) collective-permute-start(bf16[640,1280]{1,0:T(8,128)(2,1)S(1)} %shard_map.109), channel_id=1, source_target_pairs={{0,4},{4,0},{1,5},{5,1},{2,6},{6,2},{3,7},{7,3},{8,12},{12,8},{9,1... | collective-permute-start | bytes 4915208 | tf_op jit(solution)/shard_map/ppermute | solution.py:345
  89.8 10.7 %collective-permute-start = (bf16[256,640]{1,0:T(8,128)(2,1)S(1)}, bf16[256,640]{1,0:T(8,128)(2,1)S(1)}, u32[]{:S(2)}, u32[]{:S(2)}) collective-permute-start(bf16[256,640]{1,0:T(8,128)(2,1)S(1)} %get-tuple-element.11), channel_id=1, source_target_pairs={{0,1},{1,2},{2,3},{3,0},{4,5},{5,6},{6,7},{7,4},{8,9},{9,10},{10,1... | collective-permute-start | bytes 983048 | tf_op jit(solution)/shard_map/ppermute | solution.py:324
  90.1 17.0 %collective-permute-start.1 = (bf16[256,640]{1,0:T(8,128)(2,1)S(1)}, bf16[256,640]{1,0:T(8,128)(2,1)S(1)}, u32[]{:S(2)}, u32[]{:S(2)}) collective-permute-start(bf16[256,640]{1,0:T(8,128)(2,1)S(1)} %get-tuple-element.12), channel_id=1, source_target_pairs={{0,2},{1,3},{2,0},{3,1},{4,6},{5,7},{6,4},{7,5},{8,10},{9,11},{10,... | collective-permute-start | bytes 983048 | tf_op jit(solution)/shard_map/ppermute | solution.py:324
  92.3 15.3 %collective-permute-start.2 = (bf16[256,640]{1,0:T(8,128)(2,1)S(1)}, bf16[256,640]{1,0:T(8,128)(2,1)S(1)}, u32[]{:S(2)}, u32[]{:S(2)}) collective-permute-start(bf16[256,640]{1,0:T(8,128)(2,1)S(1)} %get-tuple-element.13), channel_id=1, source_target_pairs={{0,3},{1,0},{2,1},{3,2},{4,7},{5,4},{6,5},{7,6},{8,11},{9,8},{10,9... | collective-permute-start | bytes 983048 | tf_op jit(solution)/shard_map/ppermute | solution.py:324
  129.6 8.7 %collective-permute-start.5 = (bf16[256,640]{1,0:T(8,128)(2,1)S(1)}, bf16[256,640]{1,0:T(8,128)(2,1)S(1)}, u32[]{:S(2)}, u32[]{:S(2)}) collective-permute-start(bf16[256,640]{1,0:T(8,128)(2,1)S(1)} %bitcast.25), channel_id=1, source_target_pairs={{0,3},{1,0},{2,1},{3,2},{4,7},{5,4},{6,5},{7,6},{8,11},{9,8},{10,9... | collective-permute-start | bytes 983048 | tf_op jit(solution)/shard_map/ppermute | solution.py:324
  132.0 9.2 %collective-permute-start.4 = (bf16[256,640]{1,0:T(8,128)(2,1)S(1)}, bf16[256,640]{1,0:T(8,128)(2,1)S(1)}, u32[]{:S(2)}, u32[]{:S(2)}) collective-permute-start(bf16[256,640]{1,0:T(8,128)(2,1)S(1)} %bitcast.26), channel_id=1, source_target_pairs={{0,2},{1,3},{2,0},{3,1},{4,6},{5,7},{6,4},{7,5},{8,10},{9,11},{10,... | collective-permute-start | bytes 983048 | tf_op jit(solution)/shard_map/ppermute | solution.py:324
  132.3 17.8 %collective-permute-start.3 = (bf16[256,640]{1,0:T(8,128)(2,1)S(1)}, bf16[256,640]{1,0:T(8,128)(2,1)S(1)}, u32[]{:S(2)}, u32[]{:S(2)}) collective-permute-start(bf16[256,640]{1,0:T(8,128)(2,1)S(1)} %bitcast.27), channel_id=1, source_target_pairs={{0,1},{1,2},{2,3},{3,0},{4,5},{5,6},{6,7},{7,4},{8,9},{9,10},{10,1... | collective-permute-start | bytes 983048 | tf_op jit(solution)/shard_map/ppermute | solution.py:324
  134.4 18.6 %all-to-all-start.3 = ((bf16[8,20,1280]{2,1,0:T(8,128)(2,1)}), bf16[8,20,1280]{2,1,0:T(8,128)(2,1)S(1)}, u32[]{:S(2)}, u32[]{:S(2)}) async-start(bf16[8,20,1280]{2,1,0:T(8,128)(2,1)} %shard_map.111), calls=%async_computation.4 | async-start | bytes 983040 | tf_op jit(solution)/shard_map/all_to_all | solution.py:360
Sparse Core Ops, SparseCore 0:
  41.6 34.9 all-gather.1
  96.2 28.7 reduce-scatter.1

commit v9 on v8

--- a/solution.py
+++ b/solution.py
@@ -263,7 +263,7 @@
 def weight_kernel(half_ref, gon_ref, grads_ref, *refs):
     del half_ref
     out_ref = refs[-1]
-    gon_t = gon_ref[0].reshape(TOK, 2 * W).astype(F32).T.astype(BF)
+    gon_t = gon_ref[0].reshape(TOK, 2 * W).T
     for rows, cols in ((slice(W, 2 * W), slice(0, 3 * W)), (slice(0, W), slice(3 * W, 4 * W))):
         total = dot(gon_t[rows], grads_ref[:, cols])
         if len(refs) == 2:

time: 163 us -> 163 us (level)
  no operation moved by 1% of the time
where the time goes in v9:
time: 163 us; the launch traced here: 160 us
  blocking collectives  52.9 us (32%)
  waiting for transfers between devices  51.6 us (32%)
  Pallas kernels  25.7 us (16%)
  starting transfers between devices  16.1 us (10%)
  between operations  14.2 us (9%)
    all_to_all x1, blocking collectives, on_device(): gon = lax.all_to_all(gon, TM, 0, 0, tiled=True)  31 us
    all_to_all x1, waiting for transfers between devices, on_device(): qkv = lax.all_to_all(qkv, TM, 0, 0, tiled=True)  24.7 us
    ppermute x6, waiting for transfers between devices, shift(): return lax.ppermute(array, 'x', [(i, (i + k) % NX) for i in range(NX)])  23.8 us
    all_to_all x1, blocking collectives, on_device(): lax.all_to_all(own_norm.reshape(NT, PT, 2 * W), TM, 0, 0, tiled=True)  21.9 us
    pallas_call x1, Pallas kernels, attend(): call(attend_kernel, (jax.ShapeDtypeStruct((TOK, 4 * W), BF),) + (jax.Shap...  10.7 us
    ppermute x6, starting transfers between devices, shift(): return lax.ppermute(array, 'x', [(i, (i + k) % NX) for i in range(NX)])  6.59 us
    all_to_all x1, starting transfers between devices, on_device(): qkv = lax.all_to_all(qkv, TM, 0, 0, tiled=True)  5.06 us
    pallas_call x2, Pallas kernels, weight_half(): call(weight_kernel, shape, 4000000000, spec, 20 * 1024 * 1024)  4.16 us
  transfers between devices with their start and end apart: 11, of which 9 were waited for; matrix products, arithmetic and copies ran while one was open for 0% of the time, Pallas kernels for 6%

profile of v9, /device:TPU:1, one launch (start us, length us, event | category | flops | bytes accessed | tf_op | source)
XLA Modules:
  0.0 160.5 jit_solution(12866776929665150136)
XLA Ops:
  7.2 0.0 all-gather.2.cloned.1.call-start
  7.2 3.2 %shard_map.104 = bf16[32,16,640]{2,1,0:T(8,128)(2,1)} custom-call(s32[1]{0:T(128)} %bitcast.x_ref, bf16[2,256,1280]{2,1,0:T(8,128)(2,1)} %bitcast.37, bf16[2,256,1280]{2,1,0:T(8,128)(2,1)} %bitcast.38), custom_call_target="tpu_custom_call" | custom-call | flops 850000000 | bytes 4000000 | tf_op jit(solution)/shard_map/pallas_call | solution.py:119
  10.5 31.0 %all_to_all.20 = bf16[32,16,640]{2,1,0:T(8,128)(2,1)} all-to-all(bf16[32,16,640]{2,1,0:T(8,128)(2,1)} %shard_map.104), channel_id=1, replica_groups=mesh['dp'=2,'z'=8,'yl'=2,'core'=2,'x'=4] {'z','yl','core'}, dimensions={0} | all-to-all | bytes 1310720 | tf_op jit(solution)/shard_map/all_to_all | solution.py:334
  41.5 1.3 shard_map.103
  42.8 5.1 %all-to-all-start = ((bf16[32,24,640]{2,1,0:T(8,128)(2,1)}), bf16[32,24,640]{2,1,0:T(8,128)(2,1)S(1)}, u32[]{:S(2)}, u32[]{:S(2)}) async-start(bf16[32,24,640]{2,1,0:T(8,128)(2,1)} %shard_map.103), calls=%async_computation | async-start | bytes 1966080 | tf_op jit(solution)/shard_map/all_to_all | solution.py:339
  47.9 0.2 reduce-scatter.2.cloned.1.call-start
  48.1 1.9 %shard_map.105.wout_ref = bf16[4,320,320]{2,1,0:T(8,128)(2,1)S(1)} custom-call(s32[4,1,320]{2,1,0:T(1,128)S(1)} %copy-done.5, bf16[320,1280]{1,0:T(8,128)(2,1)S(1)} %copy-done.1), custom_call_target="tpu_custom_call" | custom-call | flops 1000000000 | bytes 4000000 | tf_op jit(solution)/shard_map/pallas_call | solution.py:340
  50.0 24.7 %all-to-all-done.qkv_ref = bf16[32,24,640]{2,1,0:T(8,128)(2,1)S(1)} async-done(((bf16[32,24,640]{2,1,0:T(8,128)(2,1)}), bf16[32,24,640]{2,1,0:T(8,128)(2,1)S(1)}, u32[]{:S(2)}, u32[]{:S(2)}) %all-to-all-start) | async-done | bytes 983072 | tf_op jit(solution)/shard_map/all_to_all | solution.py:339
  74.7 1.9 %all-gather.2.cloned.1.call-done = bf16[2048,640]{1,0:T(8,128)(2,1)} async-done(((bf16[512,640]{1,0:T(8,128)(2,1)}), bf16[2048,640]{1,0:T(8,128)(2,1)}) %all-gather.2.cloned.1.call-update) | async-done | bytes 2621456 | tf_op jit(solution)/shard_map/all_gather | solution.py:335
  76.6 10.7 %shard_map.106 = (bf16[512,1280]{1,0:T(8,128)(2,1)S(1)}, bf16[256,640]{1,0:T(8,128)(2,1)S(1)}, bf16[256,640]{1,0:T(8,128)(2,1)S(1)}, bf16[256,640]{1,0:T(8,128)(2,1)S(1)}, bf16[256,640]{1,0:T(8,128)(2,1)S(1)}) custom-call(s32[1]{0:T(128)} %bitcast.x_ref, bf16[32,24,640]{2,1,0:T(8,128)(2,1)S(1)} %all-to-all-done.qkv_ref, bf16[4,32,16,640]{3,2,1,0:T(8,128)(2,1)} %bitcast.30, ...), custom_call_target="tpu_custom_call" | custom-call | flops 5000000000 | bytes 4000000 | tf_op jit(solution)/shard_map/pallas_call | solution.py:244
  87.3 1.6 %shard_map.109 = bf16[640,1280]{1,0:T(8,128)(2,1)S(1)} custom-call(s32[1]{0:T(128)} %bitcast.17.half_ref, bf16[4,32,16,640]{3,2,1,0:T(8,128)(2,1)S(1)} %bitcast.31, bf16[512,1280]{1,0:T(8,128)(2,1)S(1)} %get-tuple-element.14.grads_ref), custom_call_target="tpu_custom_call" | custom-call | flops 4000000000 | bytes 4000000 | tf_op jit(solution)/shard_map/pallas_call | solution.py:287
  88.9 0.8 collective-permute-start.6
  89.7 0.4 collective-permute-start
  90.1 2.1 %collective-permute-start.1 = (bf16[256,640]{1,0:T(8,128)(2,1)S(1)}, bf16[256,640]{1,0:T(8,128)(2,1)S(1)}, u32[]{:S(2)}, u32[]{:S(2)}) collective-permute-start(bf16[256,640]{1,0:T(8,128)(2,1)S(1)} %get-tuple-element.12), channel_id=1, source_target_pairs={{0,2},{1,3},{2,0},{3,1},{4,6},{5,7},{6,4},{7,5},{8,10},{9,11},{10,... | collective-permute-start | bytes 983048 | tf_op jit(solution)/shard_map/ppermute | solution.py:324
  92.2 1.2 collective-permute-start.2
  93.4 2.5 %shard_map.110 = bf16[640,1280]{1,0:T(8,128)(2,1)} custom-call(s32[1]{0:T(128)} %bitcast.16.half_ref, bf16[4,32,16,640]{3,2,1,0:T(8,128)(2,1)S(1)} %bitcast.32, bf16[512,1280]{1,0:T(8,128)(2,1)S(1)} %get-tuple-element.14.grads_ref, bf16[640,1280]{1,0:T(8,128)(2,1)S(1)} %collective-permute-done.6.refs_0_), custom_call_target="tpu_custom_call" | custom-call | flops 4000000000 | bytes 4000000 | tf_op jit(solution)/shard_map/pallas_call | solution.py:287
  95.9 4.4 %collective-permute-done.refs_1_ = bf16[256,640]{1,0:T(8,128)(2,1)S(1)} collective-permute-done((bf16[256,640]{1,0:T(8,128)(2,1)S(1)}, bf16[256,640]{1,0:T(8,128)(2,1)S(1)}, u32[]{:S(2)}, u32[]{:S(2)}) %collective-permute-start) | collective-permute-done | bytes 327712 | tf_op jit(solution)/shard_map/ppermute | solution.py:324
  100.4 6.7 %collective-permute-done.1.refs_2_ = bf16[256,640]{1,0:T(8,128)(2,1)S(1)} collective-permute-done((bf16[256,640]{1,0:T(8,128)(2,1)S(1)}, bf16[256,640]{1,0:T(8,128)(2,1)S(1)}, u32[]{:S(2)}, u32[]{:S(2)}) %collective-permute-start.1) | collective-permute-done | bytes 327712 | tf_op jit(solution)/shard_map/ppermute | solution.py:324
  107.1 0.5 collective-permute-done.2.refs_3_
  107.5 0.2 shard_map.107
  107.7 21.9 %all_to_all.21 = bf16[32,8,640]{2,1,0:T(8,128)(2,1)S(1)} all-to-all(bf16[32,8,640]{2,1,0:T(8,128)(2,1)S(1)} %bitcast.29), channel_id=1, replica_groups=mesh['dp'=2,'z'=8,'yl'=2,'core'=2,'x'=4] {'z','yl','core'}, dimensions={0} | all-to-all | bytes 655360 | tf_op jit(solution)/shard_map/all_to_all | solution.py:350
  129.5 2.4 %collective-permute-start.5 = (bf16[256,640]{1,0:T(8,128)(2,1)S(1)}, bf16[256,640]{1,0:T(8,128)(2,1)S(1)}, u32[]{:S(2)}, u32[]{:S(2)}) collective-permute-start(bf16[256,640]{1,0:T(8,128)(2,1)S(1)} %bitcast.25), channel_id=1, source_target_pairs={{0,3},{1,0},{2,1},{3,2},{4,7},{5,4},{6,5},{7,6},{8,11},{9,8},{10,9... | collective-permute-start | bytes 983048 | tf_op jit(solution)/shard_map/ppermute | solution.py:324
  131.9 0.4 collective-permute-start.4
  132.2 0.2 collective-permute-start.3
  132.5 1.8 %shard_map.111 = bf16[8,20,1280]{2,1,0:T(8,128)(2,1)} custom-call(bf16[160,1280]{1,0:T(8,128)(2,1)} %bitcast.39), custom_call_target="tpu_custom_call" | custom-call | bytes 4000000 | tf_op jit(solution)/shard_map/pallas_call | solution.py:359
  134.3 3.5 %all-to-all-start.3 = ((bf16[8,20,1280]{2,1,0:T(8,128)(2,1)}), bf16[8,20,1280]{2,1,0:T(8,128)(2,1)S(1)}, u32[]{:S(2)}, u32[]{:S(2)}) async-start(bf16[8,20,1280]{2,1,0:T(8,128)(2,1)} %shard_map.111), calls=%async_computation.4 | async-start | bytes 983040 | tf_op jit(solution)/shard_map/all_to_all | solution.py:360
  137.8 0.5 collective-permute-done.5.refs_3_
  138.3 2.8 %collective-permute-done.4.refs_2_ = bf16[256,640]{1,0:T(8,128)(2,1)S(1)} collective-permute-done((bf16[256,640]{1,0:T(8,128)(2,1)S(1)}, bf16[256,640]{1,0:T(8,128)(2,1)S(1)}, u32[]{:S(2)}, u32[]{:S(2)}) %collective-permute-start.4) | collective-permute-done | bytes 327712 | tf_op jit(solution)/shard_map/ppermute | solution.py:324
  141.1 8.9 %collective-permute-done.3.refs_1_ = bf16[256,640]{1,0:T(8,128)(2,1)S(1)} collective-permute-done((bf16[256,640]{1,0:T(8,128)(2,1)S(1)}, bf16[256,640]{1,0:T(8,128)(2,1)S(1)}, u32[]{:S(2)}, u32[]{:S(2)}) %collective-permute-start.3) | collective-permute-done | bytes 327712 | tf_op jit(solution)/shard_map/ppermute | solution.py:324
  150.0 1.7 %shard_map.108 = bf16[2,256,1280]{2,1,0:T(8,128)(2,1)} custom-call(s32[1]{0:T(128)} %bitcast.x_ref, bf16[256,640]{1,0:T(8,128)(2,1)S(1)} %bitcast.28, bf16[256,640]{1,0:T(8,128)(2,1)S(1)} %collective-permute-done.3.refs_1_, bf16[256,640]{1,0:T(8,128)(2,1)S(1)} %collective-permute-done.4.refs_2_, bf16[256,640]{1,0:T(8,128)(2,1)S(1)} %collective-permute-done.5.refs_3_), custom_call_target="tpu_custom_call" | custom-call | flops 40000000000 | bytes 4000000 | tf_op jit(solution)/shard_map/pallas_call | solution.py:352
  151.8 1.1 all-to-all-done.3.in_ref
  152.9 0.8 shard_map.112
  (16 shorter events, 0.1 us)
Async XLA Ops:
  7.2 69.4 %all-gather.2.cloned.1.call-start = ((), (), s32[]{:S(2)}) async-start(), calls=%async_computation.5 | async-start | bytes 3276800 | tf_op jit(solution)/shard_map/all_gather | solution.py:335
  10.4 31.1 %copy-start.2 = (bf16[1,2,256,320]{2,3,1,0:T(8,128)(2,1)S(1)}, bf16[1,2,256,320]{2,3,1,0:T(8,128)(2,1)}, u32[]{:S(2)}) copy-start(bf16[1,2,256,320]{2,3,1,0:T(8,128)(2,1)} %param.8) | copy-start | bytes 983044
  10.4 31.1 %copy-start.3 = (bf16[1,2,256,320]{2,3,1,0:T(8,128)(2,1)S(1)}, bf16[1,2,256,320]{2,3,1,0:T(8,128)(2,1)}, u32[]{:S(2)}) copy-start(bf16[1,2,256,320]{2,3,1,0:T(8,128)(2,1)} %param.9) | copy-start | bytes 983044
  10.5 31.1 %copy-start.4 = (bf16[1,2,256,320]{2,3,1,0:T(8,128)(2,1)S(1)}, bf16[1,2,256,320]{2,3,1,0:T(8,128)(2,1)}, u32[]{:S(2)}) copy-start(bf16[1,2,256,320]{2,3,1,0:T(8,128)(2,1)} %param.10) | copy-start | bytes 983044
  42.8 5.3 %copy-start.1 = (bf16[320,1280]{1,0:T(8,128)(2,1)S(1)}, bf16[320,1280]{1,0:T(8,128)(2,1)}, u32[]{:S(2)}) copy-start(bf16[320,1280]{1,0:T(8,128)(2,1)} %w_ref.1) | copy-start | bytes 2457604
  42.8 5.3 %copy-start.5 = (s32[4,1,320]{2,1,0:T(1,128)S(1)}, s32[4,1,320]{2,1,0:T(1,128)}, u32[]{:S(2)}) copy-start(s32[4,1,320]{2,1,0:T(1,128)} %constant.13.clone.feat_ref) | copy-start | bytes 15364
  42.8 31.9 %all-to-all-start = ((bf16[32,24,640]{2,1,0:T(8,128)(2,1)}), bf16[32,24,640]{2,1,0:T(8,128)(2,1)S(1)}, u32[]{:S(2)}, u32[]{:S(2)}) async-start(bf16[32,24,640]{2,1,0:T(8,128)(2,1)} %shard_map.103), calls=%async_computation | async-start | bytes 1966080 | tf_op jit(solution)/shard_map/all_to_all | solution.py:339
  47.9 84.6 %reduce-scatter.2.cloned.1.call-start = ((), (), s32[]{:S(2)}) async-start(), calls=%async_computation.6 | async-start | bytes 2048000 | tf_op jit(solution)/shard_map/reduce_scatter | solution.py:347
  76.6 10.7 %copy-start = (bf16[2048,640]{1,0:T(8,128)(2,1)S(1)}, bf16[2048,640]{1,0:T(8,128)(2,1)}, u32[]{:S(2)}) copy-start(bf16[2048,640]{1,0:T(8,128)(2,1)} %all-gather.2.cloned.1.call-done) | copy-start | bytes 7864324
  88.9 4.4 %collective-permute-start.6 = (bf16[640,1280]{1,0:T(8,128)(2,1)S(1)}, bf16[640,1280]{1,0:T(8,128)(2,1)S(1)}, u32[]{:S(2)}, u32[]{:S(2)}) collective-permute-start(bf16[640,1280]{1,0:T(8,128)(2,1)S(1)} %shard_map.109), channel_id=1, source_target_pairs={{0,4},{4,0},{1,5},{5,1},{2,6},{6,2},{3,7},{7,3},{8,12},{12,8},{9,1... | collective-permute-start | bytes 4915208 | tf_op jit(solution)/shard_map/ppermute | solution.py:345
  89.7 10.7 %collective-permute-start = (bf16[256,640]{1,0:T(8,128)(2,1)S(1)}, bf16[256,640]{1,0:T(8,128)(2,1)S(1)}, u32[]{:S(2)}, u32[]{:S(2)}) collective-permute-start(bf16[256,640]{1,0:T(8,128)(2,1)S(1)} %get-tuple-element.11), channel_id=1, source_target_pairs={{0,1},{1,2},{2,3},{3,0},{4,5},{5,6},{6,7},{7,4},{8,9},{9,10},{10,1... | collective-permute-start | bytes 983048 | tf_op jit(solution)/shard_map/ppermute | solution.py:324
  90.1 17.0 %collective-permute-start.1 = (bf16[256,640]{1,0:T(8,128)(2,1)S(1)}, bf16[256,640]{1,0:T(8,128)(2,1)S(1)}, u32[]{:S(2)}, u32[]{:S(2)}) collective-permute-start(bf16[256,640]{1,0:T(8,128)(2,1)S(1)} %get-tuple-element.12), channel_id=1, source_target_pairs={{0,2},{1,3},{2,0},{3,1},{4,6},{5,7},{6,4},{7,5},{8,10},{9,11},{10,... | collective-permute-start | bytes 983048 | tf_op jit(solution)/shard_map/ppermute | solution.py:324
  92.2 15.3 %collective-permute-start.2 = (bf16[256,640]{1,0:T(8,128)(2,1)S(1)}, bf16[256,640]{1,0:T(8,128)(2,1)S(1)}, u32[]{:S(2)}, u32[]{:S(2)}) collective-permute-start(bf16[256,640]{1,0:T(8,128)(2,1)S(1)} %get-tuple-element.13), channel_id=1, source_target_pairs={{0,3},{1,0},{2,1},{3,2},{4,7},{5,4},{6,5},{7,6},{8,11},{9,8},{10,9... | collective-permute-start | bytes 983048 | tf_op jit(solution)/shard_map/ppermute | solution.py:324
  129.5 8.7 %collective-permute-start.5 = (bf16[256,640]{1,0:T(8,128)(2,1)S(1)}, bf16[256,640]{1,0:T(8,128)(2,1)S(1)}, u32[]{:S(2)}, u32[]{:S(2)}) collective-permute-start(bf16[256,640]{1,0:T(8,128)(2,1)S(1)} %bitcast.25), channel_id=1, source_target_pairs={{0,3},{1,0},{2,1},{3,2},{4,7},{5,4},{6,5},{7,6},{8,11},{9,8},{10,9... | collective-permute-start | bytes 983048 | tf_op jit(solution)/shard_map/ppermute | solution.py:324
  131.9 9.2 %collective-permute-start.4 = (bf16[256,640]{1,0:T(8,128)(2,1)S(1)}, bf16[256,640]{1,0:T(8,128)(2,1)S(1)}, u32[]{:S(2)}, u32[]{:S(2)}) collective-permute-start(bf16[256,640]{1,0:T(8,128)(2,1)S(1)} %bitcast.26), channel_id=1, source_target_pairs={{0,2},{1,3},{2,0},{3,1},{4,6},{5,7},{6,4},{7,5},{8,10},{9,11},{10,... | collective-permute-start | bytes 983048 | tf_op jit(solution)/shard_map/ppermute | solution.py:324
  132.2 17.8 %collective-permute-start.3 = (bf16[256,640]{1,0:T(8,128)(2,1)S(1)}, bf16[256,640]{1,0:T(8,128)(2,1)S(1)}, u32[]{:S(2)}, u32[]{:S(2)}) collective-permute-start(bf16[256,640]{1,0:T(8,128)(2,1)S(1)} %bitcast.27), channel_id=1, source_target_pairs={{0,1},{1,2},{2,3},{3,0},{4,5},{5,6},{6,7},{7,4},{8,9},{9,10},{10,1... | collective-permute-start | bytes 983048 | tf_op jit(solution)/shard_map/ppermute | solution.py:324
  134.3 18.6 %all-to-all-start.3 = ((bf16[8,20,1280]{2,1,0:T(8,128)(2,1)}), bf16[8,20,1280]{2,1,0:T(8,128)(2,1)S(1)}, u32[]{:S(2)}, u32[]{:S(2)}) async-start(bf16[8,20,1280]{2,1,0:T(8,128)(2,1)} %shard_map.111), calls=%async_computation.4 | async-start | bytes 983040 | tf_op jit(solution)/shard_map/all_to_all | solution.py:360
Sparse Core Ops, SparseCore 0:
  41.6 34.9 all-gather.1
  96.1 28.5 reduce-scatter.1
